TPU v7x, 128 devices: a whole 4x4x4 slice. The times are simulated.
128 devices in a mesh: row: 16 (over x, y), col: 8 (over z, core).
Axes of the slice: x: 4, y: 4, z: 4, core: 2. Of those that a mesh axis runs over, the one named last changes fastest.
Arguments:
- tiles: bfloat16 [32768, 128, 128], P(('row', 'col'))
- tile_src: int32 [32768], P(('row', 'col')), may hold values from 0 to 15
- tile_slot: int32 [32768], P(('row', 'col')), may hold values from 0 to 127
- slot_block: int32 [16384], P(('row', 'col')), may hold values from 0 to 15
- out_degree: int32 [262144], P(('row', 'col')), may hold values from 512 to 2047
- good_seeds: int32 [128, 16384], P(None, ('row', 'col')), may hold values from 0 to 262143, as said below
- spam_cores: int32 [128, 8192], P(None, ('row', 'col')), may hold values from 0 to 262143, as said below
Outputs:
- trust: float32 [262144, 128], P(('row', 'col'))
- distrust: float32 [262144, 128], P(('row', 'col'))
Inputs may be any that keep to these rules, and one draw needn't show every extreme that they name: `tile_slot`: slot s of a device belongs to the peer with index s // 1 along row+col. `slot_block`: entry p * 128 + s is the local index, among the 16 blocks held by peer s, of the target block of slot s of device p. `good_seeds`: entries j * 128 to (j + 1) * 128 - 1 of each column's list are hosts of device j, from j * 2048 to (j + 1) * 2048 - 1. `spam_cores`: entries j * 64 to (j + 1) * 64 - 1 of each column's list are hosts of device j, from j * 2048 to (j + 1) * 2048 - 1.
All inputs are finite; a program needn't handle non-finite values.
Results may differ from a plain program's by a relative error of at most 0.0003.
Values may be sent and summed in bfloat16 or wider, within the bound.
No kernel may reach another device: no remote copies, remote signals or barrier semaphores. Data moves between devices by JAX's collectives and lax.ppermute only.
A program may use at most 128 MiB of HBM per device.

v0:
```python
import jax
import jax.numpy as jnp
from jax import lax
from jax.sharding import PartitionSpec as P

TRUST_ITERS = 2
ANTI_ITERS = 2


def teleport(seeds, host_count, factor):
    column_index = jnp.broadcast_to(
        jnp.arange(seeds.shape[0], dtype=jnp.int32)[:, None], seeds.shape
    )
    counts = (
        jnp.zeros((host_count, seeds.shape[0]), jnp.float32)
        .at[seeds % host_count, column_index]
        .add(jnp.float32(1.0))
    )
    return counts * jnp.float32(factor)


def first_push(outgoing, col_terms, slot_ids):
    return (
        lax.all_to_all(outgoing, ("row", "col"), split_axis=0, concat_axis=0, tiled=True),
        lax.all_to_all(col_terms, ("row", "col"), split_axis=0, concat_axis=0, tiled=True),
        lax.all_to_all(slot_ids, ("row", "col"), split_axis=0, concat_axis=0, tiled=True),
    )


def later_push(outgoing):
    return lax.all_to_all(outgoing, ("row", "col"), split_axis=0, concat_axis=0, tiled=True)


def pull_shares(outgoing):
    return lax.all_to_all(outgoing, ("row", "col"), split_axis=0, concat_axis=0, tiled=True)


def body(tiles, tile_src, tile_slot, slot_block, out_degree, good_seeds, spam_cores):
    tile_size = tiles.shape[1]
    host_count = out_degree.shape[0]
    block_count = host_count // tile_size
    column_count = good_seeds.shape[0]
    slot_count = slot_block.shape[0]
    good_start = teleport(good_seeds, host_count, host_count / good_seeds.shape[1])
    spam_start = teleport(spam_cores, host_count, host_count / spam_cores.shape[1])
    col_terms = jax.ops.segment_sum(
        jnp.sum(tiles, axis=1, dtype=jnp.float32), tile_slot, num_segments=slot_count
    )
    slot_ids = slot_block.astype(jnp.float32)
    degree = out_degree.astype(jnp.float32)[:, None]
    trust = good_start
    block_ids = jnp.zeros((slot_count,), jnp.int32)
    in_weight = jnp.ones((host_count,), jnp.float32)
    for iteration in range(TRUST_ITERS):
        scaled = (trust / degree).astype(jnp.bfloat16)
        sources = scaled.reshape(block_count, tile_size, column_count)[tile_src]
        products = jnp.einsum("kij,kis->kjs", tiles, sources, preferred_element_type=jnp.float32)
        outgoing = jax.ops.segment_sum(products, tile_slot, num_segments=slot_count)
        if iteration == 0:
            arrived, arrived_cols, arrived_ids = first_push(outgoing, col_terms, slot_ids)
            block_ids = arrived_ids.astype(jnp.int32)
            in_weight = 1.0 + jax.ops.segment_sum(
                arrived_cols, block_ids, num_segments=block_count
            ).reshape(host_count)
        else:
            arrived = later_push(outgoing)
        inflow = jax.ops.segment_sum(arrived, block_ids, num_segments=block_count).reshape(
            host_count, column_count
        )
        trust = 0.85 * inflow + 0.15 * good_start
    shield = 1.0 / (1.0 + trust)
    distrust = spam_start
    for iteration in range(ANTI_ITERS):
        share = (shield * distrust / in_weight[:, None]).astype(jnp.bfloat16)
        requested = share.reshape(block_count, tile_size, column_count)[block_ids]
        fetched = pull_shares(requested)
        targets = fetched[tile_slot]
        products = jnp.einsum("kij,kjs->kis", tiles, targets, preferred_element_type=jnp.float32)
        gathered_back = jax.ops.segment_sum(products, tile_src, num_segments=block_count).reshape(
            host_count, column_count
        )
        distrust = 0.85 * gathered_back + 0.15 * spam_start
    return (trust, distrust)


def solution(mesh):
    in_specs = (
        P(("row", "col"), None, None),
        P(("row", "col")),
        P(("row", "col")),
        P(("row", "col")),
        P(("row", "col")),
        P(None, ("row", "col")),
        P(None, ("row", "col")),
    )
    out_specs = (P(("row", "col"), None), P(("row", "col"), None))
    return jax.shard_map(body, mesh=mesh, in_specs=in_specs, out_specs=out_specs, check_vma=False)
```

profile of v0, /device:TPU:1, one launch (start us, length us, event | category | flops | bytes accessed | tf_op | source)
XLA Modules:
  0.0 858.3 jit_solution(11124743647027967751)
XLA Ops:
  2.0 11.5 %all-to-all-start = ((f32[128,1,1]{2,1,0:T(1,128)}), f32[128,1,1]{2,1,0:T(1,128)S(1)}, u32[]{:S(2)}, u32[]{:S(2)}) async-start(f32[128,1,1]{2,1,0:T(1,128)} %copy.31), calls=%async_computation | async-start | bytes 131072 | tf_op jit(solution)/shard_map/all_to_all | solution.py:26
  17.4 86.1 %scatter_custom_fusion.8 = f32[262144]{0:T(1024)S(1)} fusion(s32[16384]{0:T(1024)S(1)} %select_bitcast_fusion, f32[16384]{0:T(1024)S(1)} %broadcast.152, f32[]{:T(128)} %constant.17.clone.1), kind=kCustom, calls=%fused_computation.38 | custom fusion | flops 16384 | bytes 1048580
  103.8 8.6 %gather_fusion = bf16[256,128,128]{2,1,0:T(8,128)(2,1)} fusion(bf16[16,128,128]{2,1,0:T(8,128)(2,1)S(1)} %bitcast.72, s32[1024]{0:T(1024)S(1)} %pad_clamp_fusion.2), kind=kCustom, calls=%fused_computation | custom fusion | bytes 16778240 | tf_op jit(solution)/shard_map/gather | solution.py:56
  112.4 14.4 %convolution_bitcast_fusion.3 = f32[256,128,128]{1,2,0:T(8,128)} fusion(bf16[256,128,128]{2,1,0:T(8,128)(2,1)} %gather_fusion, bf16[256,128,128]{2,1,0:T(8,128)(2,1)} %param.7), kind=kOutput, calls=%fused_computation.20 | convolution fusion | flops 1073741824 | bytes 33554432 | tf_op jit(solution)/shard_map/kij,kis->kjs/dot_general | solution.py:57
  126.8 17.5 %copy.33 = f32[256,128,128]{2,1,0:T(8,128)} copy(f32[256,128,128]{1,2,0:T(8,128)} %convolution_bitcast_fusion.3) | data formatting | bytes 33554432 | tf_op jit(solution)/shard_map/kij,kis->kjs/dot_general | solution.py:57
  144.2 4.3 broadcast.115.clone
  148.5 51.9 %scatter_fusion = f32[128,128,128]{2,1,0:T(8,128)} fusion(f32[128,128,128]{2,1,0:T(8,128)} %broadcast.115.clone, s32[256]{0:T(256)S(1)} %copy-done.2, f32[256,128,128]{2,1,0:T(8,128)} %copy.33), kind=kCustom, calls=%fused_computation.6 | custom fusion | flops 4194304 | bytes 50332672 | tf_op jit(solution)/shard_map/scatter-add | solution.py:58
  200.4 22.2 %all-to-all-start.1 = ((f32[128,128,128]{2,1,0:T(8,128)}), f32[128,128,128]{2,1,0:T(8,128)}, u32[]{:S(2)}, u32[]{:S(2)}) async-start(f32[128,128,128]{2,1,0:T(8,128)} %scatter_fusion), calls=%async_computation.1 | async-start | bytes 16777216 | tf_op jit(solution)/shard_map/all_to_all | solution.py:24
  222.6 6.2 convert_reduce_fusion
  233.1 92.0 %all-to-all-done.1 = f32[128,128,128]{2,1,0:T(8,128)} async-done(((f32[128,128,128]{2,1,0:T(8,128)}), f32[128,128,128]{2,1,0:T(8,128)}, u32[]{:S(2)}, u32[]{:S(2)}) %all-to-all-start.1) | async-done | bytes 8388640 | tf_op jit(solution)/shard_map/all_to_all | solution.py:24
  325.1 8.7 %all-to-all-start.3 = ((f32[128,1,128]{2,1,0:T(1,128)}), f32[128,1,128]{2,1,0:T(1,128)S(1)}, u32[]{:S(2)}, u32[]{:S(2)}) async-start(f32[128,1,128]{2,1,0:T(1,128)} %bitcast.13), calls=%async_computation.3 | async-start | bytes 131072 | tf_op jit(solution)/shard_map/all_to_all | solution.py:25
  333.9 17.0 %scatter_fusion.1 = f32[16,128,128]{2,1,0:T(8,128)S(1)} fusion(f32[16,128,128]{2,1,0:T(8,128)S(1)} %broadcast.114.clone.1, s32[128]{0:T(128)S(1)} %convert_reduce_fusion.1, f32[128,128,128]{2,1,0:T(8,128)} %all-to-all-done.1), kind=kCustom, calls=%fused_computation.7 | custom fusion | flops 2097152 | bytes 25166336 | tf_op jit(solution)/shard_map/scatter-add | solution.py:67
  351.4 8.6 %gather_fusion.1 = bf16[256,128,128]{2,1,0:T(8,128)(2,1)} fusion(bf16[16,128,128]{2,1,0:T(8,128)(2,1)S(1)} %bitcast.71, s32[1024]{0:T(1024)S(1)} %pad_clamp_fusion.2), kind=kCustom, calls=%fused_computation.1 | custom fusion | bytes 16778240 | tf_op jit(solution)/shard_map/gather | solution.py:56
  360.0 14.4 %convolution_bitcast_fusion.2 = f32[256,128,128]{1,2,0:T(8,128)} fusion(bf16[256,128,128]{2,1,0:T(8,128)(2,1)} %gather_fusion.1, bf16[256,128,128]{2,1,0:T(8,128)(2,1)} %param.7), kind=kOutput, calls=%fused_computation.19 | convolution fusion | flops 1073741824 | bytes 33554432 | tf_op jit(solution)/shard_map/kij,kis->kjs/dot_general | solution.py:57
  374.3 17.5 %copy.35 = f32[256,128,128]{2,1,0:T(8,128)} copy(f32[256,128,128]{1,2,0:T(8,128)} %convolution_bitcast_fusion.2) | data formatting | bytes 33554432 | tf_op jit(solution)/shard_map/kij,kis->kjs/dot_general | solution.py:57
  391.8 4.3 broadcast.115
  396.1 51.9 %scatter_fusion.2 = f32[128,128,128]{2,1,0:T(8,128)} fusion(f32[128,128,128]{2,1,0:T(8,128)} %broadcast.115, s32[256]{0:T(256)S(1)} %copy-done.2, f32[256,128,128]{2,1,0:T(8,128)} %copy.35), kind=kCustom, calls=%fused_computation.8 | custom fusion | flops 4194304 | bytes 50332672 | tf_op jit(solution)/shard_map/scatter-add | solution.py:58
  448.0 10.3 %all-to-all-start.2 = ((f32[128,128,128]{2,1,0:T(8,128)}), f32[128,128,128]{2,1,0:T(8,128)}, u32[]{:S(2)}, u32[]{:S(2)}) async-start(f32[128,128,128]{2,1,0:T(8,128)} %scatter_fusion.2), calls=%async_computation.2 | async-start | bytes 16777216 | tf_op jit(solution)/shard_map/all_to_all | solution.py:31
  458.7 43.5 %scatter_custom_fusion.9 = f32[262144]{0:T(1024)S(1)} fusion(s32[8192]{0:T(1024)S(1)} %reshape.227, f32[8192]{0:T(1024)S(1)} %broadcast.154, f32[]{:T(128)} %constant.17.clone.1), kind=kCustom, calls=%fused_computation.36 | custom fusion | flops 8192 | bytes 1048580
  503.3 57.5 %all-to-all-done.2 = f32[128,128,128]{2,1,0:T(8,128)} async-done(((f32[128,128,128]{2,1,0:T(8,128)}), f32[128,128,128]{2,1,0:T(8,128)}, u32[]{:S(2)}, u32[]{:S(2)}) %all-to-all-start.2) | async-done | bytes 8388640 | tf_op jit(solution)/shard_map/all_to_all | solution.py:31
  561.0 17.0 %scatter_fusion.3 = f32[16,128,128]{2,1,0:T(8,128)S(1)} fusion(f32[16,128,128]{2,1,0:T(8,128)S(1)} %broadcast.114.clone, s32[128]{0:T(128)S(1)} %convert_reduce_fusion.1, f32[128,128,128]{2,1,0:T(8,128)} %all-to-all-done.2), kind=kCustom, calls=%fused_computation.9 | custom fusion | flops 2097152 | bytes 25166336 | tf_op jit(solution)/shard_map/scatter-add | solution.py:67
  582.5 10.0 %all-to-all-start.4 = ((bf16[128,128,128]{2,1,0:T(8,128)(2,1)}), bf16[128,128,128]{2,1,0:T(8,128)(2,1)}, u32[]{:S(2)}, u32[]{:S(2)}) async-start(bf16[128,128,128]{2,1,0:T(8,128)(2,1)} %gather_fusion.2), calls=%async_computation.4 | async-start | bytes 8388608 | tf_op jit(solution)/shard_map/all_to_all | solution.py:35
  592.5 52.8 %all-to-all-done.4 = bf16[128,128,128]{2,1,0:T(8,128)(2,1)} async-done(((bf16[128,128,128]{2,1,0:T(8,128)(2,1)}), bf16[128,128,128]{2,1,0:T(8,128)(2,1)}, u32[]{:S(2)}, u32[]{:S(2)}) %all-to-all-start.4) | async-done | bytes 4194336 | tf_op jit(solution)/shard_map/all_to_all | solution.py:35
  645.3 10.8 %gather_fusion.3 = bf16[256,128,128]{2,1,0:T(8,128)(2,1)} fusion(bf16[128,128,128]{2,1,0:T(8,128)(2,1)} %all-to-all-done.4, s32[1024]{0:T(1024)S(1)} %pad_clamp_fusion), kind=kCustom, calls=%fused_computation.3 | custom fusion | bytes 16778240 | tf_op jit(solution)/shard_map/gather | solution.py:77
  656.1 12.8 %convolution_bitcast_fusion.1 = f32[256,128,128]{1,2,0:T(8,128)} fusion(bf16[256,128,128]{2,1,0:T(8,128)(2,1)} %gather_fusion.3, bf16[256,128,128]{2,1,0:T(8,128)(2,1)} %param.7), kind=kOutput, calls=%fused_computation.18 | convolution fusion | flops 1073741824 | bytes 33554432 | tf_op jit(solution)/shard_map/kij,kjs->kis/dot_general | solution.py:78
  668.9 17.5 %copy.38 = f32[256,128,128]{2,1,0:T(8,128)} copy(f32[256,128,128]{1,2,0:T(8,128)} %convolution_bitcast_fusion.1) | data formatting | bytes 33554432 | tf_op jit(solution)/shard_map/kij,kjs->kis/dot_general | solution.py:78
  686.5 33.2 %scatter_fusion.4 = f32[16,128,128]{2,1,0:T(8,128)S(1)} fusion(f32[16,128,128]{2,1,0:T(8,128)S(1)} %broadcast.114.clone.2, s32[256]{0:T(256)S(1)} %copy-done.3, f32[256,128,128]{2,1,0:T(8,128)} %copy.38), kind=kCustom, calls=%fused_computation.12 | custom fusion | flops 4194304 | bytes 50332672 | tf_op jit(solution)/shard_map/scatter-add | solution.py:79
  723.2 59.0 %all_to_all.41 = bf16[128,128,128]{2,1,0:T(8,128)(2,1)} all-to-all(bf16[128,128,128]{2,1,0:T(8,128)(2,1)} %gather_fusion.4), channel_id=1, replica_groups=mesh['row'=16,'col'=8] {'row','col'}, dimensions={0} | all-to-all | bytes 8388608 | tf_op jit(solution)/shard_map/all_to_all | solution.py:35
  782.3 10.8 %gather_fusion.5 = bf16[256,128,128]{2,1,0:T(8,128)(2,1)} fusion(bf16[128,128,128]{2,1,0:T(8,128)(2,1)} %all_to_all.41, s32[1024]{0:T(1024)S(1)} %pad_clamp_fusion), kind=kCustom, calls=%fused_computation.5 | custom fusion | bytes 16778240 | tf_op jit(solution)/shard_map/gather | solution.py:77
  793.1 12.8 %convolution_bitcast_fusion = f32[256,128,128]{1,2,0:T(8,128)} fusion(bf16[256,128,128]{2,1,0:T(8,128)(2,1)} %gather_fusion.5, bf16[256,128,128]{2,1,0:T(8,128)(2,1)} %param.7), kind=kOutput, calls=%fused_computation.17 | convolution fusion | flops 1073741824 | bytes 33554432 | tf_op jit(solution)/shard_map/kij,kjs->kis/dot_general | solution.py:78
  805.9 17.5 %copy.40 = f32[256,128,128]{2,1,0:T(8,128)} copy(f32[256,128,128]{1,2,0:T(8,128)} %convolution_bitcast_fusion) | data formatting | bytes 33554432 | tf_op jit(solution)/shard_map/kij,kjs->kis/dot_general | solution.py:78
  823.5 33.2 %scatter_fusion.5 = f32[16,128,128]{2,1,0:T(8,128)S(1)} fusion(f32[16,128,128]{2,1,0:T(8,128)S(1)} %broadcast.114, s32[256]{0:T(256)S(1)} %copy-done.3, f32[256,128,128]{2,1,0:T(8,128)} %copy.40), kind=kCustom, calls=%fused_computation.13 | custom fusion | flops 4194304 | bytes 50332672 | tf_op jit(solution)/shard_map/scatter-add | solution.py:79
  (55 shorter events, 21.5 us)
Async XLA Ops:
  2.0 198.3 %all-to-all-start = ((f32[128,1,1]{2,1,0:T(1,128)}), f32[128,1,1]{2,1,0:T(1,128)S(1)}, u32[]{:S(2)}, u32[]{:S(2)}) async-start(f32[128,1,1]{2,1,0:T(1,128)} %copy.31), calls=%async_computation | async-start | bytes 131072 | tf_op jit(solution)/shard_map/all_to_all | solution.py:26
  144.2 4.3 copy-start.2
  200.4 124.7 %all-to-all-start.1 = ((f32[128,128,128]{2,1,0:T(8,128)}), f32[128,128,128]{2,1,0:T(8,128)}, u32[]{:S(2)}, u32[]{:S(2)}) async-start(f32[128,128,128]{2,1,0:T(8,128)} %scatter_fusion), calls=%async_computation.1 | async-start | bytes 16777216 | tf_op jit(solution)/shard_map/all_to_all | solution.py:24
  325.1 122.9 %all-to-all-start.3 = ((f32[128,1,128]{2,1,0:T(1,128)}), f32[128,1,128]{2,1,0:T(1,128)S(1)}, u32[]{:S(2)}, u32[]{:S(2)}) async-start(f32[128,1,128]{2,1,0:T(1,128)} %bitcast.13), calls=%async_computation.3 | async-start | bytes 131072 | tf_op jit(solution)/shard_map/all_to_all | solution.py:25
  447.9 10.3 %copy-start.1 = (s32[128,64]{0,1:T(8,128)S(1)}, s32[128,64]{0,1:T(8,128)}, u32[]{:S(2)}) copy-start(s32[128,64]{0,1:T(8,128)} %param.13) | copy-start | bytes 98308
  447.9 10.3 %copy-start.4 = (s32[2]{0:T(128)S(1)}, s32[2]{0:T(128)}, u32[]{:S(2)}) copy-start(s32[2]{0:T(128)} %constant.33) | copy-start | bytes 28
  448.0 10.4 %copy-start.5 = (s32[2]{0:T(128)S(1)}, s32[2]{0:T(128)}, u32[]{:S(2)}) copy-start(s32[2]{0:T(128)} %constant.65) | copy-start | bytes 28
  448.0 112.9 %all-to-all-start.2 = ((f32[128,128,128]{2,1,0:T(8,128)}), f32[128,128,128]{2,1,0:T(8,128)}, u32[]{:S(2)}, u32[]{:S(2)}) async-start(f32[128,128,128]{2,1,0:T(8,128)} %scatter_fusion.2), calls=%async_computation.2 | async-start | bytes 16777216 | tf_op jit(solution)/shard_map/all_to_all | solution.py:31
  582.5 62.8 %all-to-all-start.4 = ((bf16[128,128,128]{2,1,0:T(8,128)(2,1)}), bf16[128,128,128]{2,1,0:T(8,128)(2,1)}, u32[]{:S(2)}, u32[]{:S(2)}) async-start(bf16[128,128,128]{2,1,0:T(8,128)(2,1)} %gather_fusion.2), calls=%async_computation.4 | async-start | bytes 8388608 | tf_op jit(solution)/shard_map/all_to_all | solution.py:35
  668.9 17.6 %copy-start.3 = (s32[256]{0:T(256)S(1)}, s32[256]{0:T(256)}, u32[]{:S(2)}) copy-start(s32[256]{0:T(256)} %param.8) | copy-start | bytes 3076
  686.5 33.3 %copy-start = (f32[2048,128]{1,0:T(8,128)S(1)}, f32[2048,128]{1,0:T(8,128)}, u32[]{:S(2)}) copy-start(f32[2048,128]{1,0:T(8,128)} %get-tuple-element.3) | copy-start | bytes 3145732
where the time goes:
time: 870 us; the launch traced here: 858 us
  other arithmetic  354 us (41%)
  waiting for transfers between devices  202 us (23%)
  local copies, waits for them, and re-layouts  125 us (14%)
  starting transfers between devices  62.6 us (7%)
  blocking collectives  59 us (7%)
  matrix products  54.4 us (6%)
    unnamed x8, other arithmetic  131 us
    scatter-add x2, other arithmetic, body(): outgoing = jax.ops.segment_sum(products, tile_slot, num_segments=slot_count)  104 us
    all_to_all x1, waiting for transfers between devices, first_push(): lax.all_to_all(outgoing, ('row', 'col'), split_axis=0, concat_axis=0, til...  92 us
    scatter-add x2, other arithmetic, body(): jax.ops.segment_sum(products, tile_src, num_segments=block_count)  66.3 us
    all_to_all x1, blocking collectives, pull_shares(): lax.all_to_all(outgoing, ('row', 'col'), split_axis=0, concat_axis=0, til...  59 us
    all_to_all x1, waiting for transfers between devices, later_push(): lax.all_to_all(outgoing, ('row', 'col'), split_axis=0, concat_axis=0, til...  57.5 us
    all_to_all x1, waiting for transfers between devices, pull_shares(): lax.all_to_all(outgoing, ('row', 'col'), split_axis=0, concat_axis=0, til...  52.8 us
    dot_general x2, local copies, waits for them, and re-layouts, body(): jnp.einsum('kij,kjs->kis', tiles, targets, preferred_element_type=jnp.flo...  34.9 us
  transfers between devices with their start and end apart: 5, of which 3 were waited for; matrix products, arithmetic and copies ran while one was open for 42% of the time, Pallas kernels for 0%

commit v1 on v0

v1 whole, which is shorter than its diff:
```python
import functools

import jax
import jax.numpy as jnp
from jax import lax
from jax.experimental import pallas as pl
from jax.experimental.pallas import tpu as pltpu
from jax.sharding import PartitionSpec as P

AXES = ("row", "col")
F32, BF16, I16, I32 = jnp.float32, jnp.bfloat16, jnp.int16, jnp.int32
BS = 128
EXTRA = 8
LOG_TOP = 14.997
STEPS = 64.0
LEAST = 1e-30
FINE = 65000.0

ANY = pl.BlockSpec(memory_space=pl.ANY)
SMEM = pl.BlockSpec(memory_space=pltpu.SMEM)
VMEM = pl.BlockSpec(memory_space=pltpu.VMEM)


def params(mib):
    return pltpu.CompilerParams(vmem_limit_bytes=mib << 20)


def exchange(x):
    return lax.all_to_all(x, AXES, split_axis=0, concat_axis=0, tiled=True)


def fetch(hbm, vmem, sems, chunk):
    return [
        pltpu.make_async_copy(
            hbm.at[pl.ds(c * chunk, chunk)], vmem.at[pl.ds(c * chunk, chunk)], sems.at[c]
        )
        for c in range(hbm.shape[0] // chunk)
    ]


def histogram(seeds_ref, out_ref, factor):
    columns, depth = seeds_ref.shape
    blocks = out_ref.shape[0] // columns
    unroll = 8

    def group(g, _):
        for u in range(unroll):
            s = g * unroll + u
            local = seeds_ref[pl.ds(s, 1), :] & (blocks * BS - 1)
            high = (lax.broadcasted_iota(I32, (blocks, depth), 0) == (local >> 7)).astype(F32).astype(BF16)
            low = (lax.broadcasted_iota(I32, (BS, depth), 0) == (local & (BS - 1))).astype(F32).astype(BF16)
            count = lax.dot_general(high, low, (((1,), (1,)), ((), ())), preferred_element_type=F32)
            out_ref[pl.ds(s, blocks, stride=columns), :] = count * factor
        return 0

    lax.fori_loop(0, columns // unroll, group, 0)


def encode_scale(largest):
    return jnp.ceil(jnp.log2(jnp.maximum(largest, LEAST)) * STEPS)


def up(code):
    return jnp.exp2(LOG_TOP - code * (1.0 / STEPS))


def down(code):
    return jnp.exp2(code * (1.0 / STEPS) - LOG_TOP)


def to_i16(x):
    return jnp.round(x).astype(I32).astype(I16)


def push(x_ref, tile_copies, tiles, src, slot, acc, chunk):
    def clear(g, _):
        acc[g] = jnp.zeros(acc.shape[1:], F32)
        return 0

    lax.fori_loop(0, acc.shape[0], clear, 0)
    unroll = 8
    for c, copy in enumerate(tile_copies):
        copy.wait()

        def group(g, _):
            base = c * chunk + g * unroll
            parts = [
                jnp.dot(x_ref[src[base + u]], tiles[base + u], preferred_element_type=F32)
                for u in range(unroll)
            ]
            for u in range(unroll):
                at = slot[base + u]
                acc[at] = acc[at] + parts[u]
            return 0

        lax.fori_loop(0, chunk // unroll, group, 0)


def send(acc, extra_row, staged, out_hbm, sems, chunk):
    copies = []
    row = lax.broadcasted_iota(I32, (EXTRA, BS), 0)
    unroll = 4
    for c in range(acc.shape[0] // chunk):

        def group(g, _):
            for u in range(unroll):
                p = c * chunk + g * unroll + u
                block = acc[p]
                code = encode_scale(jnp.max(jnp.abs(block), axis=0, keepdims=True))
                staged[p, 0:BS, :] = to_i16(block * up(code))
                tail = jnp.where(row == 0, jnp.broadcast_to(code.astype(I32), (EXTRA, BS)), extra_row(p))
                staged[p, BS : BS + EXTRA, :] = tail.astype(I16)
            return 0

        lax.fori_loop(0, chunk // unroll, group, 0)
        copy = pltpu.make_async_copy(
            staged.at[pl.ds(c * chunk, chunk)], out_hbm.at[pl.ds(c * chunk, chunk)], sems.at[c]
        )
        copy.start()
        copies.append(copy)
    for copy in copies:
        copy.wait()


def receive(arrived, copies, ids, total, chunk, also=None):
    for b in range(total.shape[0]):
        total[b] = jnp.zeros(total.shape[1:], F32)
    unroll = 4
    for c, copy in enumerate(copies):
        copy.wait()

        def group(g, _):
            for u in range(unroll):
                p = c * chunk + g * unroll + u
                tail = arrived[p, BS : BS + EXTRA, :].astype(I32).astype(F32)
                values = arrived[p, 0:BS, :].astype(I32).astype(F32) * down(tail[0:1])
                at = ids[p]
                total[at] = total[at] + values
                if also is not None:
                    also(at, tail)
            return 0

        lax.fori_loop(0, chunk // unroll, group, 0)


def first_kernel(chunk, slots_chunk, factor, seeds, degree, src, slot, slot_block, tiles_hbm,
                 out_hbm, good, tiles, x, acc, staged, counts, tile_sems, out_sems):
    copies = fetch(tiles_hbm, tiles, tile_sems, chunk)
    for copy in copies:
        copy.start()
    histogram(seeds, counts, factor)
    blocks, columns = x.shape[0], x.shape[1]

    def scale(b, _):
        trust = counts[pl.ds(b * columns, columns), :]
        good[b] = trust.astype(BF16)
        x[b] = (trust / degree[b].astype(F32)).astype(BF16)
        return 0

    lax.fori_loop(0, blocks, scale, 0)
    push(x, copies, tiles, src, slot, acc, chunk)
    send(acc, lambda p: slot_block[p], staged, out_hbm, out_sems, slots_chunk)


def second_kernel(chunk, slots_chunk, ids, degree, src, slot, good, weights, arrived_hbm, tiles_hbm,
                  out_hbm, arrived, tiles, x, total, acc, staged, in_sems, tile_sems, out_sems):
    incoming = fetch(arrived_hbm, arrived, in_sems, slots_chunk)
    copies = fetch(tiles_hbm, tiles, tile_sems, chunk)
    for copy in incoming + copies:
        copy.start()
    receive(arrived, incoming, ids, total, slots_chunk)

    def scale(b, _):
        trust = 0.85 * total[b] + 0.15 * good[b].astype(F32)
        x[b] = (trust / degree[b].astype(F32)).astype(BF16)
        return 0

    lax.fori_loop(0, x.shape[0], scale, 0)
    push(x, copies, tiles, src, slot, acc, chunk)
    send(acc, lambda p: weights[p].astype(I32), staged, out_hbm, out_sems, slots_chunk)


def requests(share, ids, staged, out_hbm, sems, chunk):
    copies = []
    unroll = min(8, chunk)
    for c in range(staged.shape[0] // chunk):

        def group(g, _):
            for u in range(unroll):
                p = c * chunk + g * unroll + u
                staged[p] = share[ids[p]]
            return 0

        lax.fori_loop(0, chunk // unroll, group, 0)
        copy = pltpu.make_async_copy(
            staged.at[pl.ds(c * chunk, chunk)], out_hbm.at[pl.ds(c * chunk, chunk)], sems.at[c]
        )
        copy.start()
        copies.append(copy)
    for copy in copies:
        copy.wait()


def third_kernel(slots_chunk, ids, good, spam, arrived_hbm, out_hbm, trust, shield, in_weight,
                 arrived, total, share, staged, in_sems, out_sems):
    incoming = fetch(arrived_hbm, arrived, in_sems, slots_chunk)
    for copy in incoming:
        copy.start()
    blocks = total.shape[0]
    in_weight[...] = jnp.ones(in_weight.shape, F32)

    def add_weight(at, tail):
        value = (tail[2:3] + tail[3:4] * (1.0 / FINE)) * down(tail[1:2])
        in_weight[at] = in_weight[at] + value

    receive(arrived, incoming, ids, total, slots_chunk, add_weight)

    def finish(b, _):
        value = 0.85 * total[b] + 0.15 * good[b].astype(F32)
        trust[b] = value
        keep = 1.0 / (1.0 + value)
        shield[b] = keep
        share[b] = (keep * spam[b].astype(F32) / in_weight[b]).astype(BF16)
        return 0

    lax.fori_loop(0, blocks, finish, 0)
    requests(share, ids, staged, out_hbm, out_sems, slots_chunk)


def pull(y, incoming, tiles, copies, src, slot, total, chunk):
    for b in range(total.shape[0]):
        total[b] = jnp.zeros(total.shape[1:], F32)
    for copy in incoming:
        copy.wait()
    unroll = 8
    for c, copy in enumerate(copies):
        copy.wait()

        def group(g, _):
            base = c * chunk + g * unroll
            parts = [
                lax.dot_general(
                    y[slot[base + u]], tiles[base + u], (((1,), (1,)), ((), ())), preferred_element_type=F32
                )
                for u in range(unroll)
            ]
            for u in range(unroll):
                at = src[base + u]
                total[at] = total[at] + parts[u]
            return 0

        lax.fori_loop(0, chunk // unroll, group, 0)


def fourth_kernel(chunk, slots_chunk, ids, src, slot, spam, shield, in_weight, arrived_hbm, tiles_hbm, out_hbm,
                  arrived, tiles, total, share, staged, in_sems, tile_sems, out_sems):
    incoming = fetch(arrived_hbm, arrived, in_sems, slots_chunk)
    copies = fetch(tiles_hbm, tiles, tile_sems, chunk)
    for copy in incoming + copies:
        copy.start()
    pull(arrived, incoming, tiles, copies, src, slot, total, chunk)

    def finish(b, _):
        value = 0.85 * total[b] + 0.15 * spam[b].astype(F32)
        share[b] = (shield[b] * value / in_weight[b]).astype(BF16)
        return 0

    lax.fori_loop(0, share.shape[0], finish, 0)
    requests(share, ids, staged, out_hbm, out_sems, slots_chunk)


def fifth_kernel(chunk, slots_chunk, src, slot, spam, arrived_hbm, tiles_hbm, distrust,
                 arrived, tiles, total, in_sems, tile_sems):
    incoming = fetch(arrived_hbm, arrived, in_sems, slots_chunk)
    copies = fetch(tiles_hbm, tiles, tile_sems, chunk)
    for copy in incoming + copies:
        copy.start()
    pull(arrived, incoming, tiles, copies, src, slot, total, chunk)

    def finish(b, _):
        distrust[b] = jnp.transpose(0.85 * total[b] + 0.15 * spam[b].astype(F32))
        return 0

    lax.fori_loop(0, total.shape[0], finish, 0)


def turn_kernel(wide, tall):
    def turn(b, _):
        tall[b] = jnp.transpose(wide[b])
        return 0

    lax.fori_loop(0, wide.shape[0], turn, 0)


def side_kernel(chunk, factor, seeds, slot, tiles_hbm, spam, weights, tiles, counts, sums, tile_sems):
    copies = fetch(tiles_hbm, tiles, tile_sems, chunk)
    for copy in copies:
        copy.start()
    histogram(seeds, counts, factor)
    blocks, columns = spam.shape[0], spam.shape[1]

    def keep(b, _):
        spam[b] = counts[pl.ds(b * columns, columns), :].astype(BF16)
        return 0

    lax.fori_loop(0, blocks, keep, 0)
    sums[...] = jnp.zeros(sums.shape, F32)
    unroll = 4
    for c, copy in enumerate(copies):
        copy.wait()

        def group(g, _):
            for u in range(unroll):
                k = c * chunk + g * unroll + u
                at = slot[k]
                sums[at] = sums[at] + jnp.sum(tiles[k].astype(F32), axis=0, keepdims=True)
            return 0

        lax.fori_loop(0, chunk // unroll, group, 0)
    row = lax.broadcasted_iota(I32, (EXTRA, BS), 0)

    def pack(p, _):
        value = sums[p]
        code = encode_scale(jnp.abs(value))
        whole = value * up(code)
        coarse = jnp.round(whole)
        fine = jnp.round((whole - coarse) * FINE)
        wide = lambda v: jnp.broadcast_to(v, (EXTRA, BS)).astype(I32)
        tail = jnp.where(row == 1, wide(code), jnp.where(row == 2, wide(coarse), jnp.where(row == 3, wide(fine), 0)))
        weights[p] = tail.astype(I16)
        return 0

    lax.fori_loop(0, sums.shape[0], pack, 0)


def cost(flops, bytes_moved):
    return pl.CostEstimate(flops=flops, bytes_accessed=bytes_moved, transcendentals=0)


def body(tiles, tile_src, tile_slot, slot_block, out_degree, good_seeds, spam_cores):
    count, size = tiles.shape[0], tiles.shape[1]
    hosts = out_degree.shape[0]
    blocks = hosts // size
    columns = good_seeds.shape[0]
    slots = slot_block.shape[0]
    chunk, slots_chunk = min(16, count), min(16, slots)
    dma = pltpu.SemaphoreType.DMA
    tile_sems, slot_sems = dma((count // chunk,)), dma((slots // slots_chunk,))
    sds = jax.ShapeDtypeStruct
    sent = sds((slots, columns + EXTRA, size), I16)
    asked = sds((slots, columns, size), BF16)
    panel = (blocks, columns, size)
    tiles_buf = pltpu.VMEM(tiles.shape, BF16)
    sent_buf = pltpu.VMEM(sent.shape, I16)
    asked_buf = pltpu.VMEM(asked.shape, BF16)
    total_buf = pltpu.VMEM(panel, F32)
    half_buf = pltpu.VMEM(panel, BF16)
    acc_buf = pltpu.VMEM((slots, columns, size), F32)
    counts_buf = pltpu.VMEM((blocks * columns, size), F32)
    degree = out_degree.reshape(blocks, 1, size)
    work = 2 * count * size * size * columns
    tile_bytes = 2 * count * size * size

    outgoing, good = pl.pallas_call(
        functools.partial(first_kernel, chunk, slots_chunk, float(hosts / good_seeds.shape[1])),
        out_shape=(sent, sds(panel, BF16)),
        in_specs=[VMEM, VMEM, SMEM, SMEM, SMEM, ANY],
        out_specs=(ANY, VMEM),
        scratch_shapes=[tiles_buf, half_buf, acc_buf, sent_buf, counts_buf, tile_sems, slot_sems],
        compiler_params=params(56),
        cost_estimate=cost(work, 2 * tile_bytes),
        name="first_push",
    )(good_seeds, degree, tile_src, tile_slot, slot_block, tiles)
    arrived = exchange(outgoing)
    spam_seeds, slot_after, _ = lax.optimization_barrier((spam_cores, tile_slot, good))
    spam, weights = pl.pallas_call(
        functools.partial(side_kernel, chunk, float(hosts / spam_cores.shape[1])),
        out_shape=(sds(panel, BF16), sds((slots, EXTRA, size), I16)),
        in_specs=[VMEM, SMEM, ANY],
        out_specs=(VMEM, VMEM),
        scratch_shapes=[tiles_buf, counts_buf, pltpu.VMEM((slots, 1, size), F32), tile_sems],
        compiler_params=params(40),
        cost_estimate=cost(work // 4, tile_bytes),
        name="side",
    )(spam_seeds, slot_after, tiles)
    ids = arrived[:, columns + 1, 0].astype(I32)
    outgoing = pl.pallas_call(
        functools.partial(second_kernel, chunk, slots_chunk),
        out_shape=sent,
        in_specs=[SMEM, VMEM, SMEM, SMEM, VMEM, VMEM, ANY, ANY],
        out_specs=ANY,
        scratch_shapes=[sent_buf, tiles_buf, half_buf, total_buf, acc_buf, sent_buf, slot_sems, tile_sems, slot_sems],
        compiler_params=params(56),
        cost_estimate=cost(work, 2 * tile_bytes),
        name="second_push",
    )(ids, degree, tile_src, tile_slot, good, weights, arrived, tiles)
    arrived = exchange(outgoing)
    asked_for, trust, shield, in_weight = pl.pallas_call(
        functools.partial(third_kernel, slots_chunk),
        out_shape=(asked, sds(panel, F32), sds(panel, F32), sds((blocks, 1, size), F32)),
        in_specs=[SMEM, VMEM, VMEM, ANY],
        out_specs=(ANY, VMEM, VMEM, VMEM),
        scratch_shapes=[sent_buf, total_buf, half_buf, asked_buf, slot_sems, slot_sems],
        compiler_params=params(56),
        cost_estimate=cost(work // 8, tile_bytes),
        name="first_shares",
    )(ids, good, spam, arrived)
    arrived = exchange(asked_for)
    trust_out = pl.pallas_call(
        turn_kernel,
        out_shape=sds((blocks, size, columns), F32),
        in_specs=[VMEM],
        out_specs=VMEM,
        compiler_params=params(16),
        cost_estimate=cost(work // 64, tile_bytes // 4),
        name="turn",
    )(trust)
    asked_for = pl.pallas_call(
        functools.partial(fourth_kernel, chunk, slots_chunk),
        out_shape=asked,
        in_specs=[SMEM, SMEM, SMEM, VMEM, VMEM, VMEM, ANY, ANY],
        out_specs=ANY,
        scratch_shapes=[asked_buf, tiles_buf, total_buf, half_buf, asked_buf, slot_sems, tile_sems, slot_sems],
        compiler_params=params(56),
        cost_estimate=cost(work, 2 * tile_bytes),
        name="second_shares",
    )(ids, tile_src, tile_slot, spam, shield, in_weight, arrived, tiles)
    arrived = exchange(asked_for)
    distrust = pl.pallas_call(
        functools.partial(fifth_kernel, chunk, slots_chunk),
        out_shape=sds((blocks, size, columns), F32),
        in_specs=[SMEM, SMEM, VMEM, ANY, ANY],
        out_specs=VMEM,
        scratch_shapes=[asked_buf, tiles_buf, total_buf, slot_sems, tile_sems],
        compiler_params=params(56),
        cost_estimate=cost(work, 2 * tile_bytes),
        name="last_pull",
    )(tile_src, tile_slot, spam, arrived, tiles)
    return trust_out.reshape(hosts, columns), distrust.reshape(hosts, columns)


def solution(mesh):
    in_specs = (
        P(AXES, None, None),
        P(AXES),
        P(AXES),
        P(AXES),
        P(AXES),
        P(None, AXES),
        P(None, AXES),
    )
    out_specs = (P(AXES, None), P(AXES, None))
    return jax.shard_map(body, mesh=mesh, in_specs=in_specs, out_specs=out_specs, check_vma=False)
```

time: 870 us -> 332 us (0.38); the launches traced: 858 us -> 331 us
  other arithmetic: 354 us -> 3.85 us
  local copies, waits for them, and re-layouts: 125 us -> 5.03 us
  waiting for transfers between devices: 202 us -> 89.1 us
  Pallas kernels: 0 us -> 93.8 us
  blocking collectives: 59 us -> 121 us
  matrix products: 54.4 us -> 0 us
  starting transfers between devices: 62.6 us -> 17.7 us
    scatter-add x8 -> x0, other arithmetic: 207 us -> none  [the longest x2 104 us: body(): outgoing = jax.ops.segment_sum(products, tile_slot, num_segments=slot_count)]
    unnamed x8 -> x0, other arithmetic: 131 us -> none
    all_to_all x5 -> x2, waiting for transfers between devices: 202 us -> 89.1 us  [exchange(): return lax.all_to_all(x, AXES, split_axis=0, concat_axis=0, tiled=True)]
    pallas_call x0 -> x7, Pallas kernels: none -> 93.8 us  [the longest x1 18.4 us: body(): pl.pallas_call(functools.partial(fourth_kernel, chunk, slots_chunk), out_...]
    dot_general x4 -> x0, local copies, waits for them, and re-layouts: 69.9 us -> none  [the longest x2 34.9 us: body(): jnp.einsum('kij,kjs->kis', tiles, targets, preferred_element_type=jnp.flo...]
    all_to_all x1 -> x2, blocking collectives: 59 us -> 121 us  [exchange(): return lax.all_to_all(x, AXES, split_axis=0, concat_axis=0, tiled=True)]
    dot_general x4 -> x0, matrix products: 54.4 us -> none  [the longest x2 28.7 us: body(): jnp.einsum('kij,kis->kjs', tiles, sources, preferred_element_type=jnp.flo...]
    gather x6 -> x0, local copies, waits for them, and re-layouts: 44.9 us -> none  [the longest x2 21.6 us: body(): targets = fetched[tile_slot]]
  transfers between devices with their start and end apart: 5 -> 2, of which waited for: 3 -> 2; matrix products, arithmetic and copies ran while one was open for 42% -> 0% of each run, Pallas kernels for 0% -> 4%
where the time goes in v1:
time: 332 us; the launch traced here: 331 us
  blocking collectives  121 us (36%)
  Pallas kernels  93.8 us (28%)
  waiting for transfers between devices  89.1 us (27%)
  starting transfers between devices  17.7 us (5%)
  local copies, waits for them, and re-layouts  5.03 us (2%)
  other arithmetic  3.85 us (1%)
    all_to_all x2, blocking collectives, exchange(): return lax.all_to_all(x, AXES, split_axis=0, concat_axis=0, tiled=True)  121 us
    all_to_all x2, waiting for transfers between devices, exchange(): return lax.all_to_all(x, AXES, split_axis=0, concat_axis=0, tiled=True)  89.1 us
    pallas_call x1, Pallas kernels, body(): pl.pallas_call(functools.partial(fourth_kernel, chunk, slots_chunk), out_...  18.4 us
    pallas_call x1, Pallas kernels, body(): pl.pallas_call(functools.partial(fifth_kernel, chunk, slots_chunk), out_s...  18.4 us
    all_to_all x2, starting transfers between devices, exchange(): return lax.all_to_all(x, AXES, split_axis=0, concat_axis=0, tiled=True)  17.7 us
    pallas_call x1, Pallas kernels, body(): pl.pallas_call(functools.partial(second_kernel, chunk, slots_chunk), out_...  17.4 us
    pallas_call x1, Pallas kernels, body(): pl.pallas_call(functools.partial(first_kernel, chunk, slots_chunk, float(...  17.4 us
    pallas_call x1, Pallas kernels, body(): pl.pallas_call(functools.partial(side_kernel, chunk, float(hosts / spam_c...  11.8 us
  transfers between devices with their start and end apart: 2, of which 2 were waited for; matrix products, arithmetic and copies ran while one was open for 0% of the time, Pallas kernels for 4%

profile of v1, /device:TPU:1, one launch (start us, length us, event | category | flops | bytes accessed | tf_op | source)
XLA Modules:
  0.0 331.1 jit_solution(5805387945040598842)
XLA Ops:
  0.6 17.4 %first_push.1 = (s16[128,136,128]{2,1,0:T(8,128)(2,1)}, bf16[16,128,128]{2,1,0:T(8,128)(2,1)}) custom-call(s32[128,128]{1,0:T(8,128)} %seeds.1, s32[16,1,128]{2,1,0:T(1,128)} %bitcast.5, s32[256]{0:T(256)} %src.7, s32[256]{0:T(256)} %slot.8, s32[128]{0:T(128)} %slot_block.1, bf16[256,128,128]{2,1,0:T(8,128)(2,1)} %tiles_hbm.9), custom_call_target="tpu_custom_call" | custom-call | flops 1073741824 | bytes 16777216 | tf_op jit(solution)/shard_map/first_push/pallas_call | solution.py:364
  18.0 0.0 copy-start.5
  18.0 0.0 copy-start.4
  18.0 11.9 %all-to-all-start = ((s16[128,136,128]{2,1,0:T(8,128)(2,1)}), s16[128,136,128]{2,1,0:T(8,128)(2,1)}, u32[]{:S(2)}, u32[]{:S(2)}) async-start(s16[128,136,128]{2,1,0:T(8,128)(2,1)} %get-tuple-element.12), calls=%async_computation | async-start | bytes 8912896 | tf_op jit(solution)/shard_map/all_to_all | solution.py:29
  30.0 0.0 copy-done.5
  30.0 0.1 copy.10.seeds
  30.1 0.0 copy-done.4
  30.1 0.0 copy-start
  30.1 3.4 %copy-done = bf16[256,128,128]{2,1,0:T(8,128)(2,1)S(1)} copy-done((bf16[256,128,128]{2,1,0:T(8,128)(2,1)S(1)}, bf16[256,128,128]{2,1,0:T(8,128)(2,1)}, u32[]{:S(2)}) %copy-start) | copy-done | bytes 8388632
  33.5 11.8 %side.1 = (bf16[16,128,128]{2,1,0:T(8,128)(2,1)S(1)}, s16[128,8,128]{2,1,0:T(8,128)(2,1)S(1)}) custom-call(s32[128,64]{1,0:T(8,128)S(1)} %copy.10.seeds, s32[256]{0:T(256)S(1)} %copy-done.4, bf16[256,128,128]{2,1,0:T(8,128)(2,1)S(1)} %copy-done), custom_call_target="tpu_custom_call" | custom-call | flops 268435456 | bytes 8388608 | tf_op jit(solution)/shard_map/side/pallas_call | solution.py:376
  45.3 0.0 copy-start.1
  45.3 0.8 copy-done.1
  46.1 0.0 copy-start.3
  46.1 0.7 copy-done.3
  46.8 38.7 %all-to-all-done.arrived_hbm = s16[128,136,128]{2,1,0:T(8,128)(2,1)} async-done(((s16[128,136,128]{2,1,0:T(8,128)(2,1)}), s16[128,136,128]{2,1,0:T(8,128)(2,1)}, u32[]{:S(2)}, u32[]{:S(2)}) %all-to-all-start) | async-done | bytes 4456480 | tf_op jit(solution)/shard_map/all_to_all | solution.py:29
  85.6 3.8 %fusion.ids = s32[128]{0:T(128)} fusion(s16[128,136,128]{2,1,0:T(8,128)(2,1)} %all-to-all-done.arrived_hbm), kind=kLoop, calls=%fused_computation.1 | loop fusion | flops 128 | bytes 768 | tf_op jit(solution)/shard_map/convert_element_type | solution.py:386
  89.4 17.4 %second_push.1 = s16[128,136,128]{2,1,0:T(8,128)(2,1)} custom-call(s32[128]{0:T(128)} %fusion.ids, s32[16,1,128]{2,1,0:T(1,128)} %bitcast.6, s32[256]{0:T(256)} %src.7, s32[256]{0:T(256)} %slot.8, bf16[16,128,128]{2,1,0:T(8,128)(2,1)} %get-tuple-element.13.good, s16[128,8,128]{2,1,0:T(8,128)(2,1)} %copy-done.3, ...), custom_call_target="tpu_custom_call" | custom-call | flops 1073741824 | bytes 16777216 | tf_op jit(solution)/shard_map/second_push/pallas_call | solution.py:387
  106.8 61.7 %all_to_all.20.arrived_hbm = s16[128,136,128]{2,1,0:T(8,128)(2,1)} all-to-all(s16[128,136,128]{2,1,0:T(8,128)(2,1)} %second_push.1), channel_id=1, replica_groups=mesh['row'=16,'col'=8] {'row','col'}, dimensions={0} | all-to-all | bytes 8912896 | tf_op jit(solution)/shard_map/all_to_all | solution.py:29
  168.5 7.9 %first_shares.1 = (bf16[128,128,128]{2,1,0:T(8,128)(2,1)}, f32[16,128,128]{2,1,0:T(8,128)}, f32[16,128,128]{2,1,0:T(8,128)}, f32[16,1,128]{2,1,0:T(1,128)}) custom-call(s32[128]{0:T(128)} %fusion.ids, bf16[16,128,128]{2,1,0:T(8,128)(2,1)} %get-tuple-element.13.good, bf16[16,128,128]{2,1,0:T(8,128)(2,1)} %copy-done.1, ...), custom_call_target="tpu_custom_call" | custom-call | flops 134217728 | bytes 8388608 | tf_op jit(solution)/shard_map/first_shares/pallas_call | solution.py:398
  176.4 59.0 %all_to_all.21.arrived_hbm = bf16[128,128,128]{2,1,0:T(8,128)(2,1)} all-to-all(bf16[128,128,128]{2,1,0:T(8,128)(2,1)} %get-tuple-element.21), channel_id=1, replica_groups=mesh['row'=16,'col'=8] {'row','col'}, dimensions={0} | all-to-all | bytes 8388608 | tf_op jit(solution)/shard_map/all_to_all | solution.py:29
  235.4 18.4 %second_shares.1 = bf16[128,128,128]{2,1,0:T(8,128)(2,1)} custom-call(s32[128]{0:T(128)} %fusion.ids, s32[256]{0:T(256)} %src.7, s32[256]{0:T(256)} %slot.8, bf16[16,128,128]{2,1,0:T(8,128)(2,1)} %copy-done.1, f32[16,128,128]{2,1,0:T(8,128)} %get-tuple-element.19.shield, f32[16,1,128]{2,1,0:T(1,128)} %get-tuple-element.20.in_weight, ...), custom_call_target="tpu_custom_call" | custom-call | flops 1073741824 | bytes 16777216 | tf_op jit(solution)/shard_map/second_shares/pallas_call | solution.py:418
  253.8 0.0 copy-start.2
  253.9 5.8 %all-to-all-start.3 = ((bf16[128,128,128]{2,1,0:T(8,128)(2,1)}), bf16[128,128,128]{2,1,0:T(8,128)(2,1)}, u32[]{:S(2)}, u32[]{:S(2)}) async-start(bf16[128,128,128]{2,1,0:T(8,128)(2,1)} %second_shares.1), calls=%async_computation.3 | async-start | bytes 8388608 | tf_op jit(solution)/shard_map/all_to_all | solution.py:29
  259.7 0.0 copy-done.2
  259.7 2.6 turn.1
  262.3 50.3 %all-to-all-done.3.arrived_hbm = bf16[128,128,128]{2,1,0:T(8,128)(2,1)} async-done(((bf16[128,128,128]{2,1,0:T(8,128)(2,1)}), bf16[128,128,128]{2,1,0:T(8,128)(2,1)}, u32[]{:S(2)}, u32[]{:S(2)}) %all-to-all-start.3) | async-done | bytes 4194336 | tf_op jit(solution)/shard_map/all_to_all | solution.py:29
  312.6 18.4 %last_pull.1 = f32[16,128,128]{2,1,0:T(8,128)} custom-call(s32[256]{0:T(256)} %src.7, s32[256]{0:T(256)} %slot.8, bf16[16,128,128]{2,1,0:T(8,128)(2,1)} %copy-done.1, bf16[128,128,128]{2,1,0:T(8,128)(2,1)} %all-to-all-done.3.arrived_hbm, bf16[256,128,128]{2,1,0:T(8,128)(2,1)} %tiles_hbm.9), custom_call_target="tpu_custom_call" | custom-call | flops 1073741824 | bytes 16777216 | tf_op jit(solution)/shard_map/last_pull/pallas_call | solution.py:429
Async XLA Ops:
  18.0 11.9 %copy-start.5 = (s32[128,64]{0,1:T(8,128)S(1)}, s32[128,64]{0,1:T(8,128)}, u32[]{:S(2)}) copy-start(s32[128,64]{0,1:T(8,128)} %param.13) | copy-start | bytes 98308
  18.0 12.0 %copy-start.4 = (s32[256]{0:T(256)S(1)}, s32[256]{0:T(256)}, u32[]{:S(2)}) copy-start(s32[256]{0:T(256)} %slot.8) | copy-start | bytes 3076
  18.0 67.5 %all-to-all-start = ((s16[128,136,128]{2,1,0:T(8,128)(2,1)}), s16[128,136,128]{2,1,0:T(8,128)(2,1)}, u32[]{:S(2)}, u32[]{:S(2)}) async-start(s16[128,136,128]{2,1,0:T(8,128)(2,1)} %get-tuple-element.12), calls=%async_computation | async-start | bytes 8912896 | tf_op jit(solution)/shard_map/all_to_all | solution.py:29
  30.1 3.4 %copy-start = (bf16[256,128,128]{2,1,0:T(8,128)(2,1)S(1)}, bf16[256,128,128]{2,1,0:T(8,128)(2,1)}, u32[]{:S(2)}) copy-start(bf16[256,128,128]{2,1,0:T(8,128)(2,1)} %tiles_hbm.9) | copy-start | bytes 25165828
  45.3 0.9 copy-start.1
  46.1 0.7 copy-start.3
  253.8 5.8 %copy-start.2 = (f32[16,128,128]{2,1,0:T(8,128)S(1)}, f32[16,128,128]{2,1,0:T(8,128)}, u32[]{:S(2)}) copy-start(f32[16,128,128]{2,1,0:T(8,128)} %get-tuple-element.18.wide) | copy-start | bytes 3145732
  253.9 58.7 %all-to-all-start.3 = ((bf16[128,128,128]{2,1,0:T(8,128)(2,1)}), bf16[128,128,128]{2,1,0:T(8,128)(2,1)}, u32[]{:S(2)}, u32[]{:S(2)}) async-start(bf16[128,128,128]{2,1,0:T(8,128)(2,1)} %second_shares.1), calls=%async_computation.3 | async-start | bytes 8388608 | tf_op jit(solution)/shard_map/all_to_all | solution.py:29

commit v2 on v1

v2 whole, which is shorter than its diff:
```python
import functools

import jax
import jax.numpy as jnp
from jax import lax
from jax.experimental import pallas as pl
from jax.experimental.pallas import tpu as pltpu
from jax.sharding import PartitionSpec as P

AXES = ("row", "col")
F32, BF16, I16, I32 = jnp.float32, jnp.bfloat16, jnp.int16, jnp.int32
BS = 128
EXTRA = 8
LOG_TOP = 14.997
STEPS = 64.0
LEAST = 1e-30
FINE = 65000.0

ANY = pl.BlockSpec(memory_space=pl.ANY)
SMEM = pl.BlockSpec(memory_space=pltpu.SMEM)
VMEM = pl.BlockSpec(memory_space=pltpu.VMEM)
HBM = pl.BlockSpec(memory_space=pltpu.HBM)


def params(mib):
    return pltpu.CompilerParams(vmem_limit_bytes=mib << 20)


def exchange(x):
    return lax.all_to_all(x, AXES, split_axis=0, concat_axis=0, tiled=True)


def fetch(hbm, vmem, sems, chunk):
    return [
        pltpu.make_async_copy(
            hbm.at[pl.ds(c * chunk, chunk)], vmem.at[pl.ds(c * chunk, chunk)], sems.at[c]
        )
        for c in range(hbm.shape[0] // chunk)
    ]


def run_chunks(copies, group):
    def step(c, _):
        for k, copy in enumerate(copies):

            @pl.when(c == k)
            def _():
                copy.wait()

        group(c)
        return 0

    lax.fori_loop(0, len(copies), step, 0)


def histogram(seeds_ref, out_ref, factor):
    columns, depth = seeds_ref.shape
    blocks = out_ref.shape[0] // columns
    unroll = 16

    def group(g, _):
        for u in range(unroll):
            s = g * unroll + u
            local = seeds_ref[pl.ds(s, 1), :] & (blocks * BS - 1)
            high = (lax.broadcasted_iota(I32, (blocks, depth), 0) == (local >> 7)).astype(F32).astype(BF16)
            low = (lax.broadcasted_iota(I32, (BS, depth), 0) == (local & (BS - 1))).astype(F32).astype(BF16)
            count = lax.dot_general(high, low, (((1,), (1,)), ((), ())), preferred_element_type=F32)
            out_ref[pl.ds(s, blocks, stride=columns), :] = count * factor
        return 0

    lax.fori_loop(0, columns // unroll, group, 0)


def encode_scale(largest):
    return jnp.ceil(jnp.log2(jnp.maximum(largest, LEAST)) * STEPS)


def up(code):
    return jnp.exp2(LOG_TOP - code * (1.0 / STEPS))


def down(code):
    return jnp.exp2(code * (1.0 / STEPS) - LOG_TOP)


def to_i16(x):
    return jnp.round(x).astype(I32).astype(I16)


def push(x_ref, tiles, copies, src, slot, acc):
    def clear(g, _):
        acc[g] = jnp.zeros(acc.shape[1:], F32)
        return 0

    lax.fori_loop(0, acc.shape[0], clear, 0)
    unroll = tiles.shape[0] // len(copies)

    def group(g):
        base = g * unroll
        parts = [
            jnp.dot(x_ref[src[base + u]], tiles[base + u], preferred_element_type=F32)
            for u in range(unroll)
        ]
        for u in range(unroll):
            at = slot[base + u]
            acc[at] = acc[at] + parts[u]

    run_chunks(copies, group)


def send(acc, extra_row, staged, out_hbm, sems, chunk):
    copies = []
    row = lax.broadcasted_iota(I32, (EXTRA, BS), 0)
    unroll = 4
    for c in range(acc.shape[0] // chunk):

        def group(g, _):
            for u in range(unroll):
                p = c * chunk + g * unroll + u
                block = acc[p]
                code = encode_scale(jnp.max(jnp.abs(block), axis=0, keepdims=True))
                staged[p, 0:BS, :] = to_i16(block * up(code))
                tail = jnp.where(row == 0, jnp.broadcast_to(code.astype(I32), (EXTRA, BS)), extra_row(p))
                staged[p, BS : BS + EXTRA, :] = tail.astype(I16)
            return 0

        lax.fori_loop(0, chunk // unroll, group, 0)
        copy = pltpu.make_async_copy(
            staged.at[pl.ds(c * chunk, chunk)], out_hbm.at[pl.ds(c * chunk, chunk)], sems.at[c]
        )
        copy.start()
        copies.append(copy)
    for copy in copies:
        copy.wait()


def receive(arrived, copies, ids, total, chunk, also=None):
    for b in range(total.shape[0]):
        total[b] = jnp.zeros(total.shape[1:], F32)
    unroll = min(8, chunk)
    for c, copy in enumerate(copies):
        if copy is not None:
            copy.wait()
        at_chunk = ids(c)

        def group(g, _):
            for u in range(unroll):
                one = g * unroll + u
                p = c * chunk + one
                tail = arrived[p, BS : BS + EXTRA, :].astype(I32).astype(F32)
                values = arrived[p, 0:BS, :].astype(I32).astype(F32) * down(tail[0:1])
                at = at_chunk(one)
                total[at] = total[at] + values
                if also is not None:
                    also(at, tail)
            return 0

        lax.fori_loop(0, chunk // unroll, group, 0)


def ids_in(ids):
    return lambda c: lambda one: ids[c, 0, one]


def first_kernel(slots_chunk, tiles_chunk, factor, src, slot, slot_block, seeds, degree, tiles_hbm,
                 out_hbm, good, x, tiles, counts, acc, staged, tile_sems, out_sems):
    copies = fetch(tiles_hbm, tiles, tile_sems, tiles_chunk)
    for copy in copies:
        copy.start()
    histogram(seeds, counts, factor)
    blocks, columns = x.shape[0], x.shape[1]

    def scale(b, _):
        trust = counts[pl.ds(b * columns, columns), :]
        good[b] = trust.astype(BF16)
        x[b] = (trust / degree[b].astype(F32)).astype(BF16)
        return 0

    lax.fori_loop(0, blocks, scale, 0)
    push(x, tiles, copies, src, slot, acc)
    send(acc, lambda p: slot_block[p], staged, out_hbm, out_sems, slots_chunk)


def second_kernel(slots_chunk, tiles_chunk, src, slot, degree, good, weights, arrived_hbm, tiles_hbm, out_hbm, ids_out,
                  arrived, tiles, x, total, acc, staged, ids, in_sems, tile_sems, id_sems, out_sems):
    incoming = fetch(arrived_hbm, arrived, in_sems, slots_chunk)
    copies = fetch(tiles_hbm, tiles, tile_sems, tiles_chunk)
    for copy in incoming + copies:
        copy.start()
    lane = lax.broadcasted_iota(I32, (1, BS), 1)
    moves = []

    def collect(c):
        incoming[c].wait()
        row = jnp.zeros((1, BS), I32)
        for u in range(slots_chunk):
            tail = arrived[c * slots_chunk + u, BS : BS + EXTRA, :].astype(I32)
            row = jnp.where(lane == u, tail[1:2], row)
        ids_out[c] = row
        move = pltpu.make_async_copy(ids_out.at[c], ids.at[c], id_sems.at[c])
        move.start()
        moves.append(move)

    chunks = len(incoming)
    for c in range(min(2, chunks)):
        collect(c)

    def ids_of(c):
        if c + 2 < chunks:
            collect(c + 2)
        moves[c].wait()
        return lambda one: ids[c, 0, one]

    receive(arrived, [None] * chunks, ids_of, total, slots_chunk)

    def scale(b, _):
        trust = 0.85 * total[b] + 0.15 * good[b].astype(F32)
        x[b] = (trust / degree[b].astype(F32)).astype(BF16)
        return 0

    lax.fori_loop(0, x.shape[0], scale, 0)
    push(x, tiles, copies, src, slot, acc)
    send(acc, lambda p: weights[p].astype(I32), staged, out_hbm, out_sems, slots_chunk)


def requests(share, ids, staged, out_hbm, sems, chunk):
    copies = []
    unroll = min(16, chunk)
    for c in range(staged.shape[0] // chunk):

        def group(g, _):
            for u in range(unroll):
                one = g * unroll + u
                staged[c * chunk + one] = share[ids[c, 0, one]]
            return 0

        lax.fori_loop(0, chunk // unroll, group, 0)
        copy = pltpu.make_async_copy(
            staged.at[pl.ds(c * chunk, chunk)], out_hbm.at[pl.ds(c * chunk, chunk)], sems.at[c]
        )
        copy.start()
        copies.append(copy)
    for copy in copies:
        copy.wait()


def third_kernel(slots_chunk, ids, good, spam, arrived_hbm, out_hbm, trust, shield, in_weight,
                 arrived, total, share, staged, in_sems, out_sems):
    incoming = fetch(arrived_hbm, arrived, in_sems, slots_chunk)
    for copy in incoming:
        copy.start()
    blocks = total.shape[0]
    in_weight[...] = jnp.ones(in_weight.shape, F32)

    def add_weight(at, tail):
        value = (tail[2:3] + tail[3:4] * (1.0 / FINE)) * down(tail[1:2])
        in_weight[at] = in_weight[at] + value

    receive(arrived, incoming, ids_in(ids), total, slots_chunk, add_weight)

    def finish(b, _):
        value = 0.85 * total[b] + 0.15 * good[b].astype(F32)
        trust[b] = value
        keep = 1.0 / (1.0 + value)
        shield[b] = keep
        share[b] = (keep * spam[b].astype(F32) / in_weight[b]).astype(BF16)
        return 0

    lax.fori_loop(0, blocks, finish, 0)
    requests(share, ids, staged, out_hbm, out_sems, slots_chunk)


def pack_kernel(pairs, tiles_hbm, out_hbm, tiles, staged, sem, out_sem):
    copy = pltpu.make_async_copy(tiles_hbm, tiles, sem)
    copy.start()
    copy.wait()
    size = tiles.shape[1]

    def turn(k, _):
        staged[k, 0:size, :] = jnp.transpose(tiles[pairs[1, k]])
        staged[k, size : 2 * size, :] = jnp.transpose(tiles[pairs[2, k]])
        return 0

    lax.fori_loop(0, staged.shape[0], turn, 0)
    back = pltpu.make_async_copy(staged, out_hbm, out_sem)
    back.start()
    back.wait()


def pull(slots_chunk, pairs, arrived_hbm, packed_hbm, y, packed, total, in_sems, pair_sems):
    incoming = fetch(arrived_hbm, y, in_sems, slots_chunk)
    unroll = packed.shape[0] // pair_sems.shape[0]
    copies = fetch(packed_hbm, packed, pair_sems, unroll)
    for copy in incoming + copies:
        copy.start()
    y[arrived_hbm.shape[0]] = jnp.zeros(y.shape[1:], BF16)
    for b in range(total.shape[0]):
        total[b] = jnp.zeros(total.shape[1:], F32)
    for copy in incoming:
        copy.wait()

    def group(g):
        parts = []
        for u in range(unroll):
            k = g * unroll + u
            left = jnp.concatenate([y[pairs[3, k]], y[pairs[4, k]]], axis=1)
            parts.append(jnp.dot(left, packed[k], preferred_element_type=F32))
        for u in range(unroll):
            at = pairs[0, g * unroll + u]
            total[at] = total[at] + parts[u]

    run_chunks(copies, group)


def fourth_kernel(slots_chunk, ids, pairs, spam, shield, in_weight, arrived_hbm, packed_hbm, out_hbm,
                  y, packed, total, share, staged, in_sems, pair_sems, out_sems):
    pull(slots_chunk, pairs, arrived_hbm, packed_hbm, y, packed, total, in_sems, pair_sems)

    def finish(b, _):
        value = 0.85 * total[b] + 0.15 * spam[b].astype(F32)
        share[b] = (shield[b] * value / in_weight[b]).astype(BF16)
        return 0

    lax.fori_loop(0, share.shape[0], finish, 0)
    requests(share, ids, staged, out_hbm, out_sems, slots_chunk)


def fifth_kernel(slots_chunk, pairs, spam, arrived_hbm, packed_hbm, distrust, y, packed, total, in_sems, pair_sems):
    pull(slots_chunk, pairs, arrived_hbm, packed_hbm, y, packed, total, in_sems, pair_sems)

    def finish(b, _):
        distrust[b] = jnp.transpose(0.85 * total[b] + 0.15 * spam[b].astype(F32))
        return 0

    lax.fori_loop(0, total.shape[0], finish, 0)


def turn_kernel(wide, tall):
    def turn(b, _):
        tall[b] = jnp.transpose(wide[b])
        return 0

    lax.fori_loop(0, wide.shape[0], turn, 0)


def side_kernel(factor, seeds, slot, tiles_hbm, spam, weights, tiles, counts, sums, sem):
    copy = pltpu.make_async_copy(tiles_hbm, tiles, sem)
    copy.start()
    histogram(seeds, counts, factor)
    blocks, columns = spam.shape[0], spam.shape[1]

    def keep(b, _):
        spam[b] = counts[pl.ds(b * columns, columns), :].astype(BF16)
        return 0

    lax.fori_loop(0, blocks, keep, 0)
    copy.wait()
    sums[...] = jnp.zeros(sums.shape, F32)
    unroll = 4

    def group(g, _):
        for u in range(unroll):
            k = g * unroll + u
            at = slot[k]
            sums[at] = sums[at] + jnp.sum(tiles[k].astype(F32), axis=0, keepdims=True)
        return 0

    lax.fori_loop(0, tiles.shape[0] // unroll, group, 0)
    row = lax.broadcasted_iota(I32, (EXTRA, BS), 0)

    def pack(p, _):
        value = sums[p]
        code = encode_scale(jnp.abs(value))
        whole = value * up(code)
        coarse = jnp.round(whole)
        fine = jnp.round((whole - coarse) * FINE)
        wide = lambda v: jnp.broadcast_to(v, (EXTRA, BS)).astype(I32)
        tail = jnp.where(row == 1, wide(code), jnp.where(row == 2, wide(coarse), jnp.where(row == 3, wide(fine), 0)))
        weights[p] = tail.astype(I16)
        return 0

    lax.fori_loop(0, sums.shape[0], pack, 0)


def cost(flops, bytes_moved):
    return pl.CostEstimate(flops=flops, bytes_accessed=bytes_moved, transcendentals=0)


def pair_up(tile_src, tile_slot, blocks, slots):
    count = tile_src.shape[0]
    pairs = (count + blocks) // 2
    k = jnp.arange(count, dtype=I32)
    same = tile_src[:, None] == tile_src[None, :]
    rank = jnp.sum((same & (k[None, :] < k[:, None])).astype(I32), axis=1)
    block = jnp.arange(blocks, dtype=I32)
    held = jnp.sum((tile_src[:, None] == block[None, :]).astype(I32), axis=0)
    halves = (held + 1) // 2
    first = jnp.sum(jnp.where(block[:, None] < block[None, :], halves[:, None], 0), axis=0)
    start = jnp.sum(jnp.where(tile_src[:, None] == block[None, :], first[None, :], 0), axis=1)
    place = start + rank // 2
    here = place[None, :] == jnp.arange(pairs, dtype=I32)[:, None]
    even = here & (rank % 2 == 0)[None, :]
    odd = here & (rank % 2 == 1)[None, :]
    pick = lambda mask, v: jnp.sum(jnp.where(mask, v[None, :], 0), axis=1)
    shifted = tile_slot - slots
    return jnp.stack(
        [pick(even, tile_src), pick(even, k), pick(odd, k), slots + pick(even, shifted), slots + pick(odd, shifted)]
    )


def cost(flops, bytes_moved):
    return pl.CostEstimate(flops=flops, bytes_accessed=bytes_moved, transcendentals=0)


def body(tiles, tile_src, tile_slot, slot_block, out_degree, good_seeds, spam_cores):
    count, size = tiles.shape[0], tiles.shape[1]
    hosts = out_degree.shape[0]
    blocks = hosts // size
    columns = good_seeds.shape[0]
    slots = slot_block.shape[0]
    slots_chunk = min(16, slots)
    chunks = slots // slots_chunk
    sems = pltpu.SemaphoreType.DMA((chunks,))
    sds = jax.ShapeDtypeStruct
    sent = pltpu.HBM((slots, columns + EXTRA, size), I16)
    asked = pltpu.HBM((slots, columns, size), BF16)
    ids_shape = sds((chunks, 1, size), I32)
    panel = (blocks, columns, size)
    sent_buf = pltpu.VMEM(sent.shape, I16)
    asked_buf = pltpu.VMEM(asked.shape, BF16)
    y_buf = pltpu.VMEM((slots + 1, columns, size), BF16)
    total_buf = pltpu.VMEM(panel, F32)
    half_buf = pltpu.VMEM(panel, BF16)
    acc_buf = pltpu.VMEM((slots, columns, size), F32)
    counts_buf = pltpu.VMEM((blocks * columns, size), F32)
    degree = out_degree.reshape(blocks, 1, size)
    work = 2 * count * size * size * columns
    tile_bytes = 2 * count * size * size
    tiles_chunk = min(32, count)
    tiles_buf = pltpu.VMEM(tiles.shape, BF16)
    tile_sems = pltpu.SemaphoreType.DMA((count // tiles_chunk,))
    couples = (count + blocks) // 2
    pair_sems = pltpu.SemaphoreType.DMA((next(n for n in (8, 5, 4, 2, 1) if couples % n == 0),))
    packed_shape = (couples, 2 * size, size)
    packed_buf = pltpu.VMEM(packed_shape, BF16)

    outgoing, good = pl.pallas_call(
        functools.partial(first_kernel, slots_chunk, tiles_chunk, float(hosts / good_seeds.shape[1])),
        out_shape=(sent, sds(panel, BF16)),
        in_specs=[SMEM, SMEM, SMEM, VMEM, VMEM, ANY],
        out_specs=(HBM, VMEM),
        scratch_shapes=[half_buf, tiles_buf, counts_buf, acc_buf, sent_buf, tile_sems, sems],
        compiler_params=params(57),
        cost_estimate=cost(work, 2 * tile_bytes),
        name="first_push",
    )(tile_src, tile_slot, slot_block, good_seeds, degree, tiles)
    arrived = exchange(outgoing)
    spam_seeds, src_after, slot_after, _ = lax.optimization_barrier((spam_cores, tile_src, tile_slot, outgoing))
    spam, weights = pl.pallas_call(
        functools.partial(side_kernel, float(hosts / spam_cores.shape[1])),
        out_shape=(sds(panel, BF16), sds((slots, EXTRA, size), I16)),
        in_specs=[VMEM, SMEM, ANY],
        out_specs=(VMEM, VMEM),
        scratch_shapes=[tiles_buf, counts_buf, pltpu.VMEM((slots, 1, size), F32), pltpu.SemaphoreType.DMA],
        compiler_params=params(57),
        cost_estimate=cost(work // 4, tile_bytes),
        name="side",
    )(spam_seeds, slot_after, tiles)
    pairs = pair_up(src_after, slot_after, blocks, slots)
    outgoing, ids = pl.pallas_call(
        functools.partial(second_kernel, slots_chunk, tiles_chunk),
        out_shape=(sent, ids_shape),
        in_specs=[SMEM, SMEM, VMEM, VMEM, VMEM, HBM, ANY],
        out_specs=(HBM, VMEM),
        scratch_shapes=[
            sent_buf, tiles_buf, half_buf, total_buf, acc_buf, sent_buf, pltpu.SMEM(ids_shape.shape, I32),
            sems, tile_sems, sems, sems,
        ],
        compiler_params=params(57),
        cost_estimate=cost(work, 2 * tile_bytes),
        name="second_push",
    )(tile_src, tile_slot, degree, good, weights, arrived, tiles)
    arrived = exchange(outgoing)
    pairs_after, _ = lax.optimization_barrier((pairs, outgoing))
    packed = pl.pallas_call(
        pack_kernel,
        out_shape=pltpu.HBM(packed_shape, BF16),
        in_specs=[SMEM, ANY],
        out_specs=HBM,
        scratch_shapes=[tiles_buf, packed_buf, pltpu.SemaphoreType.DMA, pltpu.SemaphoreType.DMA],
        compiler_params=params(57),
        cost_estimate=cost(work // 4, 2 * tile_bytes),
        name="pack",
    )(pairs_after, tiles)
    asked_for, trust, shield, in_weight = pl.pallas_call(
        functools.partial(third_kernel, slots_chunk),
        out_shape=(asked, sds(panel, F32), sds(panel, F32), sds((blocks, 1, size), F32)),
        in_specs=[SMEM, VMEM, VMEM, HBM],
        out_specs=(HBM, VMEM, VMEM, VMEM),
        scratch_shapes=[sent_buf, total_buf, half_buf, asked_buf, sems, sems],
        compiler_params=params(57),
        cost_estimate=cost(work // 8, tile_bytes),
        name="first_shares",
    )(ids, good, spam, arrived)
    arrived = exchange(asked_for)
    trust_out = pl.pallas_call(
        turn_kernel,
        out_shape=sds((blocks, size, columns), F32),
        in_specs=[VMEM],
        out_specs=VMEM,
        compiler_params=params(16),
        cost_estimate=cost(work // 64, tile_bytes // 4),
        name="turn",
    )(trust)
    asked_for = pl.pallas_call(
        functools.partial(fourth_kernel, slots_chunk),
        out_shape=asked,
        in_specs=[SMEM, SMEM, VMEM, VMEM, VMEM, HBM, HBM],
        out_specs=HBM,
        scratch_shapes=[y_buf, packed_buf, total_buf, half_buf, asked_buf, sems, pair_sems, sems],
        compiler_params=params(57),
        cost_estimate=cost(work, 2 * tile_bytes),
        name="second_shares",
    )(ids, pairs, spam, shield, in_weight, arrived, packed)
    arrived = exchange(asked_for)
    distrust = pl.pallas_call(
        functools.partial(fifth_kernel, slots_chunk),
        out_shape=sds((blocks, size, columns), F32),
        in_specs=[SMEM, VMEM, HBM, HBM],
        out_specs=VMEM,
        scratch_shapes=[y_buf, packed_buf, total_buf, sems, pair_sems],
        compiler_params=params(57),
        cost_estimate=cost(work, 2 * tile_bytes),
        name="last_pull",
    )(pairs, spam, arrived, packed)
    return trust_out.reshape(hosts, columns), distrust.reshape(hosts, columns)


def solution(mesh):
    in_specs = (
        P(AXES, None, None),
        P(AXES),
        P(AXES),
        P(AXES),
        P(AXES),
        P(None, AXES),
        P(None, AXES),
    )
    out_specs = (P(AXES, None), P(AXES, None))
    return jax.shard_map(body, mesh=mesh, in_specs=in_specs, out_specs=out_specs, check_vma=False)
```

time: 332 us -> 307 us (0.925)
  blocking collectives: 121 us -> 61.7 us
  waiting for transfers between devices: 89.1 us -> 128 us
  starting transfers between devices: 17.7 us -> 23.4 us
  local copies, waits for them, and re-layouts: 5.03 us -> 1.37 us
  Pallas kernels: 93.8 us -> 90.2 us
    all_to_all x2 -> x1, blocking collectives: 121 us -> 61.7 us  [exchange(): return lax.all_to_all(x, AXES, split_axis=0, concat_axis=0, tiled=True)]
    all_to_all x2 -> x3, waiting for transfers between devices: 89.1 us -> 128 us  [exchange(): return lax.all_to_all(x, AXES, split_axis=0, concat_axis=0, tiled=True)]
    all_to_all x2 -> x3, starting transfers between devices: 17.7 us -> 23.4 us  [exchange(): return lax.all_to_all(x, AXES, split_axis=0, concat_axis=0, tiled=True)]
    unnamed x12 -> x8, local copies, waits for them, and re-layouts: 4.94 us -> 0.03 us
    convert_element_type x1 -> x0, other arithmetic: 3.85 us -> none  [body(): ids = arrived[:, columns + 1, 0].astype(I32)]
    pallas_call x5 -> x6, Pallas kernels: 83.4 us -> 80 us  [the longest x1 17.6 us: body(): pl.pallas_call(pack_kernel, out_shape=pltpu.HBM(packed_shape, BF16), in_s...]
  transfers between devices with their start and end apart: 2 -> 3, of which waited for: 2 -> 3; matrix products, arithmetic and copies ran while one was open for 0% -> 1% of each run, Pallas kernels for 4% -> 10%
where the time goes in v2:
time: 307 us; the launch traced here: 306 us
  waiting for transfers between devices  128 us (42%)
  Pallas kernels  90.2 us (29%)
  blocking collectives  61.7 us (20%)
  starting transfers between devices  23.4 us (8%)
    all_to_all x3, waiting for transfers between devices, exchange(): return lax.all_to_all(x, AXES, split_axis=0, concat_axis=0, tiled=True)  128 us
    all_to_all x1, blocking collectives, exchange(): return lax.all_to_all(x, AXES, split_axis=0, concat_axis=0, tiled=True)  61.7 us
    all_to_all x3, starting transfers between devices, exchange(): return lax.all_to_all(x, AXES, split_axis=0, concat_axis=0, tiled=True)  23.4 us
    pallas_call x1, Pallas kernels, body(): pl.pallas_call(pack_kernel, out_shape=pltpu.HBM(packed_shape, BF16), in_s...  17.6 us
    pallas_call x1, Pallas kernels, body(): pl.pallas_call(functools.partial(second_kernel, slots_chunk, tiles_chunk)...  14.9 us
    pallas_call x1, Pallas kernels, body(): pl.pallas_call(functools.partial(first_kernel, slots_chunk, tiles_chunk,...  12.9 us
    pallas_call x1, Pallas kernels, body(): pl.pallas_call(functools.partial(fourth_kernel, slots_chunk), out_shape=a...  11.7 us
    pallas_call x1, Pallas kernels, body(): pl.pallas_call(functools.partial(fifth_kernel, slots_chunk), out_shape=sd...  11.7 us
  transfers between devices with their start and end apart: 3, of which 3 were waited for; matrix products, arithmetic and copies ran while one was open for 1% of the time, Pallas kernels for 10%

profile of v2, /device:TPU:1, one launch (start us, length us, event | category | flops | bytes accessed | tf_op | source)
XLA Modules:
  0.0 306.1 jit_solution(6953549915130802935)
XLA Ops:
  0.6 12.9 %first_push.1 = (s16[128,136,128]{2,1,0:T(8,128)(2,1)}, bf16[16,128,128]{2,1,0:T(8,128)(2,1)}) custom-call(s32[256]{0:T(256)} %src.3, s32[256]{0:T(256)} %slot.4, s32[128]{0:T(128)} %slot_block.1, s32[128,128]{1,0:T(8,128)} %seeds.1, s32[16,1,128]{2,1,0:T(1,128)} %bitcast.10, bf16[256,128,128]{2,1,0:T(8,128)(2,1)} %tiles_hbm.7), custom_call_target="tpu_custom_call" | custom-call | flops 1073741824 | bytes 16777216 | tf_op jit(solution)/shard_map/first_push/pallas_call | solution.py:447
  13.5 0.0 copy-start.2
  13.6 11.9 %all-to-all-start = ((s16[128,136,128]{2,1,0:T(8,128)(2,1)}), s16[128,136,128]{2,1,0:T(8,128)(2,1)}, u32[]{:S(2)}, u32[]{:S(2)}) async-start(s16[128,136,128]{2,1,0:T(8,128)(2,1)} %get-tuple-element.17), calls=%async_computation | async-start | bytes 8912896 | tf_op jit(solution)/shard_map/all_to_all | solution.py:30
  25.5 0.0 copy-done.2
  25.5 0.7 copy.10.seeds
  26.2 11.3 %side.1 = (bf16[16,128,128]{2,1,0:T(8,128)(2,1)}, s16[128,8,128]{2,1,0:T(8,128)(2,1)}) custom-call(s32[128,64]{1,0:T(8,128)} %copy.10.seeds, s32[256]{0:T(256)} %slot.4, bf16[256,128,128]{2,1,0:T(8,128)(2,1)} %tiles_hbm.7), custom_call_target="tpu_custom_call" | custom-call | flops 268435456 | bytes 8388608 | tf_op jit(solution)/shard_map/side/pallas_call | solution.py:459
  37.5 43.6 %all-to-all-done.arrived_hbm = s16[128,136,128]{2,1,0:T(8,128)(2,1)} async-done(((s16[128,136,128]{2,1,0:T(8,128)(2,1)}), s16[128,136,128]{2,1,0:T(8,128)(2,1)}, u32[]{:S(2)}, u32[]{:S(2)}) %all-to-all-start) | async-done | bytes 4456480 | tf_op jit(solution)/shard_map/all_to_all | solution.py:30
  81.1 14.9 %second_push.1 = (s16[128,136,128]{2,1,0:T(8,128)(2,1)}, s32[8,1,128]{2,1,0:T(1,128)}) custom-call(s32[256]{0:T(256)} %src.3, s32[256]{0:T(256)} %slot.4, s32[16,1,128]{2,1,0:T(1,128)} %bitcast.11, bf16[16,128,128]{2,1,0:T(8,128)(2,1)} %get-tuple-element.16.good, s16[128,8,128]{2,1,0:T(8,128)(2,1)} %get-tuple-element.20.weights, ...), custom_call_target="tpu_custom_call" | custom-call | flops 1073741824 | bytes 16777216 | tf_op jit(solution)/shard_map/second_push/pallas_call | solution.py:470
  96.0 61.7 %all_to_all.20.arrived_hbm = s16[128,136,128]{2,1,0:T(8,128)(2,1)} all-to-all(s16[128,136,128]{2,1,0:T(8,128)(2,1)} %get-tuple-element.23), channel_id=1, replica_groups=mesh['row'=16,'col'=8] {'row','col'}, dimensions={0} | all-to-all | bytes 8912896 | tf_op jit(solution)/shard_map/all_to_all | solution.py:30
  157.7 7.7 %first_shares.1 = (bf16[128,128,128]{2,1,0:T(8,128)(2,1)}, f32[16,128,128]{2,1,0:T(8,128)}, f32[16,128,128]{2,1,0:T(8,128)}, f32[16,1,128]{2,1,0:T(1,128)}) custom-call(s32[8,1,128]{2,1,0:T(1,128)} %get-tuple-element.21.ids, bf16[16,128,128]{2,1,0:T(8,128)(2,1)} %get-tuple-element.16.good, bf16[16,128,128]{2,1,0:T(8,128)(2,1)} %get-tuple-element.22.spam, ...), custom_call_target="tpu_custom_call" | custom-call | flops 134217728 | bytes 8388608 | tf_op jit(solution)/shard_map/first_shares/pallas_call | solution.py:495
  165.3 0.0 copy-start.1
  165.3 0.0 copy-start.3
  165.4 5.7 %all-to-all-start.2 = ((bf16[128,128,128]{2,1,0:T(8,128)(2,1)}), bf16[128,128,128]{2,1,0:T(8,128)(2,1)}, u32[]{:S(2)}, u32[]{:S(2)}) async-start(bf16[128,128,128]{2,1,0:T(8,128)(2,1)} %get-tuple-element.28), calls=%async_computation.2 | async-start | bytes 8388608 | tf_op jit(solution)/shard_map/all_to_all | solution.py:30
  171.1 0.0 copy-done.1
  171.1 0.1 convert_reduce_fusion.1
  171.2 0.1 select_reduce_fusion.6
  171.3 0.1 select_reduce_fusion.5
  171.4 0.2 convert_reduce_fusion
  171.6 0.0 copy-done.3
  171.6 0.3 select_reduce_fusion
  171.9 0.6 stack.17.pairs
  172.6 17.6 %pack.1.packed_hbm = bf16[136,256,128]{2,1,0:T(8,128)(2,1)} custom-call(s32[5,136]{1,0:T(8,128)} %stack.17.pairs, bf16[256,128,128]{2,1,0:T(8,128)(2,1)} %tiles_hbm.7), custom_call_target="tpu_custom_call" | custom-call | flops 268435456 | bytes 16777216 | tf_op jit(solution)/shard_map/pack/pallas_call | solution.py:485
  190.1 33.8 %all-to-all-done.2.arrived_hbm = bf16[128,128,128]{2,1,0:T(8,128)(2,1)} async-done(((bf16[128,128,128]{2,1,0:T(8,128)(2,1)}), bf16[128,128,128]{2,1,0:T(8,128)(2,1)}, u32[]{:S(2)}, u32[]{:S(2)}) %all-to-all-start.2) | async-done | bytes 4194336 | tf_op jit(solution)/shard_map/all_to_all | solution.py:30
  223.9 11.7 %second_shares.1 = bf16[128,128,128]{2,1,0:T(8,128)(2,1)} custom-call(s32[8,1,128]{2,1,0:T(1,128)} %get-tuple-element.21.ids, s32[5,136]{1,0:T(8,128)} %stack.17.pairs, bf16[16,128,128]{2,1,0:T(8,128)(2,1)} %get-tuple-element.22.spam, f32[16,128,128]{2,1,0:T(8,128)} %get-tuple-element.26.shield, f32[16,1,128]{2,1,0:T(1,128)} %get-tuple-element.27.in_weight, ...), custom_call_target="tpu_custom_call" | custom-call | flops 1073741824 | bytes 16777216 | tf_op jit(solution)/shard_map/second_shares/pallas_call | solution.py:515
  235.7 0.0 copy-start
  235.7 5.8 %all-to-all-start.3 = ((bf16[128,128,128]{2,1,0:T(8,128)(2,1)}), bf16[128,128,128]{2,1,0:T(8,128)(2,1)}, u32[]{:S(2)}, u32[]{:S(2)}) async-start(bf16[128,128,128]{2,1,0:T(8,128)(2,1)} %second_shares.1), calls=%async_computation.3 | async-start | bytes 8388608 | tf_op jit(solution)/shard_map/all_to_all | solution.py:30
  241.5 0.0 copy-done
  241.5 2.6 turn.1
  244.1 50.3 %all-to-all-done.3.arrived_hbm = bf16[128,128,128]{2,1,0:T(8,128)(2,1)} async-done(((bf16[128,128,128]{2,1,0:T(8,128)(2,1)}), bf16[128,128,128]{2,1,0:T(8,128)(2,1)}, u32[]{:S(2)}, u32[]{:S(2)}) %all-to-all-start.3) | async-done | bytes 4194336 | tf_op jit(solution)/shard_map/all_to_all | solution.py:30
  294.4 11.7 %last_pull.1 = f32[16,128,128]{2,1,0:T(8,128)} custom-call(s32[5,136]{1,0:T(8,128)} %stack.17.pairs, bf16[16,128,128]{2,1,0:T(8,128)(2,1)} %get-tuple-element.22.spam, bf16[128,128,128]{2,1,0:T(8,128)(2,1)} %all-to-all-done.3.arrived_hbm, bf16[136,256,128]{2,1,0:T(8,128)(2,1)} %pack.1.packed_hbm), custom_call_target="tpu_custom_call" | custom-call | flops 1073741824 | bytes 16777216 | tf_op jit(solution)/shard_map/last_pull/pallas_call | solution.py:526
  (6 shorter events, 0.1 us)
Async XLA Ops:
  13.5 11.9 %copy-start.2 = (s32[128,64]{0,1:T(8,128)S(1)}, s32[128,64]{0,1:T(8,128)}, u32[]{:S(2)}) copy-start(s32[128,64]{0,1:T(8,128)} %param.13) | copy-start | bytes 98308
  13.6 67.5 %all-to-all-start = ((s16[128,136,128]{2,1,0:T(8,128)(2,1)}), s16[128,136,128]{2,1,0:T(8,128)(2,1)}, u32[]{:S(2)}, u32[]{:S(2)}) async-start(s16[128,136,128]{2,1,0:T(8,128)(2,1)} %get-tuple-element.17), calls=%async_computation | async-start | bytes 8912896 | tf_op jit(solution)/shard_map/all_to_all | solution.py:30
  165.3 5.7 %copy-start.1 = (s32[256]{0:T(256)S(1)}, s32[256]{0:T(256)}, u32[]{:S(2)}) copy-start(s32[256]{0:T(256)} %src.3) | copy-start | bytes 3076
  165.3 6.3 %copy-start.3 = (s32[256]{0:T(256)S(1)}, s32[256]{0:T(256)}, u32[]{:S(2)}) copy-start(s32[256]{0:T(256)} %slot.4) | copy-start | bytes 3076
  165.4 58.6 %all-to-all-start.2 = ((bf16[128,128,128]{2,1,0:T(8,128)(2,1)}), bf16[128,128,128]{2,1,0:T(8,128)(2,1)}, u32[]{:S(2)}, u32[]{:S(2)}) async-start(bf16[128,128,128]{2,1,0:T(8,128)(2,1)} %get-tuple-element.28), calls=%async_computation.2 | async-start | bytes 8388608 | tf_op jit(solution)/shard_map/all_to_all | solution.py:30
  235.7 5.8 %copy-start = (f32[16,128,128]{2,1,0:T(8,128)S(1)}, f32[16,128,128]{2,1,0:T(8,128)}, u32[]{:S(2)}) copy-start(f32[16,128,128]{2,1,0:T(8,128)} %get-tuple-element.24.wide) | copy-start | bytes 3145732
  235.7 58.7 %all-to-all-start.3 = ((bf16[128,128,128]{2,1,0:T(8,128)(2,1)}), bf16[128,128,128]{2,1,0:T(8,128)(2,1)}, u32[]{:S(2)}, u32[]{:S(2)}) async-start(bf16[128,128,128]{2,1,0:T(8,128)(2,1)} %second_shares.1), calls=%async_computation.3 | async-start | bytes 8388608 | tf_op jit(solution)/shard_map/all_to_all | solution.py:30

commit v3 on v2

--- a/solution.py
+++ b/solution.py
@@ -26,6 +26,10 @@
     return pltpu.CompilerParams(vmem_limit_bytes=mib << 20)
 
 
+def held(x):
+    return pltpu.with_memory_space_constraint(x, pltpu.HBM)
+
+
 def exchange(x):
     return lax.all_to_all(x, AXES, split_axis=0, concat_axis=0, tiled=True)
 
@@ -56,19 +60,28 @@
 def histogram(seeds_ref, out_ref, factor):
     columns, depth = seeds_ref.shape
     blocks = out_ref.shape[0] // columns
-    unroll = 16
+    unroll = 8
+    none = jnp.zeros((blocks, depth), BF16)
 
     def group(g, _):
         for u in range(unroll):
-            s = g * unroll + u
-            local = seeds_ref[pl.ds(s, 1), :] & (blocks * BS - 1)
-            high = (lax.broadcasted_iota(I32, (blocks, depth), 0) == (local >> 7)).astype(F32).astype(BF16)
-            low = (lax.broadcasted_iota(I32, (BS, depth), 0) == (local & (BS - 1))).astype(F32).astype(BF16)
-            count = lax.dot_general(high, low, (((1,), (1,)), ((), ())), preferred_element_type=F32)
-            out_ref[pl.ds(s, blocks, stride=columns), :] = count * factor
-        return 0
-
-    lax.fori_loop(0, columns // unroll, group, 0)
+            s = (g * unroll + u) * 2
+            highs, lows = [], []
+            for one in range(2):
+                local = seeds_ref[pl.ds(s + one, 1), :] & (blocks * BS - 1)
+                highs.append((lax.broadcasted_iota(I32, (blocks, depth), 0) == (local >> 7)).astype(F32).astype(BF16))
+                lows.append((lax.broadcasted_iota(I32, (BS, depth), 0) == (local & (BS - 1))).astype(F32).astype(BF16))
+            left = jnp.concatenate(
+                [jnp.concatenate([highs[0], none], axis=1), jnp.concatenate([none, highs[1]], axis=1)], axis=0
+            )
+            count = lax.dot_general(
+                left, jnp.concatenate(lows, axis=1), (((1,), (1,)), ((), ())), preferred_element_type=F32
+            )
+            for one in range(2):
+                out_ref[pl.ds(s + one, blocks, stride=columns), :] = count[one * blocks : (one + 1) * blocks] * factor
+        return 0
+
+    lax.fori_loop(0, columns // (2 * unroll), group, 0)
 
 
 def encode_scale(largest):
@@ -92,7 +105,7 @@
         acc[g] = jnp.zeros(acc.shape[1:], F32)
         return 0
 
-    lax.fori_loop(0, acc.shape[0], clear, 0)
+    lax.fori_loop(0, acc.shape[0], clear, 0, unroll=4)
     unroll = tiles.shape[0] // len(copies)
 
     def group(g):
@@ -111,7 +124,7 @@
 def send(acc, extra_row, staged, out_hbm, sems, chunk):
     copies = []
     row = lax.broadcasted_iota(I32, (EXTRA, BS), 0)
-    unroll = 4
+    unroll = min(8, chunk)
     for c in range(acc.shape[0] // chunk):
 
         def group(g, _):
@@ -137,7 +150,7 @@
 def receive(arrived, copies, ids, total, chunk, also=None):
     for b in range(total.shape[0]):
         total[b] = jnp.zeros(total.shape[1:], F32)
-    unroll = min(8, chunk)
+    unroll = min(16, chunk)
     for c, copy in enumerate(copies):
         if copy is not None:
             copy.wait()
@@ -176,7 +189,7 @@
         x[b] = (trust / degree[b].astype(F32)).astype(BF16)
         return 0
 
-    lax.fori_loop(0, blocks, scale, 0)
+    lax.fori_loop(0, blocks, scale, 0, unroll=4)
     push(x, tiles, copies, src, slot, acc)
     send(acc, lambda p: slot_block[p], staged, out_hbm, out_sems, slots_chunk)
 
@@ -218,7 +231,7 @@
         x[b] = (trust / degree[b].astype(F32)).astype(BF16)
         return 0
 
-    lax.fori_loop(0, x.shape[0], scale, 0)
+    lax.fori_loop(0, x.shape[0], scale, 0, unroll=4)
     push(x, tiles, copies, src, slot, acc)
     send(acc, lambda p: weights[p].astype(I32), staged, out_hbm, out_sems, slots_chunk)
 
@@ -266,7 +279,7 @@
         share[b] = (keep * spam[b].astype(F32) / in_weight[b]).astype(BF16)
         return 0
 
-    lax.fori_loop(0, blocks, finish, 0)
+    lax.fori_loop(0, blocks, finish, 0, unroll=4)
     requests(share, ids, staged, out_hbm, out_sems, slots_chunk)
 
 
@@ -291,8 +304,10 @@
     incoming = fetch(arrived_hbm, y, in_sems, slots_chunk)
     unroll = packed.shape[0] // pair_sems.shape[0]
     copies = fetch(packed_hbm, packed, pair_sems, unroll)
-    for copy in incoming + copies:
-        copy.start()
+    for copy in incoming:
+        copy.start(priority=0)
+    for copy in copies:
+        copy.start(priority=1)
     y[arrived_hbm.shape[0]] = jnp.zeros(y.shape[1:], BF16)
     for b in range(total.shape[0]):
         total[b] = jnp.zeros(total.shape[1:], F32)
@@ -321,7 +336,7 @@
         share[b] = (shield[b] * value / in_weight[b]).astype(BF16)
         return 0
 
-    lax.fori_loop(0, share.shape[0], finish, 0)
+    lax.fori_loop(0, share.shape[0], finish, 0, unroll=4)
     requests(share, ids, staged, out_hbm, out_sems, slots_chunk)
 
 
@@ -332,7 +347,7 @@
         distrust[b] = jnp.transpose(0.85 * total[b] + 0.15 * spam[b].astype(F32))
         return 0
 
-    lax.fori_loop(0, total.shape[0], finish, 0)
+    lax.fori_loop(0, total.shape[0], finish, 0, unroll=4)
 
 
 def turn_kernel(wide, tall):
@@ -436,11 +451,11 @@
     degree = out_degree.reshape(blocks, 1, size)
     work = 2 * count * size * size * columns
     tile_bytes = 2 * count * size * size
-    tiles_chunk = min(32, count)
+    tiles_chunk = min(128, count)
     tiles_buf = pltpu.VMEM(tiles.shape, BF16)
     tile_sems = pltpu.SemaphoreType.DMA((count // tiles_chunk,))
     couples = (count + blocks) // 2
-    pair_sems = pltpu.SemaphoreType.DMA((next(n for n in (8, 5, 4, 2, 1) if couples % n == 0),))
+    pair_sems = pltpu.SemaphoreType.DMA((next(n for n in (4, 5, 2, 1) if couples % n == 0),))
     packed_shape = (couples, 2 * size, size)
     packed_buf = pltpu.VMEM(packed_shape, BF16)
 
@@ -450,10 +465,10 @@
         in_specs=[SMEM, SMEM, SMEM, VMEM, VMEM, ANY],
         out_specs=(HBM, VMEM),
         scratch_shapes=[half_buf, tiles_buf, counts_buf, acc_buf, sent_buf, tile_sems, sems],
-        compiler_params=params(57),
+        compiler_params=params(40),
         cost_estimate=cost(work, 2 * tile_bytes),
         name="first_push",
-    )(tile_src, tile_slot, slot_block, good_seeds, degree, tiles)
+    )(tile_src, tile_slot, slot_block, good_seeds, degree, held(tiles))
     arrived = exchange(outgoing)
     spam_seeds, src_after, slot_after, _ = lax.optimization_barrier((spam_cores, tile_src, tile_slot, outgoing))
     spam, weights = pl.pallas_call(
@@ -462,10 +477,10 @@
         in_specs=[VMEM, SMEM, ANY],
         out_specs=(VMEM, VMEM),
         scratch_shapes=[tiles_buf, counts_buf, pltpu.VMEM((slots, 1, size), F32), pltpu.SemaphoreType.DMA],
-        compiler_params=params(57),
+        compiler_params=params(40),
         cost_estimate=cost(work // 4, tile_bytes),
         name="side",
-    )(spam_seeds, slot_after, tiles)
+    )(spam_seeds, slot_after, held(tiles))
     pairs = pair_up(src_after, slot_after, blocks, slots)
     outgoing, ids = pl.pallas_call(
         functools.partial(second_kernel, slots_chunk, tiles_chunk),
@@ -476,10 +491,10 @@
             sent_buf, tiles_buf, half_buf, total_buf, acc_buf, sent_buf, pltpu.SMEM(ids_shape.shape, I32),
             sems, tile_sems, sems, sems,
         ],
-        compiler_params=params(57),
+        compiler_params=params(40),
         cost_estimate=cost(work, 2 * tile_bytes),
         name="second_push",
-    )(tile_src, tile_slot, degree, good, weights, arrived, tiles)
+    )(tile_src, tile_slot, degree, good, weights, held(arrived), held(tiles))
     arrived = exchange(outgoing)
     pairs_after, _ = lax.optimization_barrier((pairs, outgoing))
     packed = pl.pallas_call(
@@ -488,20 +503,20 @@
         in_specs=[SMEM, ANY],
         out_specs=HBM,
         scratch_shapes=[tiles_buf, packed_buf, pltpu.SemaphoreType.DMA, pltpu.SemaphoreType.DMA],
-        compiler_params=params(57),
+        compiler_params=params(40),
         cost_estimate=cost(work // 4, 2 * tile_bytes),
         name="pack",
-    )(pairs_after, tiles)
+    )(pairs_after, held(tiles))
     asked_for, trust, shield, in_weight = pl.pallas_call(
         functools.partial(third_kernel, slots_chunk),
         out_shape=(asked, sds(panel, F32), sds(panel, F32), sds((blocks, 1, size), F32)),
         in_specs=[SMEM, VMEM, VMEM, HBM],
         out_specs=(HBM, VMEM, VMEM, VMEM),
         scratch_shapes=[sent_buf, total_buf, half_buf, asked_buf, sems, sems],
-        compiler_params=params(57),
+        compiler_params=params(40),
         cost_estimate=cost(work // 8, tile_bytes),
         name="first_shares",
-    )(ids, good, spam, arrived)
+    )(ids, good, spam, held(arrived))
     arrived = exchange(asked_for)
     trust_out = pl.pallas_call(
         turn_kernel,
@@ -518,10 +533,10 @@
         in_specs=[SMEM, SMEM, VMEM, VMEM, VMEM, HBM, HBM],
         out_specs=HBM,
         scratch_shapes=[y_buf, packed_buf, total_buf, half_buf, asked_buf, sems, pair_sems, sems],
-        compiler_params=params(57),
+        compiler_params=params(40),
         cost_estimate=cost(work, 2 * tile_bytes),
         name="second_shares",
-    )(ids, pairs, spam, shield, in_weight, arrived, packed)
+    )(ids, pairs, spam, shield, in_weight, held(arrived), held(packed))
     arrived = exchange(asked_for)
     distrust = pl.pallas_call(
         functools.partial(fifth_kernel, slots_chunk),
@@ -529,10 +544,10 @@
         in_specs=[SMEM, VMEM, HBM, HBM],
         out_specs=VMEM,
         scratch_shapes=[y_buf, packed_buf, total_buf, sems, pair_sems],
-        compiler_params=params(57),
+        compiler_params=params(40),
         cost_estimate=cost(work, 2 * tile_bytes),
         name="last_pull",
-    )(pairs, spam, arrived, packed)
+    )(pairs, spam, held(arrived), held(packed))
     return trust_out.reshape(hosts, columns), distrust.reshape(hosts, columns)
 
 

time: 307 us -> 295 us (0.961)
  Pallas kernels: 90.2 us -> 74.1 us
    unnamed x8 -> x18, local copies, waits for them, and re-layouts: 0.03 us -> 3.57 us
    pallas_call x1, Pallas kernels: 14.9 us -> 11.4 us  [body(): pl.pallas_call(functools.partial(second_kernel, slots_chunk, tiles_chunk)...]
    pallas_call x1, Pallas kernels: 12.9 us -> 9.39 us  [body(): pl.pallas_call(functools.partial(first_kernel, slots_chunk, tiles_chunk,...]
    pallas_call x1, Pallas kernels: 11.7 us -> 8.35 us  [body(): pl.pallas_call(functools.partial(fifth_kernel, slots_chunk), out_shape=sd...]
  transfers between devices with their start and end apart: 3 -> 3, of which waited for: 3 -> 3; matrix products, arithmetic and copies ran while one was open for 1% -> 0% of each run, Pallas kernels for 10% -> 10%
where the time goes in v3:
time: 295 us
  waiting for transfers between devices  130 us (44%)
  Pallas kernels  74.1 us (25%)
  blocking collectives  61.7 us (21%)
  starting transfers between devices  23.4 us (8%)
  local copies, waits for them, and re-layouts  3.68 us (1%)
    all_to_all x3, waiting for transfers between devices, exchange(): return lax.all_to_all(x, AXES, split_axis=0, concat_axis=0, tiled=True)  130 us
    all_to_all x1, blocking collectives, exchange(): return lax.all_to_all(x, AXES, split_axis=0, concat_axis=0, tiled=True)  61.7 us
    all_to_all x3, starting transfers between devices, exchange(): return lax.all_to_all(x, AXES, split_axis=0, concat_axis=0, tiled=True)  23.4 us
    pallas_call x1, Pallas kernels, body(): pl.pallas_call(pack_kernel, out_shape=pltpu.HBM(packed_shape, BF16), in_s...  17.4 us
    pallas_call x1, Pallas kernels, body(): pl.pallas_call(functools.partial(second_kernel, slots_chunk, tiles_chunk)...  11.4 us
    pallas_call x1, Pallas kernels, body(): pl.pallas_call(functools.partial(side_kernel, float(hosts / spam_cores.sh...  10.1 us
    pallas_call x1, Pallas kernels, body(): pl.pallas_call(functools.partial(first_kernel, slots_chunk, tiles_chunk,...  9.39 us
    pallas_call x1, Pallas kernels, body(): pl.pallas_call(functools.partial(fourth_kernel, slots_chunk), out_shape=a...  9.2 us
  transfers between devices with their start and end apart: 3, of which 3 were waited for; matrix products, arithmetic and copies ran while one was open for 0% of the time, Pallas kernels for 10%

profile of v3, /device:TPU:1, one launch (start us, length us, event | category | flops | bytes accessed | tf_op | source)
XLA Modules:
  0.0 294.8 jit_solution(12132465901168704414)
XLA Ops:
  0.6 0.0 copy-start
  0.6 0.8 copy-done
  1.5 0.7 copy-done.1
  2.2 0.7 copy-done.3
  2.8 0.7 copy-done.5
  3.5 0.7 copy-done.7
  4.2 9.4 %first_push.1 = (s16[128,136,128]{2,1,0:T(8,128)(2,1)}, bf16[16,128,128]{2,1,0:T(8,128)(2,1)S(1)}) custom-call(s32[256]{0:T(256)S(1)} %copy-done.1, s32[256]{0:T(256)S(1)} %copy-done.5, s32[128]{0:T(128)S(1)} %copy-done.7, s32[128,128]{1,0:T(8,128)S(1)} %copy-done, s32[16,1,128]{2,1,0:T(1,128)S(1)} %bitcast.8, bf16[256,128,128]{2,1,0:T(8,128)(2,1)} %tiles_hbm.7), custom_call_target="tpu_custom_call" | custom-call | flops 1073741824 | bytes 16777216 | tf_op jit(solution)/shard_map/first_push/pallas_call | solution.py:462
  13.6 0.0 copy-start.8
  13.6 0.0 copy-start.6
  13.6 11.9 %all-to-all-start = ((s16[128,136,128]{2,1,0:T(8,128)(2,1)}), s16[128,136,128]{2,1,0:T(8,128)(2,1)}, u32[]{:S(2)}, u32[]{:S(2)}) async-start(s16[128,136,128]{2,1,0:T(8,128)(2,1)} %get-tuple-element.17), calls=%async_computation | async-start | bytes 8912896 | tf_op jit(solution)/shard_map/all_to_all | solution.py:34
  25.5 0.0 copy-start.2
  25.5 0.0 copy-start.4
  25.6 0.1 copy.10.seeds
  25.7 10.1 %side.1 = (bf16[16,128,128]{2,1,0:T(8,128)(2,1)S(1)}, s16[128,8,128]{2,1,0:T(8,128)(2,1)S(1)}) custom-call(s32[128,64]{1,0:T(8,128)S(1)} %copy.10.seeds, s32[256]{0:T(256)S(1)} %copy-done.6, bf16[256,128,128]{2,1,0:T(8,128)(2,1)} %tiles_hbm.7), custom_call_target="tpu_custom_call" | custom-call | flops 268435456 | bytes 8388608 | tf_op jit(solution)/shard_map/side/pallas_call | solution.py:474
  35.8 45.3 %all-to-all-done.arrived_hbm = s16[128,136,128]{2,1,0:T(8,128)(2,1)} async-done(((s16[128,136,128]{2,1,0:T(8,128)(2,1)}), s16[128,136,128]{2,1,0:T(8,128)(2,1)}, u32[]{:S(2)}, u32[]{:S(2)}) %all-to-all-start) | async-done | bytes 4456480 | tf_op jit(solution)/shard_map/all_to_all | solution.py:34
  81.1 0.0 copy-done.4
  81.1 11.4 %second_push.1 = (s16[128,136,128]{2,1,0:T(8,128)(2,1)}, s32[8,1,128]{2,1,0:T(1,128)S(1)}) custom-call(s32[256]{0:T(256)S(1)} %copy-done.2, s32[256]{0:T(256)S(1)} %copy-done.6, s32[16,1,128]{2,1,0:T(1,128)S(1)} %bitcast.9, bf16[16,128,128]{2,1,0:T(8,128)(2,1)S(1)} %get-tuple-element.16.good, s16[128,8,128]{2,1,0:T(8,128)(2,1)S(1)} %get-tuple-element.20.weights, ...), custom_call_target="tpu_custom_call" | custom-call | flops 1073741824 | bytes 16777216 | tf_op jit(solution)/shard_map/second_push/pallas_call | solution.py:485
  92.5 61.7 %all_to_all.20.arrived_hbm = s16[128,136,128]{2,1,0:T(8,128)(2,1)} all-to-all(s16[128,136,128]{2,1,0:T(8,128)(2,1)} %get-tuple-element.23), channel_id=1, replica_groups=mesh['row'=16,'col'=8] {'row','col'}, dimensions={0} | all-to-all | bytes 8912896 | tf_op jit(solution)/shard_map/all_to_all | solution.py:34
  154.2 5.7 %first_shares.1 = (bf16[128,128,128]{2,1,0:T(8,128)(2,1)}, f32[16,128,128]{2,1,0:T(8,128)S(1)}, f32[16,128,128]{2,1,0:T(8,128)S(1)}, f32[16,1,128]{2,1,0:T(1,128)S(1)}) custom-call(s32[8,1,128]{2,1,0:T(1,128)S(1)} %get-tuple-element.21.ids, bf16[16,128,128]{2,1,0:T(8,128)(2,1)S(1)} %get-tuple-element.16.good, ...), custom_call_target="tpu_custom_call" | custom-call | flops 134217728 | bytes 8388608 | tf_op jit(solution)/shard_map/first_shares/pallas_call | solution.py:510
  159.9 5.7 %all-to-all-start.2 = ((bf16[128,128,128]{2,1,0:T(8,128)(2,1)}), bf16[128,128,128]{2,1,0:T(8,128)(2,1)}, u32[]{:S(2)}, u32[]{:S(2)}) async-start(bf16[128,128,128]{2,1,0:T(8,128)(2,1)} %get-tuple-element.28), calls=%async_computation.2 | async-start | bytes 8388608 | tf_op jit(solution)/shard_map/all_to_all | solution.py:34
  165.6 0.1 convert_reduce_fusion.1
  165.7 0.1 select_reduce_fusion.6
  165.8 0.1 select_reduce_fusion.5
  165.9 0.2 convert_reduce_fusion
  166.1 0.3 select_reduce_fusion
  166.5 17.4 %pack.1.packed_hbm = bf16[136,256,128]{2,1,0:T(8,128)(2,1)} custom-call(s32[5,136]{1,0:T(8,128)S(1)} %stack.17.pairs, bf16[256,128,128]{2,1,0:T(8,128)(2,1)} %tiles_hbm.7), custom_call_target="tpu_custom_call" | custom-call | flops 268435456 | bytes 16777216 | tf_op jit(solution)/shard_map/pack/pallas_call | solution.py:500
  183.9 34.5 %all-to-all-done.2.arrived_hbm = bf16[128,128,128]{2,1,0:T(8,128)(2,1)} async-done(((bf16[128,128,128]{2,1,0:T(8,128)(2,1)}), bf16[128,128,128]{2,1,0:T(8,128)(2,1)}, u32[]{:S(2)}, u32[]{:S(2)}) %all-to-all-start.2) | async-done | bytes 4194336 | tf_op jit(solution)/shard_map/all_to_all | solution.py:34
  218.4 9.2 %second_shares.1 = bf16[128,128,128]{2,1,0:T(8,128)(2,1)} custom-call(s32[8,1,128]{2,1,0:T(1,128)S(1)} %get-tuple-element.21.ids, s32[5,136]{1,0:T(8,128)S(1)} %stack.17.pairs, bf16[16,128,128]{2,1,0:T(8,128)(2,1)S(1)} %get-tuple-element.22.spam, f32[16,128,128]{2,1,0:T(8,128)S(1)} %get-tuple-element.26.shield, ...), custom_call_target="tpu_custom_call" | custom-call | flops 1073741824 | bytes 16777216 | tf_op jit(solution)/shard_map/second_shares/pallas_call | solution.py:530
  227.7 5.8 %all-to-all-start.3 = ((bf16[128,128,128]{2,1,0:T(8,128)(2,1)}), bf16[128,128,128]{2,1,0:T(8,128)(2,1)}, u32[]{:S(2)}, u32[]{:S(2)}) async-start(bf16[128,128,128]{2,1,0:T(8,128)(2,1)} %second_shares.1), calls=%async_computation.3 | async-start | bytes 8388608 | tf_op jit(solution)/shard_map/all_to_all | solution.py:34
  233.5 2.6 turn.1
  236.0 50.2 %all-to-all-done.3.arrived_hbm = bf16[128,128,128]{2,1,0:T(8,128)(2,1)} async-done(((bf16[128,128,128]{2,1,0:T(8,128)(2,1)}), bf16[128,128,128]{2,1,0:T(8,128)(2,1)}, u32[]{:S(2)}, u32[]{:S(2)}) %all-to-all-start.3) | async-done | bytes 4194336 | tf_op jit(solution)/shard_map/all_to_all | solution.py:34
  286.3 8.3 %last_pull.1 = f32[16,128,128]{2,1,0:T(8,128)} custom-call(s32[5,136]{1,0:T(8,128)S(1)} %stack.17.pairs, bf16[16,128,128]{2,1,0:T(8,128)(2,1)S(1)} %get-tuple-element.22.spam, bf16[128,128,128]{2,1,0:T(8,128)(2,1)} %all-to-all-done.3.arrived_hbm, bf16[136,256,128]{2,1,0:T(8,128)(2,1)} %pack.1.packed_hbm), custom_call_target="tpu_custom_call" | custom-call | flops 1073741824 | bytes 16777216 | tf_op jit(solution)/shard_map/last_pull/pallas_call | solution.py:541
  (14 shorter events, 0.1 us)
Async XLA Ops:
  0.6 0.8 copy-start
  1.5 0.7 copy-start.1
  2.1 0.7 copy-start.3
  2.8 0.7 copy-start.5
  3.5 0.7 copy-start.7
  13.6 11.9 %copy-start.8 = (s32[128,64]{0,1:T(8,128)S(1)}, s32[128,64]{0,1:T(8,128)}, u32[]{:S(2)}) copy-start(s32[128,64]{0,1:T(8,128)} %param.13) | copy-start | bytes 98308
  13.6 12.1 %copy-start.6 = (s32[256]{0:T(256)S(1)}, s32[256]{0:T(256)}, u32[]{:S(2)}) copy-start(s32[256]{0:T(256)} %slot.4) | copy-start | bytes 3076
  13.6 67.5 %all-to-all-start = ((s16[128,136,128]{2,1,0:T(8,128)(2,1)}), s16[128,136,128]{2,1,0:T(8,128)(2,1)}, u32[]{:S(2)}, u32[]{:S(2)}) async-start(s16[128,136,128]{2,1,0:T(8,128)(2,1)} %get-tuple-element.17), calls=%async_computation | async-start | bytes 8912896 | tf_op jit(solution)/shard_map/all_to_all | solution.py:34
  25.5 55.6 %copy-start.2 = (s32[256]{0:T(256)S(1)}, s32[256]{0:T(256)}, u32[]{:S(2)}) copy-start(s32[256]{0:T(256)} %src.3) | copy-start | bytes 3076
  25.5 55.6 %copy-start.4 = (s32[2048]{0:T(1024)S(1)}, s32[2048]{0:T(1024)}, u32[]{:S(2)}) copy-start(s32[2048]{0:T(1024)} %param.11) | copy-start | bytes 24580
  159.9 58.6 %all-to-all-start.2 = ((bf16[128,128,128]{2,1,0:T(8,128)(2,1)}), bf16[128,128,128]{2,1,0:T(8,128)(2,1)}, u32[]{:S(2)}, u32[]{:S(2)}) async-start(bf16[128,128,128]{2,1,0:T(8,128)(2,1)} %get-tuple-element.28), calls=%async_computation.2 | async-start | bytes 8388608 | tf_op jit(solution)/shard_map/all_to_all | solution.py:34
  227.7 58.6 %all-to-all-start.3 = ((bf16[128,128,128]{2,1,0:T(8,128)(2,1)}), bf16[128,128,128]{2,1,0:T(8,128)(2,1)}, u32[]{:S(2)}, u32[]{:S(2)}) async-start(bf16[128,128,128]{2,1,0:T(8,128)(2,1)} %second_shares.1), calls=%async_computation.3 | async-start | bytes 8388608 | tf_op jit(solution)/shard_map/all_to_all | solution.py:34

commit v4 on v3

--- a/solution.py
+++ b/solution.py
@@ -28,6 +28,11 @@
 
 def held(x):
     return pltpu.with_memory_space_constraint(x, pltpu.HBM)
+
+
+def swap(x):
+    cores = lax.axis_size("col")
+    return lax.ppermute(x, "col", [(k, k ^ 1) for k in range(cores)])
 
 
 def exchange(x):
@@ -121,7 +126,7 @@
     run_chunks(copies, group)
 
 
-def send(acc, extra_row, staged, out_hbm, sems, chunk):
+def send(acc, extra_row, staged, out_hbm, sems, chunk, lists=None):
     copies = []
     row = lax.broadcasted_iota(I32, (EXTRA, BS), 0)
     unroll = min(8, chunk)
@@ -135,6 +140,8 @@
                 staged[p, 0:BS, :] = to_i16(block * up(code))
                 tail = jnp.where(row == 0, jnp.broadcast_to(code.astype(I32), (EXTRA, BS)), extra_row(p))
                 staged[p, BS : BS + EXTRA, :] = tail.astype(I16)
+                if lists is not None:
+                    staged[p, BS + EXTRA :, :] = lists[u % 2]
             return 0
 
         lax.fori_loop(0, chunk // unroll, group, 0)
@@ -175,7 +182,7 @@
     return lambda c: lambda one: ids[c, 0, one]
 
 
-def first_kernel(slots_chunk, tiles_chunk, factor, src, slot, slot_block, seeds, degree, tiles_hbm,
+def first_kernel(slots_chunk, tiles_chunk, factor, src, slot, slot_block, seeds, spam_turned, degree, tiles_hbm,
                  out_hbm, good, x, tiles, counts, acc, staged, tile_sems, out_sems):
     copies = fetch(tiles_hbm, tiles, tile_sems, tiles_chunk)
     for copy in copies:
@@ -191,7 +198,10 @@
 
     lax.fori_loop(0, blocks, scale, 0, unroll=4)
     push(x, tiles, copies, src, slot, acc)
-    send(acc, lambda p: slot_block[p], staged, out_hbm, out_sems, slots_chunk)
+    local = (spam_turned[...] & (blocks * BS - 1)).astype(I16)
+    half = local.shape[0] // 2
+    lists = (local[0:half], local[half:])
+    send(acc, lambda p: slot_block[p], staged, out_hbm, out_sems, slots_chunk, lists)
 
 
 def second_kernel(slots_chunk, tiles_chunk, src, slot, degree, good, weights, arrived_hbm, tiles_hbm, out_hbm, ids_out,
@@ -257,12 +267,12 @@
         copy.wait()
 
 
-def third_kernel(slots_chunk, ids, good, spam, arrived_hbm, out_hbm, trust, shield, in_weight,
-                 arrived, total, share, staged, in_sems, out_sems):
+def third_kernel(slots_chunk, ids, good, spam, spam_hosts, arrived_hbm, out_hbm, trust, shield, in_weight,
+                 arrived, total, share, staged, in_sems, out_sem):
     incoming = fetch(arrived_hbm, arrived, in_sems, slots_chunk)
     for copy in incoming:
         copy.start()
-    blocks = total.shape[0]
+    blocks, columns = total.shape[0], total.shape[1]
     in_weight[...] = jnp.ones(in_weight.shape, F32)
 
     def add_weight(at, tail):
@@ -270,17 +280,68 @@
         in_weight[at] = in_weight[at] + value
 
     receive(arrived, incoming, ids_in(ids), total, slots_chunk, add_weight)
-
-    def finish(b, _):
+    local = spam_hosts[...] & (blocks * BS - 1)
+    low, high = local & (BS - 1), local >> 7
+    half = columns // 2
+    left = lax.broadcasted_iota(I32, low.shape, 1) < BS // 2
+
+    def finish(b, listed):
         value = 0.85 * total[b] + 0.15 * good[b].astype(F32)
         trust[b] = value
         keep = 1.0 / (1.0 + value)
         shield[b] = keep
-        share[b] = (keep * spam[b].astype(F32) / in_weight[b]).astype(BF16)
-        return 0
-
-    lax.fori_loop(0, blocks, finish, 0, unroll=4)
-    requests(share, ids, staged, out_hbm, out_sems, slots_chunk)
+        part = keep * spam[b].astype(F32) / in_weight[b]
+        found = [
+            jnp.take_along_axis(p, low, axis=1, mode="promise_in_bounds") for p in (part[0:half], part[half:])
+        ]
+        return jnp.where(high == b, jnp.where(left, found[0], found[1]), listed)
+
+    listed = lax.fori_loop(0, blocks, finish, jnp.zeros(low.shape, F32), unroll=4)
+    share[...] = listed.astype(BF16)
+    rows = half // 2
+    parts = (share[0:rows], share[rows:])
+    for p in range(staged.shape[0]):
+        staged[p] = parts[p % 2]
+    copy = pltpu.make_async_copy(staged, out_hbm, out_sem)
+    copy.start()
+    copy.wait()
+
+
+def two_halves(core, mine_hbm, other_hbm, whole, sems, rows):
+    return [
+        pltpu.make_async_copy(
+            half, whole.at[:, pl.ds(pl.multiple_of(place * rows, rows), rows)], sems.at[n]
+        )
+        for n, (half, place) in enumerate(((mine_hbm, core[0]), (other_hbm, 1 - core[0])))
+    ]
+
+
+def places_kernel(core, slot_block, mine_hbm, other_hbm, out_hbm, lists, staged, sems, out_sem):
+    columns = staged.shape[1]
+    depth = lists.shape[1]
+    copies = two_halves(core, mine_hbm, other_hbm, lists, sems, depth // 2)
+    for copy in copies:
+        copy.start()
+    for copy in copies:
+        copy.wait()
+    host = lax.broadcasted_iota(I32, (BS, columns), 0).astype(F32).astype(BF16)
+    lower = lax.broadcasted_iota(I32, (columns, BS), 0) >= columns // 2
+
+    def one(q, _):
+        offset = lists[q].astype(I32) - slot_block[q] * BS
+        offset = offset.astype(F32).astype(BF16)
+        at = jnp.full((BS, columns), -1.0, BF16)
+        for j in range(depth):
+            at = jnp.where(offset[j : j + 1] == host, jnp.array(j, BF16), at)
+        place = jnp.transpose(at.astype(F32))
+        place = jnp.where(lower & (place >= 0.0), place + float(depth), place)
+        staged[q] = place.astype(I32).astype(I16)
+        return 0
+
+    lax.fori_loop(0, staged.shape[0], one, 0)
+    back = pltpu.make_async_copy(staged, out_hbm, out_sem)
+    back.start()
+    back.wait()
 
 
 def pack_kernel(pairs, tiles_hbm, out_hbm, tiles, staged, sem, out_sem):
@@ -300,19 +361,11 @@
     back.wait()
 
 
-def pull(slots_chunk, pairs, arrived_hbm, packed_hbm, y, packed, total, in_sems, pair_sems):
-    incoming = fetch(arrived_hbm, y, in_sems, slots_chunk)
-    unroll = packed.shape[0] // pair_sems.shape[0]
-    copies = fetch(packed_hbm, packed, pair_sems, unroll)
-    for copy in incoming:
-        copy.start(priority=0)
-    for copy in copies:
-        copy.start(priority=1)
-    y[arrived_hbm.shape[0]] = jnp.zeros(y.shape[1:], BF16)
+def pull(pairs, y, packed, copies, total):
+    y[y.shape[0] - 1] = jnp.zeros(y.shape[1:], BF16)
     for b in range(total.shape[0]):
         total[b] = jnp.zeros(total.shape[1:], F32)
-    for copy in incoming:
-        copy.wait()
+    unroll = packed.shape[0] // len(copies)
 
     def group(g):
         parts = []
@@ -327,9 +380,35 @@
     run_chunks(copies, group)
 
 
-def fourth_kernel(slots_chunk, ids, pairs, spam, shield, in_weight, arrived_hbm, packed_hbm, out_hbm,
-                  y, packed, total, share, staged, in_sems, pair_sems, out_sems):
-    pull(slots_chunk, pairs, arrived_hbm, packed_hbm, y, packed, total, in_sems, pair_sems)
+def fourth_kernel(slots_chunk, core, ids, pairs, spam, shield, in_weight, mine_hbm, other_hbm, places_hbm, packed_hbm,
+                  out_hbm, values, places, y, packed, total, share, staged, half_sems, in_sems, pair_sems, out_sems):
+    halves = two_halves(core, mine_hbm, other_hbm, values, half_sems, values.shape[1] // 2)
+    incoming = fetch(places_hbm, places, in_sems, slots_chunk)
+    copies = fetch(packed_hbm, packed, pair_sems, packed.shape[0] // pair_sems.shape[0])
+    for copy in halves + incoming:
+        copy.start(priority=0)
+    for copy in copies:
+        copy.start(priority=1)
+    for copy in halves:
+        copy.wait()
+    unroll = min(8, slots_chunk)
+    rows = values.shape[1]
+
+    def expand(c):
+        def group(g, _):
+            for u in range(unroll):
+                q = c * slots_chunk + g * unroll + u
+                value = values[q].astype(F32)
+                for h in range(2):
+                    place = places[q, h * rows : (h + 1) * rows, :].astype(I32)
+                    found = jnp.take_along_axis(value, jnp.maximum(place, 0), axis=1, mode="promise_in_bounds")
+                    y[q, h * rows : (h + 1) * rows, :] = jnp.where(place >= 0, found, 0.0).astype(BF16)
+            return 0
+
+        lax.fori_loop(0, slots_chunk // unroll, group, 0)
+
+    run_chunks(incoming, expand)
+    pull(pairs, y, packed, copies, total)
 
     def finish(b, _):
         value = 0.85 * total[b] + 0.15 * spam[b].astype(F32)
@@ -341,7 +420,15 @@
 
 
 def fifth_kernel(slots_chunk, pairs, spam, arrived_hbm, packed_hbm, distrust, y, packed, total, in_sems, pair_sems):
-    pull(slots_chunk, pairs, arrived_hbm, packed_hbm, y, packed, total, in_sems, pair_sems)
+    incoming = fetch(arrived_hbm, y, in_sems, slots_chunk)
+    copies = fetch(packed_hbm, packed, pair_sems, packed.shape[0] // pair_sems.shape[0])
+    for copy in incoming:
+        copy.start(priority=0)
+    for copy in copies:
+        copy.start(priority=1)
+    for copy in incoming:
+        copy.wait()
+    pull(pairs, y, packed, copies, total)
 
     def finish(b, _):
         distrust[b] = jnp.transpose(0.85 * total[b] + 0.15 * spam[b].astype(F32))
@@ -459,18 +546,22 @@
     packed_shape = (couples, 2 * size, size)
     packed_buf = pltpu.VMEM(packed_shape, BF16)
 
+    depth = spam_cores.shape[1]
+    half = depth // 2
+    first_sent = (slots, columns + EXTRA + half, size)
     outgoing, good = pl.pallas_call(
         functools.partial(first_kernel, slots_chunk, tiles_chunk, float(hosts / good_seeds.shape[1])),
-        out_shape=(sent, sds(panel, BF16)),
-        in_specs=[SMEM, SMEM, SMEM, VMEM, VMEM, ANY],
+        out_shape=(pltpu.HBM(first_sent, I16), sds(panel, BF16)),
+        in_specs=[SMEM, SMEM, SMEM, VMEM, VMEM, VMEM, ANY],
         out_specs=(HBM, VMEM),
-        scratch_shapes=[half_buf, tiles_buf, counts_buf, acc_buf, sent_buf, tile_sems, sems],
-        compiler_params=params(40),
+        scratch_shapes=[half_buf, tiles_buf, counts_buf, acc_buf, pltpu.VMEM(first_sent, I16), tile_sems, sems],
+        compiler_params=params(57),
         cost_estimate=cost(work, 2 * tile_bytes),
         name="first_push",
-    )(tile_src, tile_slot, slot_block, good_seeds, degree, held(tiles))
+    )(tile_src, tile_slot, slot_block, good_seeds, spam_cores.T, degree, held(tiles))
     arrived = exchange(outgoing)
     spam_seeds, src_after, slot_after, _ = lax.optimization_barrier((spam_cores, tile_src, tile_slot, outgoing))
+    spam_hosts = jnp.concatenate([spam_seeds[: columns // 2], spam_seeds[columns // 2 :]], axis=1)
     spam, weights = pl.pallas_call(
         functools.partial(side_kernel, float(hosts / spam_cores.shape[1])),
         out_shape=(sds(panel, BF16), sds((slots, EXTRA, size), I16)),
@@ -482,21 +573,7 @@
         name="side",
     )(spam_seeds, slot_after, held(tiles))
     pairs = pair_up(src_after, slot_after, blocks, slots)
-    outgoing, ids = pl.pallas_call(
-        functools.partial(second_kernel, slots_chunk, tiles_chunk),
-        out_shape=(sent, ids_shape),
-        in_specs=[SMEM, SMEM, VMEM, VMEM, VMEM, HBM, ANY],
-        out_specs=(HBM, VMEM),
-        scratch_shapes=[
-            sent_buf, tiles_buf, half_buf, total_buf, acc_buf, sent_buf, pltpu.SMEM(ids_shape.shape, I32),
-            sems, tile_sems, sems, sems,
-        ],
-        compiler_params=params(40),
-        cost_estimate=cost(work, 2 * tile_bytes),
-        name="second_push",
-    )(tile_src, tile_slot, degree, good, weights, held(arrived), held(tiles))
-    arrived = exchange(outgoing)
-    pairs_after, _ = lax.optimization_barrier((pairs, outgoing))
+    pair_tiles = lax.optimization_barrier((pairs, outgoing))[0]
     packed = pl.pallas_call(
         pack_kernel,
         out_shape=pltpu.HBM(packed_shape, BF16),
@@ -506,18 +583,54 @@
         compiler_params=params(40),
         cost_estimate=cost(work // 4, 2 * tile_bytes),
         name="pack",
-    )(pairs_after, held(tiles))
-    asked_for, trust, shield, in_weight = pl.pallas_call(
+    )(pair_tiles, held(tiles))
+    arrived, packed, weights = lax.optimization_barrier((arrived, packed, weights))
+    outgoing, ids = pl.pallas_call(
+        functools.partial(second_kernel, slots_chunk, tiles_chunk),
+        out_shape=(sent, ids_shape),
+        in_specs=[SMEM, SMEM, VMEM, VMEM, VMEM, HBM, ANY],
+        out_specs=(HBM, VMEM),
+        scratch_shapes=[
+            pltpu.VMEM(first_sent, I16), tiles_buf, half_buf, total_buf, acc_buf, sent_buf,
+            pltpu.SMEM(ids_shape.shape, I32), sems, tile_sems, sems, sems,
+        ],
+        compiler_params=params(40),
+        cost_estimate=cost(work, 2 * tile_bytes),
+        name="second_push",
+    )(tile_src, tile_slot, degree, good, weights, held(arrived), held(tiles))
+    first_arrived, _ = lax.optimization_barrier((arrived, outgoing))
+    arrived = exchange(outgoing)
+    core = (lax.axis_index("col") % 2).astype(I32)[None]
+    mine = first_arrived[:, columns + EXTRA :, :]
+    places = pl.pallas_call(
+        places_kernel,
+        out_shape=pltpu.HBM((slots, columns, size), I16),
+        in_specs=[SMEM, SMEM, ANY, ANY],
+        out_specs=HBM,
+        scratch_shapes=[
+            pltpu.VMEM((slots, depth, size), I16), pltpu.VMEM((slots, columns, size), I16),
+            pltpu.SemaphoreType.DMA((2,)), pltpu.SemaphoreType.DMA,
+        ],
+        compiler_params=params(40),
+        cost_estimate=cost(work, tile_bytes),
+        name="places",
+    )(core, slot_block, mine, swap(mine))
+    arrived, places = lax.optimization_barrier((arrived, places))
+    listed_shape = (slots, columns // 4, size)
+    outgoing, trust, shield, in_weight = pl.pallas_call(
         functools.partial(third_kernel, slots_chunk),
-        out_shape=(asked, sds(panel, F32), sds(panel, F32), sds((blocks, 1, size), F32)),
-        in_specs=[SMEM, VMEM, VMEM, HBM],
+        out_shape=(pltpu.HBM(listed_shape, BF16), sds(panel, F32), sds(panel, F32), sds((blocks, 1, size), F32)),
+        in_specs=[SMEM, VMEM, VMEM, VMEM, HBM],
         out_specs=(HBM, VMEM, VMEM, VMEM),
-        scratch_shapes=[sent_buf, total_buf, half_buf, asked_buf, sems, sems],
+        scratch_shapes=[
+            sent_buf, total_buf, pltpu.VMEM((columns // 2, size), BF16), pltpu.VMEM(listed_shape, BF16),
+            sems, pltpu.SemaphoreType.DMA,
+        ],
         compiler_params=params(40),
         cost_estimate=cost(work // 8, tile_bytes),
         name="first_shares",
-    )(ids, good, spam, held(arrived))
-    arrived = exchange(asked_for)
+    )(ids, good, spam, spam_hosts, held(arrived))
+    mine = exchange(outgoing)
     trust_out = pl.pallas_call(
         turn_kernel,
         out_shape=sds((blocks, size, columns), F32),
@@ -530,13 +643,16 @@
     asked_for = pl.pallas_call(
         functools.partial(fourth_kernel, slots_chunk),
         out_shape=asked,
-        in_specs=[SMEM, SMEM, VMEM, VMEM, VMEM, HBM, HBM],
+        in_specs=[SMEM, SMEM, SMEM, VMEM, VMEM, VMEM, ANY, ANY, HBM, HBM],
         out_specs=HBM,
-        scratch_shapes=[y_buf, packed_buf, total_buf, half_buf, asked_buf, sems, pair_sems, sems],
-        compiler_params=params(40),
+        scratch_shapes=[
+            pltpu.VMEM((slots, columns // 2, size), BF16), pltpu.VMEM((slots, columns, size), I16),
+            y_buf, packed_buf, total_buf, half_buf, asked_buf, pltpu.SemaphoreType.DMA((2,)), sems, pair_sems, sems,
+        ],
+        compiler_params=params(44),
         cost_estimate=cost(work, 2 * tile_bytes),
         name="second_shares",
-    )(ids, pairs, spam, shield, in_weight, held(arrived), held(packed))
+    )(core, ids, pairs, spam, shield, in_weight, mine, swap(mine), held(places), held(packed))
     arrived = exchange(asked_for)
     distrust = pl.pallas_call(
         functools.partial(fifth_kernel, slots_chunk),

time: 295 us -> 281 us (0.953)
  Pallas kernels: 74.1 us -> 115 us
  blocking collectives: 61.7 us -> 25 us
  waiting for transfers between devices: 130 us -> 110 us
  starting transfers between devices: 23.4 us -> 27.3 us
    all_to_all x1, blocking collectives: 61.7 us -> 25 us  [exchange(): return lax.all_to_all(x, AXES, split_axis=0, concat_axis=0, tiled=True)]
    pallas_call x1 -> x2, Pallas kernels: 5.67 us -> 39.2 us  [the longest x1 33.8 us: body(): pl.pallas_call(places_kernel, out_shape=pltpu.HBM((slots, columns, size),...]
    all_to_all x3, waiting for transfers between devices: 130 us -> 106 us  [exchange(): return lax.all_to_all(x, AXES, split_axis=0, concat_axis=0, tiled=True)]
    pallas_call x1, Pallas kernels: 9.2 us -> 14.7 us  [body(): pl.pallas_call(functools.partial(fourth_kernel, slots_chunk), out_shape=a...]
    ppermute x0 -> x2, waiting for transfers between devices: none -> 4.49 us  [swap(): return lax.ppermute(x, 'col', [(k, k ^ 1) for k in range(cores)])]
    unnamed x18 -> x12, local copies, waits for them, and re-layouts: 3.57 us -> 0.04 us
  transfers between devices with their start and end apart: 3 -> 5, of which waited for: 3 -> 5; matrix products, arithmetic and copies ran while one was open for 0% -> 1% of each run, Pallas kernels for 10% -> 23%
where the time goes in v4:
time: 281 us; the launch traced here: 280 us
  Pallas kernels  115 us (41%)
  waiting for transfers between devices  110 us (39%)
  starting transfers between devices  27.3 us (10%)
  blocking collectives  25 us (9%)
    all_to_all x3, waiting for transfers between devices, exchange(): return lax.all_to_all(x, AXES, split_axis=0, concat_axis=0, tiled=True)  106 us
    pallas_call x1, Pallas kernels, body(): pl.pallas_call(places_kernel, out_shape=pltpu.HBM((slots, columns, size),...  33.8 us
    all_to_all x1, blocking collectives, exchange(): return lax.all_to_all(x, AXES, split_axis=0, concat_axis=0, tiled=True)  25 us
    all_to_all x3, starting transfers between devices, exchange(): return lax.all_to_all(x, AXES, split_axis=0, concat_axis=0, tiled=True)  24.8 us
    pallas_call x1, Pallas kernels, body(): pl.pallas_call(pack_kernel, out_shape=pltpu.HBM(packed_shape, BF16), in_s...  17.4 us
    pallas_call x1, Pallas kernels, body(): pl.pallas_call(functools.partial(fourth_kernel, slots_chunk), out_shape=a...  14.7 us
    pallas_call x1, Pallas kernels, body(): pl.pallas_call(functools.partial(second_kernel, slots_chunk, tiles_chunk)...  11.7 us
    pallas_call x1, Pallas kernels, body(): pl.pallas_call(functools.partial(first_kernel, slots_chunk, tiles_chunk,...  10.7 us
  transfers between devices with their start and end apart: 5, of which 5 were waited for; matrix products, arithmetic and copies ran while one was open for 1% of the time, Pallas kernels for 23%

profile of v4, /device:TPU:1, one launch (start us, length us, event | category | flops | bytes accessed | tf_op | source)
XLA Modules:
  0.0 280.4 jit_solution(8439214613295428010)
XLA Ops:
  0.6 10.7 %first_push.1 = (s16[128,168,128]{2,1,0:T(8,128)(2,1)}, bf16[16,128,128]{2,1,0:T(8,128)(2,1)}) custom-call(s32[256]{0:T(256)} %src.3, s32[256]{0:T(256)} %slot.4, s32[128]{0:T(128)} %slot_block.3, s32[128,128]{1,0:T(8,128)} %seeds.1, s32[64,128]{1,0:T(8,128)} %bitcast.14, s32[16,1,128]{2,1,0:T(1,128)} %bitcast.10, bf16[256,128,128]{2,1,0:T(8,128)(2,1)} %tiles_hbm.7), custom_call_target="tpu_custom_call" | custom-call | flops 1073741824 | bytes 16777216 | tf_op jit(solution)/shard_map/first_push/pallas_call | solution.py:552
  11.3 0.0 copy-start.1
  11.3 0.0 copy-start.3
  11.3 0.0 copy-start.5
  11.4 11.9 %all-to-all-start = ((s16[128,168,128]{2,1,0:T(8,128)(2,1)}), s16[128,168,128]{2,1,0:T(8,128)(2,1)}, u32[]{:S(2)}, u32[]{:S(2)}) async-start(s16[128,168,128]{2,1,0:T(8,128)(2,1)} %get-tuple-element.23), calls=%async_computation | async-start | bytes 11010048 | tf_op jit(solution)/shard_map/all_to_all | solution.py:39
  23.3 0.1 convert_reduce_fusion.1
  23.4 0.1 select_reduce_fusion.6
  23.5 0.1 select_reduce_fusion.5
  23.6 0.2 convert_reduce_fusion
  23.8 0.3 select_reduce_fusion
  24.2 0.1 copy.12.seeds
  24.3 10.1 %side.1 = (bf16[16,128,128]{2,1,0:T(8,128)(2,1)S(1)}, s16[128,8,128]{2,1,0:T(8,128)(2,1)S(1)}) custom-call(s32[128,64]{1,0:T(8,128)S(1)} %copy.12.seeds, s32[256]{0:T(256)S(1)} %copy-done.3, bf16[256,128,128]{2,1,0:T(8,128)(2,1)} %tiles_hbm.7), custom_call_target="tpu_custom_call" | custom-call | flops 268435456 | bytes 8388608 | tf_op jit(solution)/shard_map/side/pallas_call | solution.py:565
  34.4 0.0 copy-start
  34.4 17.4 %pack.1.packed_hbm = bf16[136,256,128]{2,1,0:T(8,128)(2,1)} custom-call(s32[5,136]{1,0:T(8,128)S(1)} %stack.17.pairs, bf16[256,128,128]{2,1,0:T(8,128)(2,1)} %tiles_hbm.7), custom_call_target="tpu_custom_call" | custom-call | flops 268435456 | bytes 16777216 | tf_op jit(solution)/shard_map/pack/pallas_call | solution.py:577
  51.9 38.3 %all-to-all-done.arrived_hbm = s16[128,168,128]{2,1,0:T(8,128)(2,1)} async-done(((s16[128,168,128]{2,1,0:T(8,128)(2,1)}), s16[128,168,128]{2,1,0:T(8,128)(2,1)}, u32[]{:S(2)}, u32[]{:S(2)}) %all-to-all-start) | async-done | bytes 5505056 | tf_op jit(solution)/shard_map/all_to_all | solution.py:39
  90.2 11.7 %second_push.1 = (s16[128,136,128]{2,1,0:T(8,128)(2,1)}, s32[8,1,128]{2,1,0:T(1,128)S(1)}) custom-call(s32[256]{0:T(256)S(1)} %copy-done.1, s32[256]{0:T(256)S(1)} %copy-done.3, s32[16,1,128]{2,1,0:T(1,128)S(1)} %bitcast.11, bf16[16,128,128]{2,1,0:T(8,128)(2,1)S(1)} %copy-done, s16[128,8,128]{2,1,0:T(8,128)(2,1)S(1)} %get-tuple-element.29.weights, ...), custom_call_target="tpu_custom_call" | custom-call | flops 1073741824 | bytes 16777216 | tf_op jit(solution)/shard_map/second_push/pallas_call | solution.py:588
  101.9 7.9 %all-to-all-start.1 = ((s16[128,136,128]{2,1,0:T(8,128)(2,1)}), s16[128,136,128]{2,1,0:T(8,128)(2,1)}, u32[]{:S(2)}, u32[]{:S(2)}) async-start(s16[128,136,128]{2,1,0:T(8,128)(2,1)} %get-tuple-element.33), calls=%async_computation.1 | async-start | bytes 8912896 | tf_op jit(solution)/shard_map/all_to_all | solution.py:39
  109.8 1.3 slice.11.mine_hbm
  111.1 1.4 collective-permute-start
  112.5 0.1 pad_add_fusion.spam_hosts
  112.6 2.2 collective-permute-done.other_hbm
  114.8 33.8 %places.1.places_hbm = s16[128,128,128]{2,1,0:T(8,128)(2,1)} custom-call(s32[1]{0:T(128)} %bitcast.7.core, s32[128]{0:T(128)S(1)} %copy-done.4, s16[128,32,128]{2,1,0:T(8,128)(2,1)S(1)} %slice.11.mine_hbm, s16[128,32,128]{2,1,0:T(8,128)(2,1)S(1)} %collective-permute-done.other_hbm), custom_call_target="tpu_custom_call" | custom-call | flops 1073741824 | bytes 8388608 | tf_op jit(solution)/shard_map/places/pallas_call | solution.py:605
  148.6 16.9 %all-to-all-done.1.arrived_hbm = s16[128,136,128]{2,1,0:T(8,128)(2,1)} async-done(((s16[128,136,128]{2,1,0:T(8,128)(2,1)}), s16[128,136,128]{2,1,0:T(8,128)(2,1)}, u32[]{:S(2)}, u32[]{:S(2)}) %all-to-all-start.1) | async-done | bytes 4456480 | tf_op jit(solution)/shard_map/all_to_all | solution.py:39
  165.4 5.4 %first_shares.1 = (bf16[128,32,128]{2,1,0:T(8,128)(2,1)}, f32[16,128,128]{2,1,0:T(8,128)S(1)}, f32[16,128,128]{2,1,0:T(8,128)S(1)}, f32[16,1,128]{2,1,0:T(1,128)S(1)}) custom-call(s32[8,1,128]{2,1,0:T(1,128)S(1)} %get-tuple-element.31.ids, bf16[16,128,128]{2,1,0:T(8,128)(2,1)S(1)} %copy-done, bf16[16,128,128]{2,1,0:T(8,128)(2,1)S(1)} %get-tuple-element.32.spam, ...), custom_call_target="tpu_custom_call" | custom-call | flops 134217728 | bytes 8388608 | tf_op jit(solution)/shard_map/first_shares/pallas_call | solution.py:620
  170.9 25.0 %all_to_all.20.mine_hbm = bf16[128,32,128]{2,1,0:T(8,128)(2,1)S(1)} all-to-all(bf16[128,32,128]{2,1,0:T(8,128)(2,1)} %get-tuple-element.39), channel_id=1, replica_groups=mesh['row'=16,'col'=8] {'row','col'}, dimensions={0} | all-to-all | bytes 2097152 | tf_op jit(solution)/shard_map/all_to_all | solution.py:39
  195.9 1.2 collective-permute-start.1
  197.0 2.3 collective-permute-done.1.other_hbm
  199.3 14.7 %second_shares.1 = bf16[128,128,128]{2,1,0:T(8,128)(2,1)} custom-call(s32[1]{0:T(128)} %bitcast.7.core, s32[8,1,128]{2,1,0:T(1,128)S(1)} %get-tuple-element.31.ids, s32[5,136]{1,0:T(8,128)S(1)} %stack.17.pairs, bf16[16,128,128]{2,1,0:T(8,128)(2,1)S(1)} %get-tuple-element.32.spam, f32[16,128,128]{2,1,0:T(8,128)S(1)} %get-tuple-element.37.shield, ...), custom_call_target="tpu_custom_call" | custom-call | flops 1073741824 | bytes 16777216 | tf_op jit(solution)/shard_map/second_shares/pallas_call | solution.py:643
  214.0 4.9 %all-to-all-start.3 = ((bf16[128,128,128]{2,1,0:T(8,128)(2,1)}), bf16[128,128,128]{2,1,0:T(8,128)(2,1)}, u32[]{:S(2)}, u32[]{:S(2)}) async-start(bf16[128,128,128]{2,1,0:T(8,128)(2,1)} %second_shares.1), calls=%async_computation.3 | async-start | bytes 8388608 | tf_op jit(solution)/shard_map/all_to_all | solution.py:39
  218.9 2.6 turn.1
  221.5 50.3 %all-to-all-done.3.arrived_hbm = bf16[128,128,128]{2,1,0:T(8,128)(2,1)} async-done(((bf16[128,128,128]{2,1,0:T(8,128)(2,1)}), bf16[128,128,128]{2,1,0:T(8,128)(2,1)}, u32[]{:S(2)}, u32[]{:S(2)}) %all-to-all-start.3) | async-done | bytes 4194336 | tf_op jit(solution)/shard_map/all_to_all | solution.py:39
  271.9 8.4 %last_pull.1 = f32[16,128,128]{2,1,0:T(8,128)} custom-call(s32[5,136]{1,0:T(8,128)S(1)} %stack.17.pairs, bf16[16,128,128]{2,1,0:T(8,128)(2,1)S(1)} %get-tuple-element.32.spam, bf16[128,128,128]{2,1,0:T(8,128)(2,1)} %all-to-all-done.3.arrived_hbm, bf16[136,256,128]{2,1,0:T(8,128)(2,1)} %pack.1.packed_hbm), custom_call_target="tpu_custom_call" | custom-call | flops 1073741824 | bytes 16777216 | tf_op jit(solution)/shard_map/last_pull/pallas_call | solution.py:657
  (16 shorter events, 0.1 us)
Async XLA Ops:
  11.3 11.9 %copy-start.1 = (s32[256]{0:T(256)S(1)}, s32[256]{0:T(256)}, u32[]{:S(2)}) copy-start(s32[256]{0:T(256)} %src.3) | copy-start | bytes 3076
  11.3 12.5 %copy-start.3 = (s32[256]{0:T(256)S(1)}, s32[256]{0:T(256)}, u32[]{:S(2)}) copy-start(s32[256]{0:T(256)} %slot.4) | copy-start | bytes 3076
  11.3 12.8 %copy-start.5 = (s32[128,64]{0,1:T(8,128)S(1)}, s32[128,64]{0,1:T(8,128)}, u32[]{:S(2)}) copy-start(s32[128,64]{0,1:T(8,128)} %param.13) | copy-start | bytes 98308
  11.4 78.8 %all-to-all-start = ((s16[128,168,128]{2,1,0:T(8,128)(2,1)}), s16[128,168,128]{2,1,0:T(8,128)(2,1)}, u32[]{:S(2)}, u32[]{:S(2)}) async-start(s16[128,168,128]{2,1,0:T(8,128)(2,1)} %get-tuple-element.23), calls=%async_computation | async-start | bytes 11010048 | tf_op jit(solution)/shard_map/all_to_all | solution.py:39
  34.4 55.8 %copy-start = (bf16[16,128,128]{2,1,0:T(8,128)(2,1)S(1)}, bf16[16,128,128]{2,1,0:T(8,128)(2,1)}, u32[]{:S(2)}) copy-start(bf16[16,128,128]{2,1,0:T(8,128)(2,1)} %get-tuple-element.22.good) | copy-start | bytes 1572868
  34.4 55.8 %copy-start.2 = (s32[2048]{0:T(1024)S(1)}, s32[2048]{0:T(1024)}, u32[]{:S(2)}) copy-start(s32[2048]{0:T(1024)} %param.11) | copy-start | bytes 24580
  101.9 12.9 %copy-start.4 = (s32[128]{0:T(128)S(1)}, s32[128]{0:T(128)}, u32[]{:S(2)}) copy-start(s32[128]{0:T(128)} %slot_block.3) | copy-start | bytes 1540
  101.9 63.5 %all-to-all-start.1 = ((s16[128,136,128]{2,1,0:T(8,128)(2,1)}), s16[128,136,128]{2,1,0:T(8,128)(2,1)}, u32[]{:S(2)}, u32[]{:S(2)}) async-start(s16[128,136,128]{2,1,0:T(8,128)(2,1)} %get-tuple-element.33), calls=%async_computation.1 | async-start | bytes 8912896 | tf_op jit(solution)/shard_map/all_to_all | solution.py:39
  111.1 3.7 %collective-permute-start = (s16[128,32,128]{2,1,0:T(8,128)(2,1)S(1)}, s16[128,32,128]{2,1,0:T(8,128)(2,1)S(1)}, u32[]{:S(2)}, u32[]{:S(2)}) collective-permute-start(s16[128,32,128]{2,1,0:T(8,128)(2,1)S(1)} %slice.11.mine_hbm), channel_id=1, source_target_pairs={{0,1},{1,0},{2,3},{3,2},{4,5},{5,4},{6,7},{7,6},{8,9},{9,8},{10,11... | collective-permute-start | bytes 3145736 | tf_op jit(solution)/shard_map/ppermute | solution.py:35
  195.9 3.5 %collective-permute-start.1 = (bf16[128,32,128]{2,1,0:T(8,128)(2,1)S(1)}, bf16[128,32,128]{2,1,0:T(8,128)(2,1)S(1)}, u32[]{:S(2)}, u32[]{:S(2)}) collective-permute-start(bf16[128,32,128]{2,1,0:T(8,128)(2,1)S(1)} %all_to_all.20.mine_hbm), channel_id=1, source_target_pairs={{0,1},{1,0},{2,3},{3,2},{4,5},{5,4},{6,7},{7,6},{8,9},{9,8},{10,11... | collective-permute-start | bytes 3145736 | tf_op jit(solution)/shard_map/ppermute | solution.py:35
  214.0 57.9 %all-to-all-start.3 = ((bf16[128,128,128]{2,1,0:T(8,128)(2,1)}), bf16[128,128,128]{2,1,0:T(8,128)(2,1)}, u32[]{:S(2)}, u32[]{:S(2)}) async-start(bf16[128,128,128]{2,1,0:T(8,128)(2,1)} %second_shares.1), calls=%async_computation.3 | async-start | bytes 8388608 | tf_op jit(solution)/shard_map/all_to_all | solution.py:39

commit v5 on v4

--- a/solution.py
+++ b/solution.py
@@ -48,6 +48,14 @@
     ]
 
 
+def clear_all(acc):
+    def clear(g, _):
+        acc[g] = jnp.zeros(acc.shape[1:], F32)
+        return 0
+
+    lax.fori_loop(0, acc.shape[0], clear, 0, unroll=4)
+
+
 def run_chunks(copies, group):
     def step(c, _):
         for k, copy in enumerate(copies):
@@ -62,13 +70,19 @@
     lax.fori_loop(0, len(copies), step, 0)
 
 
-def histogram(seeds_ref, out_ref, factor):
+def histogram(seeds_ref, out_ref, factor, to_clear=None):
     columns, depth = seeds_ref.shape
     blocks = out_ref.shape[0] // columns
-    unroll = 8
+    unroll = 16
     none = jnp.zeros((blocks, depth), BF16)
 
+    steps = columns // (2 * unroll)
+
     def group(g, _):
+        if to_clear is not None:
+            part = to_clear.shape[0] // steps
+            for u in range(part):
+                to_clear[g * part + u] = jnp.zeros(to_clear.shape[1:], F32)
         for u in range(unroll):
             s = (g * unroll + u) * 2
             highs, lows = [], []
@@ -86,7 +100,7 @@
                 out_ref[pl.ds(s + one, blocks, stride=columns), :] = count[one * blocks : (one + 1) * blocks] * factor
         return 0
 
-    lax.fori_loop(0, columns // (2 * unroll), group, 0)
+    lax.fori_loop(0, steps, group, 0)
 
 
 def encode_scale(largest):
@@ -106,11 +120,6 @@
 
 
 def push(x_ref, tiles, copies, src, slot, acc):
-    def clear(g, _):
-        acc[g] = jnp.zeros(acc.shape[1:], F32)
-        return 0
-
-    lax.fori_loop(0, acc.shape[0], clear, 0, unroll=4)
     unroll = tiles.shape[0] // len(copies)
 
     def group(g):
@@ -187,7 +196,7 @@
     copies = fetch(tiles_hbm, tiles, tile_sems, tiles_chunk)
     for copy in copies:
         copy.start()
-    histogram(seeds, counts, factor)
+    histogram(seeds, counts, factor, acc)
     blocks, columns = x.shape[0], x.shape[1]
 
     def scale(b, _):
@@ -208,8 +217,11 @@
                   arrived, tiles, x, total, acc, staged, ids, in_sems, tile_sems, id_sems, out_sems):
     incoming = fetch(arrived_hbm, arrived, in_sems, slots_chunk)
     copies = fetch(tiles_hbm, tiles, tile_sems, tiles_chunk)
-    for copy in incoming + copies:
-        copy.start()
+    for copy in incoming:
+        copy.start(priority=0)
+    for copy in copies:
+        copy.start(priority=1)
+    clear_all(acc)
     lane = lax.broadcasted_iota(I32, (1, BS), 1)
     moves = []
 
@@ -361,10 +373,12 @@
     back.wait()
 
 
+def before_pull(y, total):
+    y[y.shape[0] - 1] = jnp.zeros(y.shape[1:], BF16)
+    clear_all(total)
+
+
 def pull(pairs, y, packed, copies, total):
-    y[y.shape[0] - 1] = jnp.zeros(y.shape[1:], BF16)
-    for b in range(total.shape[0]):
-        total[b] = jnp.zeros(total.shape[1:], F32)
     unroll = packed.shape[0] // len(copies)
 
     def group(g):
@@ -389,9 +403,10 @@
         copy.start(priority=0)
     for copy in copies:
         copy.start(priority=1)
+    before_pull(y, total)
     for copy in halves:
         copy.wait()
-    unroll = min(8, slots_chunk)
+    unroll = min(16, slots_chunk)
     rows = values.shape[1]
 
     def expand(c):
@@ -426,6 +441,7 @@
         copy.start(priority=0)
     for copy in copies:
         copy.start(priority=1)
+    before_pull(y, total)
     for copy in incoming:
         copy.wait()
     pull(pairs, y, packed, copies, total)

time: 281 us -> 278 us (0.989)
  Pallas kernels: 115 us -> 112 us
where the time goes in v5:
time: 278 us
  Pallas kernels  112 us (40%)
  waiting for transfers between devices  110 us (40%)
  starting transfers between devices  27.3 us (10%)
  blocking collectives  25 us (9%)
    all_to_all x3, waiting for transfers between devices, exchange(): return lax.all_to_all(x, AXES, split_axis=0, concat_axis=0, tiled=True)  106 us
    pallas_call x1, Pallas kernels, body(): pl.pallas_call(places_kernel, out_shape=pltpu.HBM((slots, columns, size),...  33.8 us
    all_to_all x1, blocking collectives, exchange(): return lax.all_to_all(x, AXES, split_axis=0, concat_axis=0, tiled=True)  25 us
    all_to_all x3, starting transfers between devices, exchange(): return lax.all_to_all(x, AXES, split_axis=0, concat_axis=0, tiled=True)  24.8 us
    pallas_call x1, Pallas kernels, body(): pl.pallas_call(pack_kernel, out_shape=pltpu.HBM(packed_shape, BF16), in_s...  17.4 us
    pallas_call x1, Pallas kernels, body(): pl.pallas_call(functools.partial(fourth_kernel, slots_chunk), out_shape=a...  14 us
    pallas_call x1, Pallas kernels, body(): pl.pallas_call(functools.partial(second_kernel, slots_chunk, tiles_chunk)...  10.2 us
    pallas_call x1, Pallas kernels, body(): pl.pallas_call(functools.partial(first_kernel, slots_chunk, tiles_chunk,...  10.2 us
  transfers between devices with their start and end apart: 5, of which 5 were waited for; matrix products, arithmetic and copies ran while one was open for 1% of the time, Pallas kernels for 23%

profile of v5, /device:TPU:1, one launch (start us, length us, event | category | flops | bytes accessed | tf_op | source)
XLA Modules:
  0.0 277.9 jit_solution(4217022699517695925)
XLA Ops:
  0.6 10.2 %first_push.1 = (s16[128,168,128]{2,1,0:T(8,128)(2,1)}, bf16[16,128,128]{2,1,0:T(8,128)(2,1)}) custom-call(s32[256]{0:T(256)} %src.3, s32[256]{0:T(256)} %slot.4, s32[128]{0:T(128)} %slot_block.3, s32[128,128]{1,0:T(8,128)} %seeds.1, s32[64,128]{1,0:T(8,128)} %bitcast.14, s32[16,1,128]{2,1,0:T(1,128)} %bitcast.10, bf16[256,128,128]{2,1,0:T(8,128)(2,1)} %tiles_hbm.7), custom_call_target="tpu_custom_call" | custom-call | flops 1073741824 | bytes 16777216 | tf_op jit(solution)/shard_map/first_push/pallas_call | solution.py:568
  10.9 0.0 copy-start.3
  10.9 0.0 copy-start.5
  10.9 11.9 %all-to-all-start = ((s16[128,168,128]{2,1,0:T(8,128)(2,1)}), s16[128,168,128]{2,1,0:T(8,128)(2,1)}, u32[]{:S(2)}, u32[]{:S(2)}) async-start(s16[128,168,128]{2,1,0:T(8,128)(2,1)} %get-tuple-element.23), calls=%async_computation | async-start | bytes 11010048 | tf_op jit(solution)/shard_map/all_to_all | solution.py:39
  22.8 0.1 convert_reduce_fusion.1
  22.9 0.1 select_reduce_fusion.6
  23.0 0.1 select_reduce_fusion.5
  23.1 0.2 convert_reduce_fusion
  23.4 0.3 select_reduce_fusion
  23.7 0.1 copy.12.seeds
  23.8 10.1 %side.1 = (bf16[16,128,128]{2,1,0:T(8,128)(2,1)S(1)}, s16[128,8,128]{2,1,0:T(8,128)(2,1)S(1)}) custom-call(s32[128,64]{1,0:T(8,128)S(1)} %copy.12.seeds, s32[256]{0:T(256)S(1)} %copy-done.3, bf16[256,128,128]{2,1,0:T(8,128)(2,1)} %tiles_hbm.7), custom_call_target="tpu_custom_call" | custom-call | flops 268435456 | bytes 8388608 | tf_op jit(solution)/shard_map/side/pallas_call | solution.py:581
  33.9 0.0 copy-start.2
  34.0 17.4 %pack.1.packed_hbm = bf16[136,256,128]{2,1,0:T(8,128)(2,1)} custom-call(s32[5,136]{1,0:T(8,128)S(1)} %stack.17.pairs, bf16[256,128,128]{2,1,0:T(8,128)(2,1)} %tiles_hbm.7), custom_call_target="tpu_custom_call" | custom-call | flops 268435456 | bytes 16777216 | tf_op jit(solution)/shard_map/pack/pallas_call | solution.py:593
  51.4 38.3 %all-to-all-done.arrived_hbm = s16[128,168,128]{2,1,0:T(8,128)(2,1)} async-done(((s16[128,168,128]{2,1,0:T(8,128)(2,1)}), s16[128,168,128]{2,1,0:T(8,128)(2,1)}, u32[]{:S(2)}, u32[]{:S(2)}) %all-to-all-start) | async-done | bytes 5505056 | tf_op jit(solution)/shard_map/all_to_all | solution.py:39
  89.7 10.2 %second_push.1 = (s16[128,136,128]{2,1,0:T(8,128)(2,1)}, s32[8,1,128]{2,1,0:T(1,128)S(1)}) custom-call(s32[256]{0:T(256)S(1)} %copy-done.1, s32[256]{0:T(256)S(1)} %copy-done.3, s32[16,1,128]{2,1,0:T(1,128)S(1)} %bitcast.11, bf16[16,128,128]{2,1,0:T(8,128)(2,1)S(1)} %copy-done, s16[128,8,128]{2,1,0:T(8,128)(2,1)S(1)} %get-tuple-element.29.weights, ...), custom_call_target="tpu_custom_call" | custom-call | flops 1073741824 | bytes 16777216 | tf_op jit(solution)/shard_map/second_push/pallas_call | solution.py:604
  100.0 0.0 copy-start.4
  100.0 7.9 %all-to-all-start.1 = ((s16[128,136,128]{2,1,0:T(8,128)(2,1)}), s16[128,136,128]{2,1,0:T(8,128)(2,1)}, u32[]{:S(2)}, u32[]{:S(2)}) async-start(s16[128,136,128]{2,1,0:T(8,128)(2,1)} %get-tuple-element.33), calls=%async_computation.1 | async-start | bytes 8912896 | tf_op jit(solution)/shard_map/all_to_all | solution.py:39
  107.9 1.3 slice.11.mine_hbm
  109.2 1.4 collective-permute-start
  110.6 0.1 pad_add_fusion.spam_hosts
  110.7 2.2 collective-permute-done.other_hbm
  112.9 33.8 %places.1.places_hbm = s16[128,128,128]{2,1,0:T(8,128)(2,1)} custom-call(s32[1]{0:T(128)} %bitcast.7.core, s32[128]{0:T(128)S(1)} %copy-done.4, s16[128,32,128]{2,1,0:T(8,128)(2,1)S(1)} %slice.11.mine_hbm, s16[128,32,128]{2,1,0:T(8,128)(2,1)S(1)} %collective-permute-done.other_hbm), custom_call_target="tpu_custom_call" | custom-call | flops 1073741824 | bytes 8388608 | tf_op jit(solution)/shard_map/places/pallas_call | solution.py:621
  146.7 16.9 %all-to-all-done.1.arrived_hbm = s16[128,136,128]{2,1,0:T(8,128)(2,1)} async-done(((s16[128,136,128]{2,1,0:T(8,128)(2,1)}), s16[128,136,128]{2,1,0:T(8,128)(2,1)}, u32[]{:S(2)}, u32[]{:S(2)}) %all-to-all-start.1) | async-done | bytes 4456480 | tf_op jit(solution)/shard_map/all_to_all | solution.py:39
  163.5 5.4 %first_shares.1 = (bf16[128,32,128]{2,1,0:T(8,128)(2,1)}, f32[16,128,128]{2,1,0:T(8,128)S(1)}, f32[16,128,128]{2,1,0:T(8,128)S(1)}, f32[16,1,128]{2,1,0:T(1,128)S(1)}) custom-call(s32[8,1,128]{2,1,0:T(1,128)S(1)} %get-tuple-element.31.ids, bf16[16,128,128]{2,1,0:T(8,128)(2,1)S(1)} %copy-done, bf16[16,128,128]{2,1,0:T(8,128)(2,1)S(1)} %get-tuple-element.32.spam, ...), custom_call_target="tpu_custom_call" | custom-call | flops 134217728 | bytes 8388608 | tf_op jit(solution)/shard_map/first_shares/pallas_call | solution.py:636
  169.0 25.0 %all_to_all.20.mine_hbm = bf16[128,32,128]{2,1,0:T(8,128)(2,1)S(1)} all-to-all(bf16[128,32,128]{2,1,0:T(8,128)(2,1)} %get-tuple-element.39), channel_id=1, replica_groups=mesh['row'=16,'col'=8] {'row','col'}, dimensions={0} | all-to-all | bytes 2097152 | tf_op jit(solution)/shard_map/all_to_all | solution.py:39
  194.0 1.2 collective-permute-start.1
  195.1 2.3 collective-permute-done.1.other_hbm
  197.4 14.0 %second_shares.1 = bf16[128,128,128]{2,1,0:T(8,128)(2,1)} custom-call(s32[1]{0:T(128)} %bitcast.7.core, s32[8,1,128]{2,1,0:T(1,128)S(1)} %get-tuple-element.31.ids, s32[5,136]{1,0:T(8,128)S(1)} %stack.17.pairs, bf16[16,128,128]{2,1,0:T(8,128)(2,1)S(1)} %get-tuple-element.32.spam, f32[16,128,128]{2,1,0:T(8,128)S(1)} %get-tuple-element.37.shield, ...), custom_call_target="tpu_custom_call" | custom-call | flops 1073741824 | bytes 16777216 | tf_op jit(solution)/shard_map/second_shares/pallas_call | solution.py:659
  211.5 4.9 %all-to-all-start.3 = ((bf16[128,128,128]{2,1,0:T(8,128)(2,1)}), bf16[128,128,128]{2,1,0:T(8,128)(2,1)}, u32[]{:S(2)}, u32[]{:S(2)}) async-start(bf16[128,128,128]{2,1,0:T(8,128)(2,1)} %second_shares.1), calls=%async_computation.3 | async-start | bytes 8388608 | tf_op jit(solution)/shard_map/all_to_all | solution.py:39
  216.4 2.6 turn.1
  219.0 50.3 %all-to-all-done.3.arrived_hbm = bf16[128,128,128]{2,1,0:T(8,128)(2,1)} async-done(((bf16[128,128,128]{2,1,0:T(8,128)(2,1)}), bf16[128,128,128]{2,1,0:T(8,128)(2,1)}, u32[]{:S(2)}, u32[]{:S(2)}) %all-to-all-start.3) | async-done | bytes 4194336 | tf_op jit(solution)/shard_map/all_to_all | solution.py:39
  269.3 8.4 %last_pull.1 = f32[16,128,128]{2,1,0:T(8,128)} custom-call(s32[5,136]{1,0:T(8,128)S(1)} %stack.17.pairs, bf16[16,128,128]{2,1,0:T(8,128)(2,1)S(1)} %get-tuple-element.32.spam, bf16[128,128,128]{2,1,0:T(8,128)(2,1)} %all-to-all-done.3.arrived_hbm, bf16[136,256,128]{2,1,0:T(8,128)(2,1)} %pack.1.packed_hbm), custom_call_target="tpu_custom_call" | custom-call | flops 1073741824 | bytes 16777216 | tf_op jit(solution)/shard_map/last_pull/pallas_call | solution.py:673
  (16 shorter events, 0.1 us)
Async XLA Ops:
  10.9 11.9 %copy-start.1 = (s32[256]{0:T(256)S(1)}, s32[256]{0:T(256)}, u32[]{:S(2)}) copy-start(s32[256]{0:T(256)} %src.3) | copy-start | bytes 3076
  10.9 12.5 %copy-start.3 = (s32[256]{0:T(256)S(1)}, s32[256]{0:T(256)}, u32[]{:S(2)}) copy-start(s32[256]{0:T(256)} %slot.4) | copy-start | bytes 3076
  10.9 12.8 %copy-start.5 = (s32[128,64]{0,1:T(8,128)S(1)}, s32[128,64]{0,1:T(8,128)}, u32[]{:S(2)}) copy-start(s32[128,64]{0,1:T(8,128)} %param.13) | copy-start | bytes 98308
  10.9 78.8 %all-to-all-start = ((s16[128,168,128]{2,1,0:T(8,128)(2,1)}), s16[128,168,128]{2,1,0:T(8,128)(2,1)}, u32[]{:S(2)}, u32[]{:S(2)}) async-start(s16[128,168,128]{2,1,0:T(8,128)(2,1)} %get-tuple-element.23), calls=%async_computation | async-start | bytes 11010048 | tf_op jit(solution)/shard_map/all_to_all | solution.py:39
  33.9 55.8 %copy-start = (bf16[16,128,128]{2,1,0:T(8,128)(2,1)S(1)}, bf16[16,128,128]{2,1,0:T(8,128)(2,1)}, u32[]{:S(2)}) copy-start(bf16[16,128,128]{2,1,0:T(8,128)(2,1)} %get-tuple-element.22.good) | copy-start | bytes 1572868
  33.9 55.8 %copy-start.2 = (s32[2048]{0:T(1024)S(1)}, s32[2048]{0:T(1024)}, u32[]{:S(2)}) copy-start(s32[2048]{0:T(1024)} %param.11) | copy-start | bytes 24580
  100.0 13.0 %copy-start.4 = (s32[128]{0:T(128)S(1)}, s32[128]{0:T(128)}, u32[]{:S(2)}) copy-start(s32[128]{0:T(128)} %slot_block.3) | copy-start | bytes 1540
  100.0 63.6 %all-to-all-start.1 = ((s16[128,136,128]{2,1,0:T(8,128)(2,1)}), s16[128,136,128]{2,1,0:T(8,128)(2,1)}, u32[]{:S(2)}, u32[]{:S(2)}) async-start(s16[128,136,128]{2,1,0:T(8,128)(2,1)} %get-tuple-element.33), calls=%async_computation.1 | async-start | bytes 8912896 | tf_op jit(solution)/shard_map/all_to_all | solution.py:39
  109.2 3.7 %collective-permute-start = (s16[128,32,128]{2,1,0:T(8,128)(2,1)S(1)}, s16[128,32,128]{2,1,0:T(8,128)(2,1)S(1)}, u32[]{:S(2)}, u32[]{:S(2)}) collective-permute-start(s16[128,32,128]{2,1,0:T(8,128)(2,1)S(1)} %slice.11.mine_hbm), channel_id=1, source_target_pairs={{0,1},{1,0},{2,3},{3,2},{4,5},{5,4},{6,7},{7,6},{8,9},{9,8},{10,11... | collective-permute-start | bytes 3145736 | tf_op jit(solution)/shard_map/ppermute | solution.py:35
  194.0 3.5 %collective-permute-start.1 = (bf16[128,32,128]{2,1,0:T(8,128)(2,1)S(1)}, bf16[128,32,128]{2,1,0:T(8,128)(2,1)S(1)}, u32[]{:S(2)}, u32[]{:S(2)}) collective-permute-start(bf16[128,32,128]{2,1,0:T(8,128)(2,1)S(1)} %all_to_all.20.mine_hbm), channel_id=1, source_target_pairs={{0,1},{1,0},{2,3},{3,2},{4,5},{5,4},{6,7},{7,6},{8,9},{9,8},{10,11... | collective-permute-start | bytes 3145736 | tf_op jit(solution)/shard_map/ppermute | solution.py:35
  211.5 57.9 %all-to-all-start.3 = ((bf16[128,128,128]{2,1,0:T(8,128)(2,1)}), bf16[128,128,128]{2,1,0:T(8,128)(2,1)}, u32[]{:S(2)}, u32[]{:S(2)}) async-start(bf16[128,128,128]{2,1,0:T(8,128)(2,1)} %second_shares.1), calls=%async_computation.3 | async-start | bytes 8388608 | tf_op jit(solution)/shard_map/all_to_all | solution.py:39

commit v6 on v5

--- a/solution.py
+++ b/solution.py
@@ -394,35 +394,85 @@
     run_chunks(copies, group)
 
 
-def fourth_kernel(slots_chunk, core, ids, pairs, spam, shield, in_weight, mine_hbm, other_hbm, places_hbm, packed_hbm,
-                  out_hbm, values, places, y, packed, total, share, staged, half_sems, in_sems, pair_sems, out_sems):
-    halves = two_halves(core, mine_hbm, other_hbm, values, half_sems, values.shape[1] // 2)
-    incoming = fetch(places_hbm, places, in_sems, slots_chunk)
-    copies = fetch(packed_hbm, packed, pair_sems, packed.shape[0] // pair_sems.shape[0])
-    for copy in halves + incoming:
-        copy.start(priority=0)
-    for copy in copies:
-        copy.start(priority=1)
-    before_pull(y, total)
-    for copy in halves:
-        copy.wait()
-    unroll = min(16, slots_chunk)
+def place_copies(at_core, places_hbm, places, sems):
+    rows = places.shape[1] // 2
+    half = places_hbm.shape[1] // 2
+    chunks = sems.shape[0]
+    size = places.shape[0] // chunks
+    first = pl.multiple_of(at_core * rows, rows)
+    return [
+        [
+            pltpu.make_async_copy(
+                places_hbm.at[pl.ds(c * size, size), pl.ds(h * half + first, rows)],
+                places.at[pl.ds(c * size, size), h * rows : (h + 1) * rows],
+                sems.at[c, h],
+            )
+            for h in range(2)
+        ]
+        for c in range(chunks)
+    ]
+
+
+def expand(values, places, copies, store):
     rows = values.shape[1]
-
-    def expand(c):
+    size = values.shape[0] // len(copies)
+    unroll = min(16, size)
+    for c, pair in enumerate(copies):
+        for copy in pair:
+            copy.wait()
+
         def group(g, _):
             for u in range(unroll):
-                q = c * slots_chunk + g * unroll + u
+                q = c * size + g * unroll + u
                 value = values[q].astype(F32)
                 for h in range(2):
                     place = places[q, h * rows : (h + 1) * rows, :].astype(I32)
                     found = jnp.take_along_axis(value, jnp.maximum(place, 0), axis=1, mode="promise_in_bounds")
-                    y[q, h * rows : (h + 1) * rows, :] = jnp.where(place >= 0, found, 0.0).astype(BF16)
+                    store(q, h, jnp.where(place >= 0, found, 0.0).astype(BF16))
             return 0
 
-        lax.fori_loop(0, slots_chunk // unroll, group, 0)
-
-    run_chunks(incoming, expand)
+        lax.fori_loop(0, size // unroll, group, 0)
+
+
+def own_kernel(core, mine_hbm, places_hbm, part, values, places, sem, place_sems):
+    value_copy = pltpu.make_async_copy(mine_hbm, values, sem)
+    value_copy.start()
+    copies = place_copies(core[0], places_hbm, places, place_sems)
+    for pair in copies:
+        for copy in pair:
+            copy.start()
+    value_copy.wait()
+    rows = values.shape[1]
+
+    def store(q, h, found):
+        part[q, h * rows : (h + 1) * rows, :] = found
+
+    expand(values, places, copies, store)
+
+
+def fourth_kernel(slots_chunk, core, ids, pairs, spam, shield, in_weight, part, other_hbm, places_hbm, packed_hbm,
+                  out_hbm, values, places, y, packed, total, share, staged, sem, place_sems, pair_sems, out_sems):
+    value_copy = pltpu.make_async_copy(other_hbm, values, sem)
+    value_copy.start(priority=0)
+    places_in = place_copies(1 - core[0], places_hbm, places, place_sems)
+    for pair in places_in:
+        for copy in pair:
+            copy.start(priority=0)
+    copies = fetch(packed_hbm, packed, pair_sems, packed.shape[0] // pair_sems.shape[0])
+    for copy in copies:
+        copy.start(priority=1)
+    before_pull(y, total)
+    rows = values.shape[1]
+    half = y.shape[1] // 2
+    here = pl.multiple_of(core[0] * rows, rows)
+    there = pl.multiple_of((1 - core[0]) * rows, rows)
+    value_copy.wait()
+
+    def store(q, h, found):
+        y[q, pl.ds(h * half + there, rows), :] = found
+        y[q, pl.ds(h * half + here, rows), :] = part[q, h * rows : (h + 1) * rows, :]
+
+    expand(values, places, places_in, store)
     pull(pairs, y, packed, copies, total)
 
     def finish(b, _):
@@ -434,7 +484,7 @@
     requests(share, ids, staged, out_hbm, out_sems, slots_chunk)
 
 
-def fifth_kernel(slots_chunk, pairs, spam, arrived_hbm, packed_hbm, distrust, y, packed, total, in_sems, pair_sems):
+def fifth_kernel(slots_chunk, pairs, spam, arrived_hbm, packed_hbm, out_hbm, y, packed, total, distrust, in_sems, pair_sems, out_sems):
     incoming = fetch(arrived_hbm, y, in_sems, slots_chunk)
     copies = fetch(packed_hbm, packed, pair_sems, packed.shape[0] // pair_sems.shape[0])
     for copy in incoming:
@@ -450,7 +500,13 @@
         distrust[b] = jnp.transpose(0.85 * total[b] + 0.15 * spam[b].astype(F32))
         return 0
 
-    lax.fori_loop(0, total.shape[0], finish, 0, unroll=4)
+    part = total.shape[0] // out_sems.shape[0]
+    back = fetch(distrust, out_hbm, out_sems, part)
+    for n, copy in enumerate(back):
+        lax.fori_loop(n * part, (n + 1) * part, finish, 0, unroll=4)
+        copy.start()
+    for copy in back:
+        copy.wait()
 
 
 def turn_kernel(wide, tall):
@@ -656,26 +712,42 @@
         cost_estimate=cost(work // 64, tile_bytes // 4),
         name="turn",
     )(trust)
+    quarter_buf = pltpu.VMEM(listed_shape, BF16)
+    places_buf = pltpu.VMEM((slots, columns // 2, size), I16)
+    place_sems = pltpu.SemaphoreType.DMA((min(4, chunks), 2))
+    part = pl.pallas_call(
+        own_kernel,
+        out_shape=sds((slots, columns // 2, size), BF16),
+        in_specs=[SMEM, ANY, HBM],
+        out_specs=VMEM,
+        scratch_shapes=[quarter_buf, places_buf, pltpu.SemaphoreType.DMA, place_sems],
+        compiler_params=params(24),
+        cost_estimate=cost(work // 4, tile_bytes // 2),
+        name="own_values",
+    )(core, mine, held(places))
     asked_for = pl.pallas_call(
         functools.partial(fourth_kernel, slots_chunk),
         out_shape=asked,
-        in_specs=[SMEM, SMEM, SMEM, VMEM, VMEM, VMEM, ANY, ANY, HBM, HBM],
+        in_specs=[SMEM, SMEM, SMEM, VMEM, VMEM, VMEM, VMEM, ANY, HBM, HBM],
         out_specs=HBM,
         scratch_shapes=[
-            pltpu.VMEM((slots, columns // 2, size), BF16), pltpu.VMEM((slots, columns, size), I16),
-            y_buf, packed_buf, total_buf, half_buf, asked_buf, pltpu.SemaphoreType.DMA((2,)), sems, pair_sems, sems,
+            quarter_buf, places_buf, y_buf, packed_buf, total_buf, half_buf, asked_buf,
+            pltpu.SemaphoreType.DMA, place_sems, pair_sems, sems,
         ],
         compiler_params=params(44),
         cost_estimate=cost(work, 2 * tile_bytes),
         name="second_shares",
-    )(core, ids, pairs, spam, shield, in_weight, mine, swap(mine), held(places), held(packed))
+    )(core, ids, pairs, spam, shield, in_weight, part, swap(mine), held(places), held(packed))
     arrived = exchange(asked_for)
     distrust = pl.pallas_call(
         functools.partial(fifth_kernel, slots_chunk),
-        out_shape=sds((blocks, size, columns), F32),
+        out_shape=pltpu.HBM((blocks, size, columns), F32),
         in_specs=[SMEM, VMEM, HBM, HBM],
-        out_specs=VMEM,
-        scratch_shapes=[y_buf, packed_buf, total_buf, sems, pair_sems],
+        out_specs=HBM,
+        scratch_shapes=[
+            y_buf, packed_buf, total_buf, pltpu.VMEM((blocks, size, columns), F32), sems, pair_sems,
+            pltpu.SemaphoreType.DMA((blocks // 4,)),
+        ],
         compiler_params=params(40),
         cost_estimate=cost(work, 2 * tile_bytes),
         name="last_pull",

time: 278 us -> 277 us (level)
    pallas_call x1 -> x2, Pallas kernels: 8.37 us -> 12.6 us  [the longest x1 7.96 us: body(): pl.pallas_call(functools.partial(fifth_kernel, slots_chunk), out_shape=pl...]
    pallas_call x1, Pallas kernels: 14 us -> 10.9 us  [body(): pl.pallas_call(functools.partial(fourth_kernel, slots_chunk), out_shape=a...]
  transfers between devices with their start and end apart: 5 -> 5, of which waited for: 5 -> 4; matrix products, arithmetic and copies ran while one was open for 1% -> 1% of each run, Pallas kernels for 23% -> 25%
where the time goes in v6:
time: 277 us; the launch traced here: 276 us
  Pallas kernels  113 us (41%)
  waiting for transfers between devices  108 us (39%)
  starting transfers between devices  27.2 us (10%)
  blocking collectives  25 us (9%)
    all_to_all x3, waiting for transfers between devices, exchange(): return lax.all_to_all(x, AXES, split_axis=0, concat_axis=0, tiled=True)  105 us
    pallas_call x1, Pallas kernels, body(): pl.pallas_call(places_kernel, out_shape=pltpu.HBM((slots, columns, size),...  33.7 us
    all_to_all x1, blocking collectives, exchange(): return lax.all_to_all(x, AXES, split_axis=0, concat_axis=0, tiled=True)  25 us
    all_to_all x3, starting transfers between devices, exchange(): return lax.all_to_all(x, AXES, split_axis=0, concat_axis=0, tiled=True)  24.6 us
    pallas_call x1, Pallas kernels, body(): pl.pallas_call(pack_kernel, out_shape=pltpu.HBM(packed_shape, BF16), in_s...  17.4 us
    pallas_call x1, Pallas kernels, body(): pl.pallas_call(functools.partial(fourth_kernel, slots_chunk), out_shape=a...  10.9 us
    pallas_call x1, Pallas kernels, body(): pl.pallas_call(functools.partial(second_kernel, slots_chunk, tiles_chunk)...  10.2 us
    pallas_call x1, Pallas kernels, body(): pl.pallas_call(functools.partial(first_kernel, slots_chunk, tiles_chunk,...  10.2 us
  transfers between devices with their start and end apart: 5, of which 4 were waited for; matrix products, arithmetic and copies ran while one was open for 1% of the time, Pallas kernels for 25%

profile of v6, /device:TPU:1, one launch (start us, length us, event | category | flops | bytes accessed | tf_op | source)
XLA Modules:
  0.0 276.3 jit_solution(17204338818993620225)
XLA Ops:
  0.6 10.2 %first_push.1 = (s16[128,168,128]{2,1,0:T(8,128)(2,1)}, bf16[16,128,128]{2,1,0:T(8,128)(2,1)}) custom-call(s32[256]{0:T(256)} %src.3, s32[256]{0:T(256)} %slot.4, s32[128]{0:T(128)} %slot_block.3, s32[128,128]{1,0:T(8,128)} %seeds.1, s32[64,128]{1,0:T(8,128)} %bitcast.14, s32[16,1,128]{2,1,0:T(1,128)} %bitcast.10, bf16[256,128,128]{2,1,0:T(8,128)(2,1)} %tiles_hbm.7), custom_call_target="tpu_custom_call" | custom-call | flops 1073741824 | bytes 16777216 | tf_op jit(solution)/shard_map/first_push/pallas_call | solution.py:624
  10.9 0.0 copy-start.3
  10.9 0.0 copy-start.5
  10.9 11.9 %all-to-all-start = ((s16[128,168,128]{2,1,0:T(8,128)(2,1)}), s16[128,168,128]{2,1,0:T(8,128)(2,1)}, u32[]{:S(2)}, u32[]{:S(2)}) async-start(s16[128,168,128]{2,1,0:T(8,128)(2,1)} %get-tuple-element.23), calls=%async_computation | async-start | bytes 11010048 | tf_op jit(solution)/shard_map/all_to_all | solution.py:39
  22.8 0.1 convert_reduce_fusion.1
  22.9 0.1 select_reduce_fusion.6
  23.0 0.1 select_reduce_fusion.5
  23.1 0.2 convert_reduce_fusion
  23.4 0.3 select_reduce_fusion
  23.7 0.1 copy.12.seeds
  23.8 10.1 %side.1 = (bf16[16,128,128]{2,1,0:T(8,128)(2,1)S(1)}, s16[128,8,128]{2,1,0:T(8,128)(2,1)S(1)}) custom-call(s32[128,64]{1,0:T(8,128)S(1)} %copy.12.seeds, s32[256]{0:T(256)S(1)} %copy-done.3, bf16[256,128,128]{2,1,0:T(8,128)(2,1)} %tiles_hbm.7), custom_call_target="tpu_custom_call" | custom-call | flops 268435456 | bytes 8388608 | tf_op jit(solution)/shard_map/side/pallas_call | solution.py:637
  33.9 0.0 copy-start.2
  34.0 17.4 %pack.1.packed_hbm = bf16[136,256,128]{2,1,0:T(8,128)(2,1)} custom-call(s32[5,136]{1,0:T(8,128)S(1)} %stack.17.pairs, bf16[256,128,128]{2,1,0:T(8,128)(2,1)} %tiles_hbm.7), custom_call_target="tpu_custom_call" | custom-call | flops 268435456 | bytes 16777216 | tf_op jit(solution)/shard_map/pack/pallas_call | solution.py:649
  51.4 38.3 %all-to-all-done.arrived_hbm = s16[128,168,128]{2,1,0:T(8,128)(2,1)} async-done(((s16[128,168,128]{2,1,0:T(8,128)(2,1)}), s16[128,168,128]{2,1,0:T(8,128)(2,1)}, u32[]{:S(2)}, u32[]{:S(2)}) %all-to-all-start) | async-done | bytes 5505056 | tf_op jit(solution)/shard_map/all_to_all | solution.py:39
  89.7 10.2 %second_push.1 = (s16[128,136,128]{2,1,0:T(8,128)(2,1)}, s32[8,1,128]{2,1,0:T(1,128)S(1)}) custom-call(s32[256]{0:T(256)S(1)} %copy-done.1, s32[256]{0:T(256)S(1)} %copy-done.3, s32[16,1,128]{2,1,0:T(1,128)S(1)} %bitcast.11, bf16[16,128,128]{2,1,0:T(8,128)(2,1)S(1)} %copy-done, s16[128,8,128]{2,1,0:T(8,128)(2,1)S(1)} %get-tuple-element.29.weights, ...), custom_call_target="tpu_custom_call" | custom-call | flops 1073741824 | bytes 16777216 | tf_op jit(solution)/shard_map/second_push/pallas_call | solution.py:660
  100.0 0.0 copy-start.4
  100.0 7.9 %all-to-all-start.1 = ((s16[128,136,128]{2,1,0:T(8,128)(2,1)}), s16[128,136,128]{2,1,0:T(8,128)(2,1)}, u32[]{:S(2)}, u32[]{:S(2)}) async-start(s16[128,136,128]{2,1,0:T(8,128)(2,1)} %get-tuple-element.33), calls=%async_computation.1 | async-start | bytes 8912896 | tf_op jit(solution)/shard_map/all_to_all | solution.py:39
  108.0 1.3 slice.11.mine_hbm
  109.3 1.4 collective-permute-start
  110.7 0.1 pad_add_fusion.spam_hosts
  110.7 2.2 collective-permute-done.other_hbm
  113.0 33.7 %places.1.places_hbm = s16[128,128,128]{2,1,0:T(8,128)(2,1)} custom-call(s32[1]{0:T(128)} %bitcast.7.core, s32[128]{0:T(128)S(1)} %copy-done.4, s16[128,32,128]{2,1,0:T(8,128)(2,1)S(1)} %slice.11.mine_hbm, s16[128,32,128]{2,1,0:T(8,128)(2,1)S(1)} %collective-permute-done.other_hbm), custom_call_target="tpu_custom_call" | custom-call | flops 1073741824 | bytes 8388608 | tf_op jit(solution)/shard_map/places/pallas_call | solution.py:677
  146.7 16.9 %all-to-all-done.1.arrived_hbm = s16[128,136,128]{2,1,0:T(8,128)(2,1)} async-done(((s16[128,136,128]{2,1,0:T(8,128)(2,1)}), s16[128,136,128]{2,1,0:T(8,128)(2,1)}, u32[]{:S(2)}, u32[]{:S(2)}) %all-to-all-start.1) | async-done | bytes 4456480 | tf_op jit(solution)/shard_map/all_to_all | solution.py:39
  163.6 5.4 %first_shares.1 = (bf16[128,32,128]{2,1,0:T(8,128)(2,1)}, f32[16,128,128]{2,1,0:T(8,128)S(1)}, f32[16,128,128]{2,1,0:T(8,128)S(1)}, f32[16,1,128]{2,1,0:T(1,128)S(1)}) custom-call(s32[8,1,128]{2,1,0:T(1,128)S(1)} %get-tuple-element.31.ids, bf16[16,128,128]{2,1,0:T(8,128)(2,1)S(1)} %copy-done, bf16[16,128,128]{2,1,0:T(8,128)(2,1)S(1)} %get-tuple-element.32.spam, ...), custom_call_target="tpu_custom_call" | custom-call | flops 134217728 | bytes 8388608 | tf_op jit(solution)/shard_map/first_shares/pallas_call | solution.py:692
  169.0 25.0 %all_to_all.20.mine_hbm = bf16[128,32,128]{2,1,0:T(8,128)(2,1)S(1)} all-to-all(bf16[128,32,128]{2,1,0:T(8,128)(2,1)} %get-tuple-element.39), channel_id=1, replica_groups=mesh['row'=16,'col'=8] {'row','col'}, dimensions={0} | all-to-all | bytes 2097152 | tf_op jit(solution)/shard_map/all_to_all | solution.py:39
  194.0 1.2 collective-permute-start.1
  195.2 4.6 %own_values.1.part = bf16[128,64,128]{2,1,0:T(8,128)(2,1)S(1)} custom-call(s32[1]{0:T(128)} %bitcast.7.core, bf16[128,32,128]{2,1,0:T(8,128)(2,1)S(1)} %all_to_all.20.mine_hbm, s16[128,128,128]{2,1,0:T(8,128)(2,1)} %places.1.places_hbm), custom_call_target="tpu_custom_call" | custom-call | flops 268435456 | bytes 4194304 | tf_op jit(solution)/shard_map/own_values/pallas_call | solution.py:718
  199.8 10.9 %second_shares.1 = bf16[128,128,128]{2,1,0:T(8,128)(2,1)} custom-call(s32[1]{0:T(128)} %bitcast.7.core, s32[8,1,128]{2,1,0:T(1,128)S(1)} %get-tuple-element.31.ids, s32[5,136]{1,0:T(8,128)S(1)} %stack.17.pairs, bf16[16,128,128]{2,1,0:T(8,128)(2,1)S(1)} %get-tuple-element.32.spam, f32[16,128,128]{2,1,0:T(8,128)S(1)} %get-tuple-element.37.shield, ...), custom_call_target="tpu_custom_call" | custom-call | flops 1073741824 | bytes 16777216 | tf_op jit(solution)/shard_map/second_shares/pallas_call | solution.py:728
  210.7 4.8 %all-to-all-start.3 = ((bf16[128,128,128]{2,1,0:T(8,128)(2,1)}), bf16[128,128,128]{2,1,0:T(8,128)(2,1)}, u32[]{:S(2)}, u32[]{:S(2)}) async-start(bf16[128,128,128]{2,1,0:T(8,128)(2,1)} %second_shares.1), calls=%async_computation.3 | async-start | bytes 8388608 | tf_op jit(solution)/shard_map/all_to_all | solution.py:39
  215.5 2.6 turn.1
  218.0 50.1 %all-to-all-done.3.arrived_hbm = bf16[128,128,128]{2,1,0:T(8,128)(2,1)} async-done(((bf16[128,128,128]{2,1,0:T(8,128)(2,1)}), bf16[128,128,128]{2,1,0:T(8,128)(2,1)}, u32[]{:S(2)}, u32[]{:S(2)}) %all-to-all-start.3) | async-done | bytes 4194336 | tf_op jit(solution)/shard_map/all_to_all | solution.py:39
  268.2 8.0 %last_pull.1 = f32[16,128,128]{2,1,0:T(8,128)} custom-call(s32[5,136]{1,0:T(8,128)S(1)} %stack.17.pairs, bf16[16,128,128]{2,1,0:T(8,128)(2,1)S(1)} %get-tuple-element.32.spam, bf16[128,128,128]{2,1,0:T(8,128)(2,1)} %all-to-all-done.3.arrived_hbm, bf16[136,256,128]{2,1,0:T(8,128)(2,1)} %pack.1.packed_hbm), custom_call_target="tpu_custom_call" | custom-call | flops 1073741824 | bytes 16777216 | tf_op jit(solution)/shard_map/last_pull/pallas_call | solution.py:742
  (17 shorter events, 0.1 us)
Async XLA Ops:
  10.8 11.9 %copy-start.1 = (s32[256]{0:T(256)S(1)}, s32[256]{0:T(256)}, u32[]{:S(2)}) copy-start(s32[256]{0:T(256)} %src.3) | copy-start | bytes 3076
  10.9 12.5 %copy-start.3 = (s32[256]{0:T(256)S(1)}, s32[256]{0:T(256)}, u32[]{:S(2)}) copy-start(s32[256]{0:T(256)} %slot.4) | copy-start | bytes 3076
  10.9 12.8 %copy-start.5 = (s32[128,64]{0,1:T(8,128)S(1)}, s32[128,64]{0,1:T(8,128)}, u32[]{:S(2)}) copy-start(s32[128,64]{0,1:T(8,128)} %param.13) | copy-start | bytes 98308
  10.9 78.8 %all-to-all-start = ((s16[128,168,128]{2,1,0:T(8,128)(2,1)}), s16[128,168,128]{2,1,0:T(8,128)(2,1)}, u32[]{:S(2)}, u32[]{:S(2)}) async-start(s16[128,168,128]{2,1,0:T(8,128)(2,1)} %get-tuple-element.23), calls=%async_computation | async-start | bytes 11010048 | tf_op jit(solution)/shard_map/all_to_all | solution.py:39
  33.9 55.8 %copy-start = (bf16[16,128,128]{2,1,0:T(8,128)(2,1)S(1)}, bf16[16,128,128]{2,1,0:T(8,128)(2,1)}, u32[]{:S(2)}) copy-start(bf16[16,128,128]{2,1,0:T(8,128)(2,1)} %get-tuple-element.22.good) | copy-start | bytes 1572868
  33.9 55.8 %copy-start.2 = (s32[2048]{0:T(1024)S(1)}, s32[2048]{0:T(1024)}, u32[]{:S(2)}) copy-start(s32[2048]{0:T(1024)} %param.11) | copy-start | bytes 24580
  100.0 13.0 %copy-start.4 = (s32[128]{0:T(128)S(1)}, s32[128]{0:T(128)}, u32[]{:S(2)}) copy-start(s32[128]{0:T(128)} %slot_block.3) | copy-start | bytes 1540
  100.0 63.6 %all-to-all-start.1 = ((s16[128,136,128]{2,1,0:T(8,128)(2,1)}), s16[128,136,128]{2,1,0:T(8,128)(2,1)}, u32[]{:S(2)}, u32[]{:S(2)}) async-start(s16[128,136,128]{2,1,0:T(8,128)(2,1)} %get-tuple-element.33), calls=%async_computation.1 | async-start | bytes 8912896 | tf_op jit(solution)/shard_map/all_to_all | solution.py:39
  109.3 3.7 %collective-permute-start = (s16[128,32,128]{2,1,0:T(8,128)(2,1)S(1)}, s16[128,32,128]{2,1,0:T(8,128)(2,1)S(1)}, u32[]{:S(2)}, u32[]{:S(2)}) collective-permute-start(s16[128,32,128]{2,1,0:T(8,128)(2,1)S(1)} %slice.11.mine_hbm), channel_id=1, source_target_pairs={{0,1},{1,0},{2,3},{3,2},{4,5},{5,4},{6,7},{7,6},{8,9},{9,8},{10,11... | collective-permute-start | bytes 3145736 | tf_op jit(solution)/shard_map/ppermute | solution.py:35
  194.0 5.8 %collective-permute-start.1 = (bf16[128,32,128]{2,1,0:T(8,128)(2,1)S(1)}, bf16[128,32,128]{2,1,0:T(8,128)(2,1)S(1)}, u32[]{:S(2)}, u32[]{:S(2)}) collective-permute-start(bf16[128,32,128]{2,1,0:T(8,128)(2,1)S(1)} %all_to_all.20.mine_hbm), channel_id=1, source_target_pairs={{0,1},{1,0},{2,3},{3,2},{4,5},{5,4},{6,7},{7,6},{8,9},{9,8},{10,11... | collective-permute-start | bytes 3145736 | tf_op jit(solution)/shard_map/ppermute | solution.py:35
  210.7 57.5 %all-to-all-start.3 = ((bf16[128,128,128]{2,1,0:T(8,128)(2,1)}), bf16[128,128,128]{2,1,0:T(8,128)(2,1)}, u32[]{:S(2)}, u32[]{:S(2)}) async-start(bf16[128,128,128]{2,1,0:T(8,128)(2,1)} %second_shares.1), calls=%async_computation.3 | async-start | bytes 8388608 | tf_op jit(solution)/shard_map/all_to_all | solution.py:39

commit v7 on v6

--- a/solution.py
+++ b/solution.py
@@ -137,6 +137,7 @@
 
 def send(acc, extra_row, staged, out_hbm, sems, chunk, lists=None):
     copies = []
+    last = staged.shape[1] - EXTRA
     row = lax.broadcasted_iota(I32, (EXTRA, BS), 0)
     unroll = min(8, chunk)
     for c in range(acc.shape[0] // chunk):
@@ -148,9 +149,9 @@
                 code = encode_scale(jnp.max(jnp.abs(block), axis=0, keepdims=True))
                 staged[p, 0:BS, :] = to_i16(block * up(code))
                 tail = jnp.where(row == 0, jnp.broadcast_to(code.astype(I32), (EXTRA, BS)), extra_row(p))
-                staged[p, BS : BS + EXTRA, :] = tail.astype(I16)
+                staged[p, last:, :] = tail.astype(I16)
                 if lists is not None:
-                    staged[p, BS + EXTRA :, :] = lists[u % 2]
+                    staged[p, BS:last, :] = lists[u % 2]
             return 0
 
         lax.fori_loop(0, chunk // unroll, group, 0)
@@ -164,6 +165,7 @@
 
 
 def receive(arrived, copies, ids, total, chunk, also=None):
+    last = arrived.shape[1] - EXTRA
     for b in range(total.shape[0]):
         total[b] = jnp.zeros(total.shape[1:], F32)
     unroll = min(16, chunk)
@@ -176,7 +178,7 @@
             for u in range(unroll):
                 one = g * unroll + u
                 p = c * chunk + one
-                tail = arrived[p, BS : BS + EXTRA, :].astype(I32).astype(F32)
+                tail = arrived[p, last:, :].astype(I32).astype(F32)
                 values = arrived[p, 0:BS, :].astype(I32).astype(F32) * down(tail[0:1])
                 at = at_chunk(one)
                 total[at] = total[at] + values
@@ -229,7 +231,7 @@
         incoming[c].wait()
         row = jnp.zeros((1, BS), I32)
         for u in range(slots_chunk):
-            tail = arrived[c * slots_chunk + u, BS : BS + EXTRA, :].astype(I32)
+            tail = arrived[c * slots_chunk + u, arrived.shape[1] - EXTRA :, :].astype(I32)
             row = jnp.where(lane == u, tail[1:2], row)
         ids_out[c] = row
         move = pltpu.make_async_copy(ids_out.at[c], ids.at[c], id_sems.at[c])
@@ -673,7 +675,7 @@
     first_arrived, _ = lax.optimization_barrier((arrived, outgoing))
     arrived = exchange(outgoing)
     core = (lax.axis_index("col") % 2).astype(I32)[None]
-    mine = first_arrived[:, columns + EXTRA :, :]
+    mine = first_arrived[:, columns : columns + half, :]
     places = pl.pallas_call(
         places_kernel,
         out_shape=pltpu.HBM((slots, columns, size), I16),

time: 277 us -> 277 us (level)
  no operation moved by 1% of the time
where the time goes in v7:
time: 277 us; the launch traced here: 276 us
  Pallas kernels  113 us (41%)
  waiting for transfers between devices  108 us (39%)
  starting transfers between devices  27.2 us (10%)
  blocking collectives  25 us (9%)
    all_to_all x3, waiting for transfers between devices, exchange(): return lax.all_to_all(x, AXES, split_axis=0, concat_axis=0, tiled=True)  105 us
    pallas_call x1, Pallas kernels, body(): pl.pallas_call(places_kernel, out_shape=pltpu.HBM((slots, columns, size),...  33.7 us
    all_to_all x1, blocking collectives, exchange(): return lax.all_to_all(x, AXES, split_axis=0, concat_axis=0, tiled=True)  25 us
    all_to_all x3, starting transfers between devices, exchange(): return lax.all_to_all(x, AXES, split_axis=0, concat_axis=0, tiled=True)  24.6 us
    pallas_call x1, Pallas kernels, body(): pl.pallas_call(pack_kernel, out_shape=pltpu.HBM(packed_shape, BF16), in_s...  17.4 us
    pallas_call x1, Pallas kernels, body(): pl.pallas_call(functools.partial(fourth_kernel, slots_chunk), out_shape=a...  10.9 us
    pallas_call x1, Pallas kernels, body(): pl.pallas_call(functools.partial(second_kernel, slots_chunk, tiles_chunk)...  10.2 us
    pallas_call x1, Pallas kernels, body(): pl.pallas_call(functools.partial(first_kernel, slots_chunk, tiles_chunk,...  10.2 us
  transfers between devices with their start and end apart: 5, of which 4 were waited for; matrix products, arithmetic and copies ran while one was open for 1% of the time, Pallas kernels for 25%

profile of v7, /device:TPU:1, one launch (start us, length us, event | category | flops | bytes accessed | tf_op | source)
XLA Modules:
  0.0 276.3 jit_solution(15684482793755298718)
XLA Ops:
  0.6 10.2 %first_push.1 = (s16[128,168,128]{2,1,0:T(8,128)(2,1)}, bf16[16,128,128]{2,1,0:T(8,128)(2,1)}) custom-call(s32[256]{0:T(256)} %src.3, s32[256]{0:T(256)} %slot.4, s32[128]{0:T(128)} %slot_block.3, s32[128,128]{1,0:T(8,128)} %seeds.1, s32[64,128]{1,0:T(8,128)} %bitcast.14, s32[16,1,128]{2,1,0:T(1,128)} %bitcast.10, bf16[256,128,128]{2,1,0:T(8,128)(2,1)} %tiles_hbm.7), custom_call_target="tpu_custom_call" | custom-call | flops 1073741824 | bytes 16777216 | tf_op jit(solution)/shard_map/first_push/pallas_call | solution.py:626
  10.8 0.0 copy-start.1
  10.9 0.0 copy-start.3
  10.9 0.0 copy-start.5
  10.9 11.9 %all-to-all-start = ((s16[128,168,128]{2,1,0:T(8,128)(2,1)}), s16[128,168,128]{2,1,0:T(8,128)(2,1)}, u32[]{:S(2)}, u32[]{:S(2)}) async-start(s16[128,168,128]{2,1,0:T(8,128)(2,1)} %get-tuple-element.23), calls=%async_computation | async-start | bytes 11010048 | tf_op jit(solution)/shard_map/all_to_all | solution.py:39
  22.8 0.1 convert_reduce_fusion.1
  22.9 0.1 select_reduce_fusion.6
  23.0 0.1 select_reduce_fusion.5
  23.1 0.2 convert_reduce_fusion
  23.4 0.3 select_reduce_fusion
  23.7 0.1 copy.12.seeds
  23.8 10.1 %side.1 = (bf16[16,128,128]{2,1,0:T(8,128)(2,1)S(1)}, s16[128,8,128]{2,1,0:T(8,128)(2,1)S(1)}) custom-call(s32[128,64]{1,0:T(8,128)S(1)} %copy.12.seeds, s32[256]{0:T(256)S(1)} %copy-done.3, bf16[256,128,128]{2,1,0:T(8,128)(2,1)} %tiles_hbm.7), custom_call_target="tpu_custom_call" | custom-call | flops 268435456 | bytes 8388608 | tf_op jit(solution)/shard_map/side/pallas_call | solution.py:639
  33.9 0.0 copy-start
  33.9 17.4 %pack.1.packed_hbm = bf16[136,256,128]{2,1,0:T(8,128)(2,1)} custom-call(s32[5,136]{1,0:T(8,128)S(1)} %stack.17.pairs, bf16[256,128,128]{2,1,0:T(8,128)(2,1)} %tiles_hbm.7), custom_call_target="tpu_custom_call" | custom-call | flops 268435456 | bytes 16777216 | tf_op jit(solution)/shard_map/pack/pallas_call | solution.py:651
  51.4 38.3 %all-to-all-done.arrived_hbm = s16[128,168,128]{2,1,0:T(8,128)(2,1)} async-done(((s16[128,168,128]{2,1,0:T(8,128)(2,1)}), s16[128,168,128]{2,1,0:T(8,128)(2,1)}, u32[]{:S(2)}, u32[]{:S(2)}) %all-to-all-start) | async-done | bytes 5505056 | tf_op jit(solution)/shard_map/all_to_all | solution.py:39
  89.7 10.2 %second_push.1 = (s16[128,136,128]{2,1,0:T(8,128)(2,1)}, s32[8,1,128]{2,1,0:T(1,128)S(1)}) custom-call(s32[256]{0:T(256)S(1)} %copy-done.1, s32[256]{0:T(256)S(1)} %copy-done.3, s32[16,1,128]{2,1,0:T(1,128)S(1)} %bitcast.11, bf16[16,128,128]{2,1,0:T(8,128)(2,1)S(1)} %copy-done, s16[128,8,128]{2,1,0:T(8,128)(2,1)S(1)} %get-tuple-element.29.weights, ...), custom_call_target="tpu_custom_call" | custom-call | flops 1073741824 | bytes 16777216 | tf_op jit(solution)/shard_map/second_push/pallas_call | solution.py:662
  100.0 7.9 %all-to-all-start.1 = ((s16[128,136,128]{2,1,0:T(8,128)(2,1)}), s16[128,136,128]{2,1,0:T(8,128)(2,1)}, u32[]{:S(2)}, u32[]{:S(2)}) async-start(s16[128,136,128]{2,1,0:T(8,128)(2,1)} %get-tuple-element.33), calls=%async_computation.1 | async-start | bytes 8912896 | tf_op jit(solution)/shard_map/all_to_all | solution.py:39
  108.0 1.3 slice.11.mine_hbm
  109.3 1.4 collective-permute-start
  110.7 0.1 pad_add_fusion.spam_hosts
  110.7 2.2 collective-permute-done.other_hbm
  113.0 33.7 %places.1.places_hbm = s16[128,128,128]{2,1,0:T(8,128)(2,1)} custom-call(s32[1]{0:T(128)} %bitcast.7.core, s32[128]{0:T(128)S(1)} %copy-done.4, s16[128,32,128]{2,1,0:T(8,128)(2,1)S(1)} %slice.11.mine_hbm, s16[128,32,128]{2,1,0:T(8,128)(2,1)S(1)} %collective-permute-done.other_hbm), custom_call_target="tpu_custom_call" | custom-call | flops 1073741824 | bytes 8388608 | tf_op jit(solution)/shard_map/places/pallas_call | solution.py:679
  146.7 16.9 %all-to-all-done.1.arrived_hbm = s16[128,136,128]{2,1,0:T(8,128)(2,1)} async-done(((s16[128,136,128]{2,1,0:T(8,128)(2,1)}), s16[128,136,128]{2,1,0:T(8,128)(2,1)}, u32[]{:S(2)}, u32[]{:S(2)}) %all-to-all-start.1) | async-done | bytes 4456480 | tf_op jit(solution)/shard_map/all_to_all | solution.py:39
  163.6 5.4 %first_shares.1 = (bf16[128,32,128]{2,1,0:T(8,128)(2,1)}, f32[16,128,128]{2,1,0:T(8,128)S(1)}, f32[16,128,128]{2,1,0:T(8,128)S(1)}, f32[16,1,128]{2,1,0:T(1,128)S(1)}) custom-call(s32[8,1,128]{2,1,0:T(1,128)S(1)} %get-tuple-element.31.ids, bf16[16,128,128]{2,1,0:T(8,128)(2,1)S(1)} %copy-done, bf16[16,128,128]{2,1,0:T(8,128)(2,1)S(1)} %get-tuple-element.32.spam, ...), custom_call_target="tpu_custom_call" | custom-call | flops 134217728 | bytes 8388608 | tf_op jit(solution)/shard_map/first_shares/pallas_call | solution.py:694
  169.0 25.0 %all_to_all.20.mine_hbm = bf16[128,32,128]{2,1,0:T(8,128)(2,1)S(1)} all-to-all(bf16[128,32,128]{2,1,0:T(8,128)(2,1)} %get-tuple-element.39), channel_id=1, replica_groups=mesh['row'=16,'col'=8] {'row','col'}, dimensions={0} | all-to-all | bytes 2097152 | tf_op jit(solution)/shard_map/all_to_all | solution.py:39
  194.0 1.2 collective-permute-start.1
  195.2 4.6 %own_values.1.part = bf16[128,64,128]{2,1,0:T(8,128)(2,1)S(1)} custom-call(s32[1]{0:T(128)} %bitcast.7.core, bf16[128,32,128]{2,1,0:T(8,128)(2,1)S(1)} %all_to_all.20.mine_hbm, s16[128,128,128]{2,1,0:T(8,128)(2,1)} %places.1.places_hbm), custom_call_target="tpu_custom_call" | custom-call | flops 268435456 | bytes 4194304 | tf_op jit(solution)/shard_map/own_values/pallas_call | solution.py:720
  199.8 10.9 %second_shares.1 = bf16[128,128,128]{2,1,0:T(8,128)(2,1)} custom-call(s32[1]{0:T(128)} %bitcast.7.core, s32[8,1,128]{2,1,0:T(1,128)S(1)} %get-tuple-element.31.ids, s32[5,136]{1,0:T(8,128)S(1)} %stack.17.pairs, bf16[16,128,128]{2,1,0:T(8,128)(2,1)S(1)} %get-tuple-element.32.spam, f32[16,128,128]{2,1,0:T(8,128)S(1)} %get-tuple-element.37.shield, ...), custom_call_target="tpu_custom_call" | custom-call | flops 1073741824 | bytes 16777216 | tf_op jit(solution)/shard_map/second_shares/pallas_call | solution.py:730
  210.7 4.8 %all-to-all-start.3 = ((bf16[128,128,128]{2,1,0:T(8,128)(2,1)}), bf16[128,128,128]{2,1,0:T(8,128)(2,1)}, u32[]{:S(2)}, u32[]{:S(2)}) async-start(bf16[128,128,128]{2,1,0:T(8,128)(2,1)} %second_shares.1), calls=%async_computation.3 | async-start | bytes 8388608 | tf_op jit(solution)/shard_map/all_to_all | solution.py:39
  215.5 2.6 turn.1
  218.0 50.1 %all-to-all-done.3.arrived_hbm = bf16[128,128,128]{2,1,0:T(8,128)(2,1)} async-done(((bf16[128,128,128]{2,1,0:T(8,128)(2,1)}), bf16[128,128,128]{2,1,0:T(8,128)(2,1)}, u32[]{:S(2)}, u32[]{:S(2)}) %all-to-all-start.3) | async-done | bytes 4194336 | tf_op jit(solution)/shard_map/all_to_all | solution.py:39
  268.2 8.0 %last_pull.1 = f32[16,128,128]{2,1,0:T(8,128)} custom-call(s32[5,136]{1,0:T(8,128)S(1)} %stack.17.pairs, bf16[16,128,128]{2,1,0:T(8,128)(2,1)S(1)} %get-tuple-element.32.spam, bf16[128,128,128]{2,1,0:T(8,128)(2,1)} %all-to-all-done.3.arrived_hbm, bf16[136,256,128]{2,1,0:T(8,128)(2,1)} %pack.1.packed_hbm), custom_call_target="tpu_custom_call" | custom-call | flops 1073741824 | bytes 16777216 | tf_op jit(solution)/shard_map/last_pull/pallas_call | solution.py:744
  (17 shorter events, 0.1 us)
Async XLA Ops:
  10.8 11.9 %copy-start.1 = (s32[256]{0:T(256)S(1)}, s32[256]{0:T(256)}, u32[]{:S(2)}) copy-start(s32[256]{0:T(256)} %src.3) | copy-start | bytes 3076
  10.9 12.5 %copy-start.3 = (s32[256]{0:T(256)S(1)}, s32[256]{0:T(256)}, u32[]{:S(2)}) copy-start(s32[256]{0:T(256)} %slot.4) | copy-start | bytes 3076
  10.9 12.8 %copy-start.5 = (s32[128,64]{0,1:T(8,128)S(1)}, s32[128,64]{0,1:T(8,128)}, u32[]{:S(2)}) copy-start(s32[128,64]{0,1:T(8,128)} %param.13) | copy-start | bytes 98308
  10.9 78.8 %all-to-all-start = ((s16[128,168,128]{2,1,0:T(8,128)(2,1)}), s16[128,168,128]{2,1,0:T(8,128)(2,1)}, u32[]{:S(2)}, u32[]{:S(2)}) async-start(s16[128,168,128]{2,1,0:T(8,128)(2,1)} %get-tuple-element.23), calls=%async_computation | async-start | bytes 11010048 | tf_op jit(solution)/shard_map/all_to_all | solution.py:39
  33.9 55.8 %copy-start = (bf16[16,128,128]{2,1,0:T(8,128)(2,1)S(1)}, bf16[16,128,128]{2,1,0:T(8,128)(2,1)}, u32[]{:S(2)}) copy-start(bf16[16,128,128]{2,1,0:T(8,128)(2,1)} %get-tuple-element.22.good) | copy-start | bytes 1572868
  33.9 55.8 %copy-start.2 = (s32[2048]{0:T(1024)S(1)}, s32[2048]{0:T(1024)}, u32[]{:S(2)}) copy-start(s32[2048]{0:T(1024)} %param.11) | copy-start | bytes 24580
  100.0 13.0 %copy-start.4 = (s32[128]{0:T(128)S(1)}, s32[128]{0:T(128)}, u32[]{:S(2)}) copy-start(s32[128]{0:T(128)} %slot_block.3) | copy-start | bytes 1540
  100.0 63.6 %all-to-all-start.1 = ((s16[128,136,128]{2,1,0:T(8,128)(2,1)}), s16[128,136,128]{2,1,0:T(8,128)(2,1)}, u32[]{:S(2)}, u32[]{:S(2)}) async-start(s16[128,136,128]{2,1,0:T(8,128)(2,1)} %get-tuple-element.33), calls=%async_computation.1 | async-start | bytes 8912896 | tf_op jit(solution)/shard_map/all_to_all | solution.py:39
  109.3 3.7 %collective-permute-start = (s16[128,32,128]{2,1,0:T(8,128)(2,1)S(1)}, s16[128,32,128]{2,1,0:T(8,128)(2,1)S(1)}, u32[]{:S(2)}, u32[]{:S(2)}) collective-permute-start(s16[128,32,128]{2,1,0:T(8,128)(2,1)S(1)} %slice.11.mine_hbm), channel_id=1, source_target_pairs={{0,1},{1,0},{2,3},{3,2},{4,5},{5,4},{6,7},{7,6},{8,9},{9,8},{10,11... | collective-permute-start | bytes 3145736 | tf_op jit(solution)/shard_map/ppermute | solution.py:35
  194.0 5.8 %collective-permute-start.1 = (bf16[128,32,128]{2,1,0:T(8,128)(2,1)S(1)}, bf16[128,32,128]{2,1,0:T(8,128)(2,1)S(1)}, u32[]{:S(2)}, u32[]{:S(2)}) collective-permute-start(bf16[128,32,128]{2,1,0:T(8,128)(2,1)S(1)} %all_to_all.20.mine_hbm), channel_id=1, source_target_pairs={{0,1},{1,0},{2,3},{3,2},{4,5},{5,4},{6,7},{7,6},{8,9},{9,8},{10,11... | collective-permute-start | bytes 3145736 | tf_op jit(solution)/shard_map/ppermute | solution.py:35
  210.7 57.5 %all-to-all-start.3 = ((bf16[128,128,128]{2,1,0:T(8,128)(2,1)}), bf16[128,128,128]{2,1,0:T(8,128)(2,1)}, u32[]{:S(2)}, u32[]{:S(2)}) async-start(bf16[128,128,128]{2,1,0:T(8,128)(2,1)} %second_shares.1), calls=%async_computation.3 | async-start | bytes 8388608 | tf_op jit(solution)/shard_map/all_to_all | solution.py:39
